TPU v7x, 128 devices: a whole 4x4x4 slice. The times are simulated.
128 devices in a mesh: expert: 32 (over x, z, core), tensor: 4 (over y).
Axes of the slice: x: 4, y: 4, z: 4, core: 2. Of those that a mesh axis runs over, the one named last changes fastest.
Arguments:
- hidden_in: bfloat16 [4096, 2048], P('expert'), may hold values from -6 to 6
- cotangent: bfloat16 [4096, 2048], P('expert'), may hold values from -6 to 6
- segments: int32 [4096], replicated, may hold values from 0 to 3, never falling along the last dimension, each value on 1 to 2048 neighbouring positions
- routes: int32 [4096, 6], P('expert'), may hold values from 0 to 63, all different within a row; in each aligned block of 128 rows (0 to 127, 128 to 255, ...) at most 24 rows name the same one
- attn_norm: float32 [2048], P('expert'), may hold values from 0.5 to 1.5
- w_query: float32 [2048, 3072], P('expert', 'tensor'), may hold values from -0.125 to 0.125
- w_latent: float32 [2048, 576], P('expert'), may hold values from -0.125 to 0.125
- latent_norm: float32 [512], P('expert'), may hold values from 0.5 to 1.5
- w_expand: float32 [512, 4096], P('expert', 'tensor'), may hold values from -0.25 to 0.25
- w_output: float32 [2048, 2048], P('tensor', 'expert'), may hold values from -0.5 to 0.5
- ffn_norm: float32 [2048], P('expert'), may hold values from 0.5 to 1.5
- w_router: float32 [2048, 64], P('expert'), may hold values from -0.0625 to 0.0625
- shared_gate: float32 [2048, 2816], P('expert', 'tensor'), may hold values from -0.125 to 0.125
- shared_up: float32 [2048, 2816], P('expert', 'tensor'), may hold values from -0.125 to 0.125
- shared_down: float32 [2816, 2048], P('tensor', 'expert'), may hold values from -0.109375 to 0.109375
- expert_gate: float32 [64, 2048, 1408], P('expert', None, 'tensor'), may hold values from -0.125 to 0.125
- routed_expert_up: float32 [64, 2048, 1408], P('expert', None, 'tensor'), may hold values from -0.125 to 0.125
- expert_down: float32 [64, 1408, 2048], P('expert', 'tensor'), may hold values from -0.3125 to 0.3125
Outputs:
- layer_out: bfloat16 [4096, 2048], P('expert')
- grad_in: bfloat16 [4096, 2048], P('expert')
- grad_attn_norm: float32 [2048], P('expert')
- grad_query: float32 [2048, 3072], P('expert', 'tensor')
- grad_latent: float32 [2048, 576], P('expert')
- grad_latent_norm: float32 [512], P('expert')
- grad_expand: float32 [512, 4096], P('expert', 'tensor')
- grad_output: float32 [2048, 2048], P('tensor', 'expert')
- grad_ffn_norm: float32 [2048], P('expert')
- grad_router: float32 [2048, 64], P('expert')
- grad_shared_gate: float32 [2048, 2816], P('expert', 'tensor')
- grad_shared_up: float32 [2048, 2816], P('expert', 'tensor')
- grad_shared_down: float32 [2816, 2048], P('tensor', 'expert')
- grad_expert_gate: float32 [64, 2048, 1408], P('expert', None, 'tensor')
- grad_expert_up: float32 [64, 2048, 1408], P('expert', None, 'tensor')
- grad_expert_down: float32 [64, 1408, 2048], P('expert', 'tensor')
Inputs may be any that keep to these rules, and one draw needn't show every extreme that they name: `segments`: document numbers never fall along the tokens; a document has 1 to 2048 tokens, and one has exactly 2048. `routes`: the 6 experts of a token differ. Among the rows of one device (aligned blocks of 128 tokens) no expert is named more than 24 times, a bound that some block reaches.
All inputs are finite; a program needn't handle non-finite values.
Results may differ from a plain program's by a relative error of at most 0.035.
Values may be sent and summed in bfloat16 or wider, within the bound.
A program may use at most 256 MiB of HBM per device.

v0:
```python
import jax
import jax.numpy as jnp
from jax import lax
from jax.sharding import PartitionSpec as P

NOPE = 128
ROPE = 64
VH = 128
RANK = 512
WINDOW = 1024


epsilon = 1e-06
masked_score = -1e30
rope_base = 10000.0


def in_one_piece(arrays, axis, dim, along):
    columns = [a.reshape(*a.shape[:along], -1) for a in arrays]
    both = jnp.concatenate(columns, axis=along)
    result, at, done = (lax.all_gather(both, axis, axis=dim, tiled=True), 0, [])
    for a, column in zip(arrays, columns):
        share = result[..., at : at + column.shape[along]]
        done.append(share.reshape(*share.shape[:along], *a.shape[along:]))
        at += column.shape[along]
    return tuple(done)


def shifted(block, axis, distance):
    devices = range(lax.axis_size(axis))
    route = [(i - distance, i) for i in devices if i - distance in devices]
    return lax.ppermute(block, axis, route)


def copy_for_each(array, axis):
    copies = jnp.broadcast_to(array, (lax.axis_size(axis), *array.shape))
    return lax.all_to_all(copies, axis, split_axis=0, concat_axis=0, tiled=True)


def over_copies(array, axis):
    return copy_for_each(array, axis).sum(axis=0)


def in_order(tiles, dim):
    tiles = jnp.moveaxis(tiles, 0, dim)
    lengths = tiles.shape
    return tiles.reshape(*lengths[:dim], lengths[dim] * lengths[dim + 1], *lengths[dim + 2 :])


def gather_together(arrays, axis, dims):
    line = jnp.concatenate([a.reshape(-1) for a in arrays])
    lines, at, done = (lax.all_gather(line, axis), 0, [])
    for a, dim in zip(arrays, dims):
        tiles = lines[:, at : at + a.size].reshape(-1, *a.shape)
        done.append(in_order(tiles, dim))
        at += a.size
    return tuple(done)


def gather_directly(array, axis, dim):
    tiles = copy_for_each(array, axis)
    return in_order(tiles, dim)


def taken_together(array, axis):
    everything = copy_for_each(array, axis)
    return jnp.sum(everything.astype(jnp.float32), axis=0)


def in_one_piece_2(arrays, axis, dim, along):
    columns = [a.reshape(*a.shape[:along], -1) for a in arrays]
    both = jnp.concatenate(columns, axis=along)
    result, at, done = (lax.psum_scatter(both, axis, scatter_dimension=dim, tiled=True), 0, [])
    for a, column in zip(arrays, columns):
        share = result[..., at : at + column.shape[along]]
        done.append(share.reshape(*share.shape[:along], *a.shape[along:]))
        at += column.shape[along]
    return tuple(done)


def product(left_side, right_side):
    return jnp.dot(left_side, right_side, preferred_element_type=jnp.float32)


def contract_rows(left_side, right_side):
    return lax.dot_general(
        left_side, right_side, (((0,), (0,)), ((), ())), preferred_element_type=jnp.float32
    )


def contract_cols(left_side, right_side):
    return lax.dot_general(
        left_side, right_side, (((1,), (1,)), ((), ())), preferred_element_type=jnp.float32
    )


def rms_forward(values, gains):
    inverse = lax.rsqrt(jnp.mean(values * values, -1, keepdims=True) + epsilon)
    return (values * inverse * gains, inverse)


def rms_backward(values, inverse, gains, grad_out):
    weighted = grad_out * gains
    inner = jnp.mean(values * weighted, -1, keepdims=True)
    grad_values = inverse * weighted - values * (inverse * inverse * inverse) * inner
    grad_gains = jnp.sum(grad_out * values * inverse, 0)
    return (grad_values, grad_gains)


def rope_tables(positions):
    half_dim = ROPE // 2
    freqs = rope_base ** (-jnp.arange(half_dim, dtype=jnp.float32) / half_dim)
    angles = positions.astype(jnp.float32)[:, None] * freqs[None, :]
    return (jnp.cos(angles), jnp.sin(angles))


def rotate(values, cosine, sine_tab):
    half_dim = values.shape[-1] // 2
    first_half = values[..., :half_dim]
    second_half = values[..., half_dim:]
    return jnp.concatenate(
        [
            first_half * cosine - second_half * sine_tab,
            second_half * cosine + first_half * sine_tab,
        ],
        -1,
    )


def silu_grad(values):
    sigmoid = jax.nn.sigmoid(values)
    return sigmoid * (1.0 + values * (1.0 - sigmoid))


def attention_scores(queries, key_nope, rope_keys, allowed):
    nope_part = jnp.einsum(
        "qhd,khd->hqk", queries[..., :NOPE], key_nope, preferred_element_type=jnp.float32
    )
    rope_part = jnp.einsum(
        "qhr,kr->hqk", queries[..., NOPE:], rope_keys, preferred_element_type=jnp.float32
    )
    scores = (nope_part + rope_part) * (NOPE + ROPE) ** (-0.5)
    return jnp.where(allowed[None], scores, masked_score)


def body(
    hidden_in,
    cotangent,
    segments,
    routes,
    attn_norm,
    w_query,
    w_latent,
    latent_norm,
    w_expand,
    w_output,
    ffn_norm,
    w_router,
    shared_gate,
    shared_up,
    shared_down,
    expert_gate,
    routed_expert_up,
    expert_down,
):
    tokens = hidden_in.shape[0]
    model_width = hidden_in.shape[1]
    devices = lax.axis_size("expert")
    own_index = lax.axis_index("expert")
    top_count = routes.shape[1]
    local_experts = expert_gate.shape[0]
    capacity = tokens * top_count * 2 // (local_experts * devices)
    head_count = w_query.shape[1] // (NOPE + ROPE)
    score_scale = (NOPE + ROPE) ** (-0.5)
    share_width = model_width // lax.axis_size("tensor")
    column_start = lax.axis_index("tensor") * share_width

    def part_move(rows):
        return lax.all_to_all(rows, "expert", split_axis=0, concat_axis=0, tiled=True)

    def to_experts(rows):
        piece = lax.dynamic_slice_in_dim(rows, column_start, share_width, 1)
        return lax.all_gather(part_move(piece), "tensor", axis=1, tiled=True)

    def ffn_reduce(terms):
        return (
            lax.psum_scatter(
                terms[0].astype(jnp.bfloat16), "tensor", scatter_dimension=3, tiled=True
            ).astype(jnp.float32),
            lax.psum_scatter(
                terms[1].astype(jnp.bfloat16), "tensor", scatter_dimension=1, tiled=True
            ).astype(jnp.float32),
        )

    gathered = (
        *in_one_piece(
            (
                attn_norm.astype(jnp.bfloat16),
                w_query.astype(jnp.bfloat16),
                w_latent.astype(jnp.bfloat16),
            ),
            "expert",
            0,
            1,
        ),
        *in_one_piece(
            (latent_norm.astype(jnp.bfloat16), w_expand.astype(jnp.bfloat16)), "expert", 0, 1
        ),
        lax.all_gather(w_output.astype(jnp.bfloat16), "expert", axis=1, tiled=True),
        *in_one_piece(
            (
                ffn_norm.astype(jnp.bfloat16),
                w_router.astype(jnp.bfloat16),
                shared_gate.astype(jnp.bfloat16),
                shared_up.astype(jnp.bfloat16),
            ),
            "expert",
            0,
            1,
        ),
        lax.all_gather(shared_down.astype(jnp.bfloat16), "expert", axis=1, tiled=True),
    )
    (
        gain_one,
        query_w,
        latent_w,
        gain_latent,
        expand_w,
        output_w,
        gain_two,
        router_w,
        sgate_w,
        sup_w,
        sdown_w,
    ) = gathered
    first_row = own_index * tokens
    row_index = first_row + jnp.arange(tokens, dtype=jnp.int32)
    own_segments = lax.dynamic_slice_in_dim(segments, first_row, tokens)
    doc_start = jnp.searchsorted(segments, own_segments, side="left")
    cosine, sine_tab = rope_tables(row_index - doc_start)
    cos_head = cosine[:, None, :]
    sin_head = sine_tab[:, None, :]
    resid_in = hidden_in.astype(jnp.float32)
    normed_f, inverse_one = rms_forward(resid_in, gain_one.astype(jnp.float32))
    normed = normed_f.astype(jnp.bfloat16)
    query_pre = product(normed, query_w).reshape(tokens, head_count, NOPE + ROPE)
    queries = jnp.concatenate(
        [query_pre[..., :NOPE], rotate(query_pre[..., NOPE:], cos_head, sin_head)], -1
    ).astype(jnp.bfloat16)
    latent = product(normed, latent_w)
    compressed_f, inverse_kv = rms_forward(latent[:, :RANK], gain_latent.astype(jnp.float32))
    key_row = jnp.concatenate(
        [
            compressed_f.astype(jnp.bfloat16),
            rotate(latent[:, RANK:], cosine, sine_tab).astype(jnp.bfloat16),
        ],
        1,
    )
    reach_back = (WINDOW + tokens - 2) // tokens
    pieces = [key_row]
    for offset in range(1, reach_back + 1):
        pieces.insert(0, shifted(key_row, "expert", offset))
    keys_all = jnp.concatenate(pieces, 0)
    key_count = keys_all.shape[0]
    key_index = first_row - reach_back * tokens + jnp.arange(key_count, dtype=jnp.int32)
    key_segments = jnp.take(segments, jnp.clip(key_index, 0, segments.shape[0] - 1))
    distance = row_index[:, None] - key_index[None, :]
    allowed = (
        (key_index[None, :] >= 0)
        & (distance >= 0)
        & (distance < WINDOW)
        & (own_segments[:, None] == key_segments[None, :])
    )
    latent_all = keys_all[:, :RANK]
    rope_keys = keys_all[:, RANK:]
    expanded = (
        product(latent_all, expand_w).astype(jnp.bfloat16).reshape(key_count, head_count, NOPE + VH)
    )
    key_nope = expanded[..., :NOPE]
    values_all = expanded[..., NOPE:]
    masked = attention_scores(queries, key_nope, rope_keys, allowed)
    row_max = jnp.max(masked, -1, keepdims=True)
    exponent = jnp.exp(masked - row_max)
    totals = jnp.sum(exponent, -1, keepdims=True)
    log_total = row_max + jnp.log(totals)
    probabilities = (exponent / totals).astype(jnp.bfloat16)
    attended = (
        jnp.einsum("hqk,khd->qhd", probabilities, values_all, preferred_element_type=jnp.float32)
        .astype(jnp.bfloat16)
        .reshape(tokens, head_count * VH)
    )
    attn_out = over_copies(product(attended, output_w), "tensor")
    middle = resid_in + attn_out
    normed_two_f, inverse_two = rms_forward(middle, gain_two.astype(jnp.float32))
    normed_two = normed_two_f.astype(jnp.bfloat16)
    logits = product(normed_two, router_w)
    expert_ids = jnp.arange(router_w.shape[1], dtype=jnp.int32)
    choose = (routes[:, :, None] == expert_ids[None, None, :]).astype(jnp.float32)
    chosen = jnp.sum(logits[:, None, :] * choose, -1)
    gate_weights = jax.nn.softmax(chosen, -1)
    shared_gate_pre = product(normed_two, sgate_w)
    shared_up_pre = product(normed_two, sup_w)
    shared_hidden = (jax.nn.silu(shared_gate_pre) * shared_up_pre).astype(jnp.bfloat16)
    shared_part = product(shared_hidden, sdown_w)
    flat_routes = routes.reshape(-1)
    onehot = (flat_routes[:, None] == expert_ids[None, :]).astype(jnp.int32)
    rank_in = jnp.sum(jnp.cumsum(onehot, 0) * onehot, 1) - 1
    slot_index = flat_routes * capacity + rank_in
    token_of = jnp.arange(flat_routes.shape[0], dtype=jnp.int32) // top_count
    slot_count = router_w.shape[1] * capacity
    send_rows = (
        jnp.zeros((slot_count, model_width), jnp.bfloat16).at[slot_index].set(normed_two[token_of])
    )
    arrived_rows = to_experts(send_rows).reshape(devices, local_experts, capacity, model_width)
    egate_w = expert_gate.astype(jnp.bfloat16)
    routed_up_weight = routed_expert_up.astype(jnp.bfloat16)
    edown_w = expert_down.astype(jnp.bfloat16)
    expert_gate_linear = jnp.einsum(
        "qzbi,zin->qzbn", arrived_rows, egate_w, preferred_element_type=jnp.float32
    )
    expert_up_pre = jnp.einsum(
        "qzbi,zin->qzbn", arrived_rows, routed_up_weight, preferred_element_type=jnp.float32
    )
    expert_hidden = (jax.nn.silu(expert_gate_linear) * expert_up_pre).astype(jnp.bfloat16)
    expert_part = jnp.einsum(
        "secf,efd->secd", expert_hidden, edown_w, preferred_element_type=jnp.float32
    )
    expert_sum, shared_out = ffn_reduce((expert_part, shared_part))
    grad_final = cotangent.astype(jnp.float32)
    returned_share = part_move(expert_sum.astype(jnp.bfloat16).reshape(slot_count, share_width))
    picked_share = (
        returned_share[slot_index].astype(jnp.float32).reshape(tokens, top_count, share_width)
    )
    combined_share = jnp.sum(gate_weights[..., None] * picked_share, 1) + shared_out
    grad_share = lax.dynamic_slice_in_dim(grad_final, column_start, share_width, 1)
    gate_share = jnp.sum(grad_share[:, None, :] * picked_share, -1)
    joined, gate_parts = tuple(
        (
            part.astype(jnp.float32)
            for part in gather_together(
                (combined_share.astype(jnp.bfloat16), gate_share[None].astype(jnp.bfloat16)),
                "tensor",
                (1, 0),
            )
        )
    )
    layer_out = middle + joined
    grad_gates = jnp.sum(gate_parts, 0)
    (
        gain_one,
        query_w,
        latent_w,
        gain_latent,
        expand_w,
        output_w,
        gain_two,
        router_w,
        sgate_w,
        sup_w,
        sdown_w,
    ) = gathered
    grad_shared = grad_final.astype(jnp.bfloat16)
    grad_sdown_w = contract_rows(shared_hidden, grad_shared)
    grad_shidden = contract_cols(grad_shared, sdown_w)
    grad_sgate = (grad_shidden * shared_up_pre * silu_grad(shared_gate_pre)).astype(jnp.bfloat16)
    grad_sup = (grad_shidden * jax.nn.silu(shared_gate_pre)).astype(jnp.bfloat16)
    grad_sgate_w = contract_rows(normed_two, grad_sgate)
    grad_sup_w = contract_rows(normed_two, grad_sup)
    shared_back = contract_cols(grad_sgate, sgate_w) + contract_cols(grad_sup, sup_w)
    grad_chosen = gate_weights * (
        grad_gates - jnp.sum(gate_weights * grad_gates, -1, keepdims=True)
    )
    grad_logits = jnp.sum(grad_chosen[:, :, None] * choose, 1)
    router_f = router_w.astype(jnp.float32)
    grad_router_w = lax.dot_general(
        normed_two.astype(jnp.float32),
        grad_logits,
        (((0,), (0,)), ((), ())),
        preferred_element_type=jnp.float32,
    )
    router_back = lax.dot_general(
        grad_logits, router_f, (((1,), (1,)), ((), ())), preferred_element_type=jnp.float32
    )
    grad_rows = (
        (gate_weights[..., None] * grad_final[:, None, :])
        .reshape(-1, model_width)
        .astype(jnp.bfloat16)
    )
    send_grads = jnp.zeros((slot_count, model_width), jnp.bfloat16).at[slot_index].set(grad_rows)
    grad_recv = to_experts(send_grads).reshape(devices, local_experts, capacity, model_width)
    grad_edown_w = jnp.einsum(
        "secf,secd->efd", expert_hidden, grad_recv, preferred_element_type=jnp.float32
    )
    gradient_expert_hidden = jnp.einsum(
        "secd,efd->secf", grad_recv, edown_w, preferred_element_type=jnp.float32
    )
    grad_egate = (gradient_expert_hidden * expert_up_pre * silu_grad(expert_gate_linear)).astype(
        jnp.bfloat16
    )
    gradient_expert_up = (gradient_expert_hidden * jax.nn.silu(expert_gate_linear)).astype(
        jnp.bfloat16
    )
    grad_egate_w = jnp.einsum(
        "ojwv,ojwa->jva", arrived_rows, grad_egate, preferred_element_type=jnp.float32
    )
    gradient_routed_up_weight = jnp.einsum(
        "ojwv,ojwa->jva", arrived_rows, gradient_expert_up, preferred_element_type=jnp.float32
    )
    expert_back = jnp.einsum(
        "yjvr,jtr->yjvt", grad_egate, egate_w, preferred_element_type=jnp.float32
    ) + jnp.einsum(
        "yjvr,jtr->yjvt", gradient_expert_up, routed_up_weight, preferred_element_type=jnp.float32
    )
    expert_back_sum, shared_back_sum = ffn_reduce((expert_back, shared_back))
    back_share = part_move(expert_back_sum.astype(jnp.bfloat16).reshape(slot_count, share_width))
    routed_share = jnp.sum(
        back_share[slot_index].astype(jnp.float32).reshape(tokens, top_count, share_width), 1
    )
    grad_normed_two = gather_directly(routed_share + shared_back_sum, "tensor", 1) + router_back
    grad_mid_part, grad_gain_two = rms_backward(
        middle, inverse_two, gain_two.astype(jnp.float32), grad_normed_two
    )
    grad_middle = grad_final + grad_mid_part
    grad_attn = grad_middle.astype(jnp.bfloat16)
    grad_output_w = contract_rows(attended, grad_attn)
    grad_attended = (
        contract_cols(grad_attn, output_w).astype(jnp.bfloat16).reshape(tokens, head_count, VH)
    )
    masked_again = attention_scores(queries, key_nope, rope_keys, allowed)
    probs_full = jnp.exp(masked_again - log_total)
    probs_low = probs_full.astype(jnp.bfloat16)
    grad_values = jnp.einsum(
        "hqk,qhd->khd", probs_low, grad_attended, preferred_element_type=jnp.float32
    )
    grad_probs = jnp.einsum(
        "qhd,khd->hqk", grad_attended, values_all, preferred_element_type=jnp.float32
    )
    grad_scores = (
        probs_full * (grad_probs - jnp.sum(probs_full * grad_probs, -1, keepdims=True))
    ).astype(jnp.bfloat16)
    grad_qnope = (
        jnp.einsum("hqk,khd->qhd", grad_scores, key_nope, preferred_element_type=jnp.float32)
        * score_scale
    )
    grad_qrope = (
        jnp.einsum("hqk,kr->qhr", grad_scores, rope_keys, preferred_element_type=jnp.float32)
        * score_scale
    )
    grad_knope = (
        jnp.einsum(
            "hqk,qhd->khd", grad_scores, queries[..., :NOPE], preferred_element_type=jnp.float32
        )
        * score_scale
    )
    grad_krope = (
        jnp.einsum(
            "hqk,qhr->kr", grad_scores, queries[..., NOPE:], preferred_element_type=jnp.float32
        )
        * score_scale
    )
    expand_cols = head_count * (NOPE + VH)
    grad_keys = jnp.concatenate(
        [
            jnp.concatenate([grad_knope, grad_values], -1).reshape(key_count, expand_cols),
            grad_krope,
        ],
        1,
    )
    grad_own = grad_keys[reach_back * tokens :]
    for offset in range(1, reach_back + 1):
        block_start = (reach_back - offset) * tokens
        grad_own = grad_own + shifted(
            grad_keys[block_start : block_start + tokens].astype(jnp.bfloat16), "expert", -offset
        ).astype(jnp.float32)
    grad_expanded = grad_own[:, :expand_cols].astype(jnp.bfloat16)
    own_latent = key_row[:, :RANK]
    grad_expand_w = contract_rows(own_latent, grad_expanded)
    latent_part = jnp.concatenate(
        [contract_cols(grad_expanded, expand_w), grad_own[:, expand_cols:]], 1
    )
    grad_query_pre = (
        jnp.concatenate([grad_qnope, rotate(grad_qrope, cos_head, -sin_head)], -1)
        .astype(jnp.bfloat16)
        .reshape(tokens, head_count * (NOPE + ROPE))
    )
    grad_query_w = contract_rows(normed, grad_query_pre)
    query_back = contract_cols(grad_query_pre, query_w)
    query_back_sum, latent_sum = (
        taken_together(query_back.astype(jnp.bfloat16), "tensor").astype(jnp.float32),
        taken_together(latent_part.astype(jnp.bfloat16), "tensor").astype(jnp.float32),
    )
    grad_compressed, grad_gain_latent = rms_backward(
        latent[:, :RANK], inverse_kv, gain_latent.astype(jnp.float32), latent_sum[:, :RANK]
    )
    grad_latent_rows = jnp.concatenate(
        [grad_compressed, rotate(latent_sum[:, RANK:], cosine, -sine_tab)], 1
    ).astype(jnp.bfloat16)
    grad_latent_w = contract_rows(normed, grad_latent_rows)
    grad_normed = query_back_sum + contract_cols(grad_latent_rows, latent_w)
    grad_in_part, grad_gain_one = rms_backward(
        resid_in, inverse_one, gain_one.astype(jnp.float32), grad_normed
    )
    grad_input = (grad_middle + grad_in_part).astype(jnp.bfloat16)
    scattered = (
        *tuple(
            (
                part.astype(jnp.float32)
                for part in in_one_piece_2(
                    (
                        grad_gain_one.astype(jnp.bfloat16),
                        grad_query_w.astype(jnp.bfloat16),
                        grad_latent_w.astype(jnp.bfloat16),
                    ),
                    "expert",
                    0,
                    1,
                )
            )
        ),
        lax.psum_scatter(
            grad_gain_latent.astype(jnp.bfloat16), "expert", scatter_dimension=0, tiled=True
        ).astype(jnp.float32),
        lax.psum_scatter(
            grad_expand_w.astype(jnp.bfloat16), "expert", scatter_dimension=0, tiled=True
        ).astype(jnp.float32),
        lax.psum_scatter(
            grad_output_w.astype(jnp.bfloat16), "expert", scatter_dimension=1, tiled=True
        ).astype(jnp.float32),
        *tuple(
            (
                part.astype(jnp.float32)
                for part in in_one_piece_2(
                    (
                        grad_gain_two.astype(jnp.bfloat16),
                        grad_router_w.astype(jnp.bfloat16),
                        grad_sgate_w.astype(jnp.bfloat16),
                        grad_sup_w.astype(jnp.bfloat16),
                    ),
                    "expert",
                    0,
                    1,
                )
            )
        ),
        lax.psum_scatter(
            grad_sdown_w.astype(jnp.bfloat16), "expert", scatter_dimension=1, tiled=True
        ).astype(jnp.float32),
    )
    (
        out_gain_one,
        out_query,
        out_latent,
        out_gain_latent,
        out_expand,
        out_output,
        out_gain_two,
        out_router,
        out_sgate,
        out_sup,
        out_sdown,
    ) = scattered
    return (
        layer_out.astype(jnp.bfloat16),
        grad_input,
        out_gain_one,
        out_query,
        out_latent,
        out_gain_latent,
        out_expand,
        out_output,
        out_gain_two,
        out_router,
        out_sgate,
        out_sup,
        out_sdown,
        grad_egate_w,
        gradient_routed_up_weight,
        grad_edown_w,
    )


def solution(mesh):
    in_specs = (
        P("expert", None),
        P("expert", None),
        P(),
        P("expert", None),
        P("expert"),
        P("expert", "tensor"),
        P("expert", None),
        P("expert"),
        P("expert", "tensor"),
        P("tensor", "expert"),
        P("expert"),
        P("expert", None),
        P("expert", "tensor"),
        P("expert", "tensor"),
        P("tensor", "expert"),
        P("expert", None, "tensor"),
        P("expert", None, "tensor"),
        P("expert", "tensor", None),
    )
    out_specs = (
        P("expert", None),
        P("expert", None),
        P("expert"),
        P("expert", "tensor"),
        P("expert", None),
        P("expert"),
        P("expert", "tensor"),
        P("tensor", "expert"),
        P("expert"),
        P("expert", None),
        P("expert", "tensor"),
        P("expert", "tensor"),
        P("tensor", "expert"),
        P("expert", None, "tensor"),
        P("expert", None, "tensor"),
        P("expert", "tensor", None),
    )
    return jax.shard_map(body, mesh=mesh, in_specs=in_specs, out_specs=out_specs, check_vma=False)
```

profile of v0, /device:TPU:0, one launch (start us, length us, event | category | flops | bytes accessed | tf_op | source)
XLA Modules:
  0.0 1120.6 jit_solution(14841992443655625176)
XLA Ops:
  19.2 15.8 %while.24 = (s32[]{:T(128)}, u32[128]{0:T(128)S(1)}, u32[128]{0:T(128)S(1)}, s32[4096]{0:T(1024)S(1)}, s32[128]{0:T(128)S(1)}, /*index=5*/s32[]{:T(128)}, s32[]{:T(128)}, s32[]{}) while((s32[]{:T(128)}, u32[128]{0:T(128)S(1)}, u32[128]{0:T(128)S(1)}, s32[4096]{0:T(1024)S(1)}, s32[128]{0:T(128)S(1)}, /*index=5*/s32[]{:T(128)}, ...), condition=%wide.region_3.4_spmd.clone, body=%wide.region_2.3_spmd.clone.sunk | while | flops 2692 | bytes 10868 | solution.py:239
  35.1 6.5 gather_fusion.1
  42.7 13.8 %all-gather.12.cloned.1.call-done = bf16[512,1025]{1,0:T(8,128)(2,1)} async-done(((bf16[16,1025]{1,0:T(8,128)(2,1)}), bf16[512,1025]{1,0:T(8,128)(2,1)}) %all-gather.12.cloned.1.call-update) | async-done | bytes 1049616 | tf_op jit(solution)/shard_map/all_gather | solution.py:21
  57.5 49.5 %all-gather.10.cloned.1.call-done = bf16[2048,1345]{1,0:T(8,128)(2,1)} async-done(((bf16[64,1345]{1,0:T(8,128)(2,1)}), bf16[2048,1345]{1,0:T(8,128)(2,1)}) %all-gather.10.cloned.1.call-update) | async-done | bytes 5509136 | tf_op jit(solution)/shard_map/all_gather | solution.py:21
  108.4 4.4 fusion.61
  119.5 3.5 collective-permute-start.2
  123.0 3.0 collective-permute-start.3
  126.0 4.4 collective-permute-start.4
  137.7 3.4 collective-permute-start.7
  146.6 13.1 %all-gather.14.cloned.1.call-done = bf16[512,2048]{0,1:T(8,128)(2,1)} async-done(((bf16[512,64]{0,1:T(8,128)(2,1)}), bf16[512,2048]{0,1:T(8,128)(2,1)}) %all-gather.14.cloned.1.call-update) | async-done | bytes 2097168 | tf_op jit(solution)/shard_map/all_gather | solution.py:209
  164.7 5.0 all-to-all-start
  172.8 38.2 %all-gather.16.cloned.1.call-done = bf16[2048,1473]{1,0:T(8,128)(2,1)} async-done(((bf16[64,1473]{1,0:T(8,128)(2,1)}), bf16[2048,1473]{1,0:T(8,128)(2,1)}) %all-gather.16.cloned.1.call-update) | async-done | bytes 6033424 | tf_op jit(solution)/shard_map/all_gather | solution.py:21
  212.2 7.0 all-to-all-done
  219.3 3.6 reduce_sum.212
  225.9 40.6 %scatter_custom_fusion = bf16[1536,2048]{1,0:T(8,128)(2,1)} fusion(s32[768]{0:T(1024)S(1)} %fusion.142, bf16[128,2048]{1,0:T(8,128)(2,1)} %multiply_convert_fusion.3, s32[1024]{0:T(1024)S(1)} %pad_clamp_fusion.3, bf16[]{:T(256)} %constant.126.clone.1), kind=kCustom, calls=%fused_computation.47 | custom fusion | bytes 6291968 | tf_op jit(solution)/shard_map/scatter | solution.py:312
  268.0 27.5 %all_to_all.68 = bf16[32,48,512]{2,1,0:T(8,128)(2,1)} all-to-all(bf16[32,48,512]{2,1,0:T(8,128)(2,1)S(1)} %bitcast.195), channel_id=1, replica_groups=mesh['expert'=32,'tensor'=4] {'expert'}, dimensions={0} | all-to-all | bytes 3145728 | tf_op jit(solution)/shard_map/all_to_all | solution.py:179
  295.6 5.4 mul.546
  300.9 8.6 mul.547
  311.7 15.7 %scatter_custom_fusion.1 = bf16[1536,2048]{1,0:T(8,128)(2,1)} fusion(s32[768]{0:T(1024)S(1)} %fusion.142, f32[768,2048]{1,0:T(8,128)} %mul.547, f32[768]{0:T(1024)S(1)} %div.100, bf16[]{:T(256)} %constant.126.clone.1), kind=kCustom, calls=%fused_computation.46 | custom fusion | flops 3145728 | bytes 12587010 | tf_op jit(solution)/shard_map/scatter | solution.py:389
  328.9 26.3 %all_to_all.69 = bf16[32,48,512]{2,1,0:T(8,128)(2,1)} all-to-all(bf16[32,48,512]{2,1,0:T(8,128)(2,1)S(1)} %bitcast.196), channel_id=1, replica_groups=mesh['expert'=32,'tensor'=4] {'expert'}, dimensions={0} | all-to-all | bytes 3145728 | tf_op jit(solution)/shard_map/all_to_all | solution.py:179
  357.7 9.4 fusion.7
  367.1 8.0 fusion.5
  375.1 50.5 %all-gather.22.cloned.1.call-done = bf16[1536,2048]{1,0:T(8,128)(2,1)} async-done(((bf16[1536,512]{1,0:T(8,128)(2,1)}), bf16[1536,2048]{1,0:T(8,128)(2,1)}) %all-gather.22.cloned.1.call-update) | async-done | bytes 6291472 | tf_op jit(solution)/shard_map/all_gather | solution.py:183
  425.5 11.0 fusion.52
  436.6 9.9 fusion.24
  446.5 9.9 fusion
  456.4 9.2 convert_bitcast_fusion
  465.6 8.7 all-gather.20.cloned.1.call-done
  474.3 4.1 fusion.156
  478.4 5.3 fusion.31
  483.7 56.2 %reduce-scatter.18.cloned.1.call-done = bf16[32,2,24,512]{3,2,0,1:T(8,128)(2,1)} async-done(((bf16[32,2,24,2048]{3,2,0,1:T(8,128)(2,1)}), bf16[32,2,24,512]{3,2,0,1:T(8,128)(2,1)}) %reduce-scatter.18.cloned.1.call-update) | async-done | bytes 1572880 | tf_op jit(solution)/shard_map/reduce_scatter | solution.py:187
  542.7 7.3 all-to-all-start.4
  550.3 6.7 multiply_convert_fusion.5
  557.7 3.4 fusion.29
  561.1 4.4 fusion.44
  565.6 40.5 %reduce-scatter.14.cloned.1.call-done = bf16[32,2,24,512]{3,2,0,1:T(8,128)(2,1)} async-done(((bf16[32,2,24,2048]{3,2,0,1:T(8,128)(2,1)}), bf16[32,2,24,512]{3,2,0,1:T(8,128)(2,1)}) %reduce-scatter.14.cloned.1.call-update) | async-done | bytes 1572880 | tf_op jit(solution)/shard_map/reduce_scatter | solution.py:187
  608.9 7.3 all-to-all-start.2
  616.3 4.1 convolution_convert_fusion.7
  622.4 3.6 convolution_convert_fusion.2
  626.0 5.0 gather_fusion.3
  641.4 4.3 all-to-all-start.5
  646.1 5.0 gather_fusion.2
  653.5 3.3 multiply_reduce_fusion.2
  658.3 15.0 %all-gather.1 = bf16[4,1,66304]{2,1,0:T(2,128)(2,1)S(1)} all-gather(bf16[1,1,66304]{2,1,0:T(2,128)(2,1)S(1)} %reshape.692), channel_id=2, replica_groups=mesh['expert'=32,'tensor'=4] {'tensor'}, dimensions={0}, use_global_device_ids=true | all-gather | bytes 663040 | tf_op jit(solution)/shard_map/all_gather | solution.py:52
  695.0 6.1 copy.199
  710.8 9.3 collective-permute-done.15
  721.4 6.1 collective-permute-done.14
  732.1 19.6 %collective-permute-done.9 = bf16[128,1088]{1,0:T(8,128)(2,1)S(1)} collective-permute-done((bf16[128,1088]{1,0:T(8,128)(2,1)S(1)}, bf16[128,1088]{1,0:T(8,128)(2,1)S(1)}, u32[]{:S(2)}, u32[]{:S(2)}) %collective-permute-start.9) | collective-permute-done | bytes 278560 | tf_op jit(solution)/shard_map/ppermute | solution.py:32
  761.0 31.6 %concatenate.63 = bf16[2048,1473]{0,1:T(8,128)(2,1)} concatenate(bf16[2048,1]{0,1:T(2,128)(2,1)S(1)} %convert_element_type.472, bf16[2048,64]{0,1:T(8,128)(2,1)S(1)} %fusion.157, bf16[2048,704]{0,1:T(8,128)(2,1)} %convolution_convert_fusion.4, bf16[2048,704]{0,1:T(8,128)(2,1)} %convolution_convert_fusion.3), dimensions={1} | concatenate | bytes 12066816 | tf_op jit(solution)/shard_map/concatenate | solution.py:72
  792.6 8.6 copy.221
  804.2 3.5 all-to-all-start.7
  810.9 6.1 all-to-all-done.7
  817.3 3.6 fusion.47
  822.6 4.6 all-to-all-start.6
  833.0 20.9 %all-to-all-done.6 = bf16[4,128,2048]{2,1,0:T(8,128)(2,1)} async-done(((bf16[4,128,2048]{2,1,0:T(8,128)(2,1)}), bf16[4,128,2048]{2,1,0:T(8,128)(2,1)}, u32[]{:S(2)}, u32[]{:S(2)}) %all-to-all-start.6) | async-done | bytes 2097184 | tf_op jit(solution)/shard_map/all_to_all | solution.py:37
  856.0 4.3 fusion.90
  860.3 29.1 %concatenate.62 = bf16[2048,1345]{0,1:T(8,128)(2,1)} concatenate(bf16[2048,1]{0,1:T(2,128)(2,1)S(1)} %convert_element_type.458, bf16[2048,768]{0,1:T(8,128)(2,1)} %convolution_convert_fusion.1, bf16[2048,576]{0,1:T(8,128)(2,1)} %convolution_convert_fusion.5), dimensions={1} | concatenate | bytes 11018240 | tf_op jit(solution)/shard_map/concatenate | solution.py:72
  889.5 8.3 copy.219
  901.3 8.0 convolution_bitcast_fusion.1
  909.3 8.0 convolution_bitcast_fusion
  917.3 5.1 fusion.10
  922.4 63.7 %all-reduce = bf16[512]{0:T(512)(128)(2,1)S(1)} all-reduce(bf16[512]{0:T(512)(128)(2,1)S(1)} %get-tuple-element.186), channel_id=8, replica_groups=mesh['expert'=32,'tensor'=4] {'expert'}, use_global_device_ids=true, to_apply=%region_35.36.clone | all-reduce | flops 512 | bytes 2048
  990.9 29.0 %reduce-scatter.30.cloned.1.call-done = bf16[64,1473]{1,0:T(8,128)(2,1)} async-done(((bf16[2048,1473]{1,0:T(8,128)(2,1)}), bf16[64,1473]{1,0:T(8,128)(2,1)}) %reduce-scatter.30.cloned.1.call-update) | async-done | bytes 188560
  1025.9 82.7 %reduce-scatter.28.cloned.1.call-done = bf16[64,1345]{1,0:T(8,128)(2,1)} async-done(((bf16[2048,1345]{1,0:T(8,128)(2,1)}), bf16[64,1345]{1,0:T(8,128)(2,1)}) %reduce-scatter.28.cloned.1.call-update) | async-done | bytes 172176
  (430 shorter events, 173.7 us)
Async XLA Ops:
  7.2 12.0 %copy-start = (s32[4096]{0:T(1024)S(1)}, s32[4096]{0:T(1024)}, u32[]{:S(2)}) copy-start(s32[4096]{0:T(1024)} %param.22) | copy-start | bytes 49156
  7.2 49.3 %all-gather.12.cloned.1.call-start = ((), (), s32[]{:S(2)}) async-start(), calls=%async_computation.18 | async-start | bytes 1216512 | tf_op jit(solution)/shard_map/all_gather | solution.py:21
  9.6 97.4 %all-gather.10.cloned.1.call-start = ((), (), s32[]{:S(2)}) async-start(), calls=%async_computation.17 | async-start | bytes 5947392 | tf_op jit(solution)/shard_map/all_gather | solution.py:21
  13.1 146.6 %all-gather.14.cloned.1.call-start = ((), (), s32[]{:S(2)}) async-start(), calls=%async_computation.19 | async-start | bytes 2162688 | tf_op jit(solution)/shard_map/all_gather | solution.py:209
  14.8 196.2 %all-gather.16.cloned.1.call-start = ((), (), s32[]{:S(2)}) async-start(), calls=%async_computation.20 | async-start | bytes 6488064 | tf_op jit(solution)/shard_map/all_gather | solution.py:21
  41.6 71.8 %copy-start.56 = (f32[32]{0:T(128)}, f32[32]{0:T(128)S(1)}, u32[]{:S(2)}) copy-start(f32[32]{0:T(128)S(1)} %multiply_power_fusion) | copy-start | bytes 388
  41.8 71.6 %copy-start.58 = (f32[128]{0:T(128)}, f32[128]{0:T(128)S(1)}, u32[]{:S(2)}) copy-start(f32[128]{0:T(128)S(1)} %subtract_convert_fusion.3) | copy-start | bytes 1540
  42.4 88.1 %copy-start.50 = (f32[128]{0:T(128)}, f32[128]{0:T(128)S(1)}, u32[]{:S(2)}) copy-start(f32[128]{0:T(128)S(1)} %get-tuple-element.234) | copy-start | bytes 1540
  57.5 56.1 %copy-start.46 = (f32[512]{0:T(512)}, f32[512]{0:T(512)S(1)}, u32[]{:S(2)}) copy-start(f32[512]{0:T(512)S(1)} %convert_reduce_fusion.4) | copy-start | bytes 6148
  107.0 23.5 %copy-start.43 = (bf16[2048,1345]{1,0:T(8,128)(2,1)S(1)}, bf16[2048,1345]{1,0:T(8,128)(2,1)}, u32[]{:S(2)}) copy-start(bf16[2048,1345]{1,0:T(8,128)(2,1)} %all-gather.10.cloned.1.call-done) | copy-start | bytes 16527364
  108.4 22.1 %copy-start.40 = (f32[2048]{0:T(1024)}, f32[2048]{0:T(1024)S(1)}, u32[]{:S(2)}) copy-start(f32[2048]{0:T(1024)S(1)} %convert_reduce_fusion.3) | copy-start | bytes 24580
  113.4 19.9 %copy-start.54 = (f32[128]{0:T(128)}, f32[128]{0:T(128)S(1)}, u32[]{:S(2)}) copy-start(f32[128]{0:T(128)S(1)} %get-tuple-element.236) | copy-start | bytes 1540
  113.6 19.8 %copy-start.37 = (f32[128,32]{0,1:T(8,128)}, f32[128,32]{0,1:T(8,128)S(1)}, u32[]{:S(2)}) copy-start(f32[128,32]{0,1:T(8,128)S(1)} %get-tuple-element.229) | copy-start | bytes 49156
  113.7 28.2 %copy-start.16 = (bf16[128,512]{0,1:T(8,128)(2,1)}, bf16[128,512]{0,1:T(8,128)(2,1)S(1)}, u32[]{:S(2)}) copy-start(bf16[128,512]{0,1:T(8,128)(2,1)S(1)} %multiply_convert_fusion.7) | copy-start | bytes 393220
  113.8 19.6 %collective-permute-start = (bf16[128,576]{0,1:T(8,128)(2,1)S(1)}, bf16[128,576]{0,1:T(8,128)(2,1)S(1)}, u32[]{:S(2)}, u32[]{:S(2)}) collective-permute-start(bf16[128,576]{0,1:T(8,128)(2,1)S(1)} %pad_maximum_fusion.4), channel_id=1, source_target_pairs={{0,32},{4,36},{8,40},{12,44},{16,48},{20,52},{24,56},{28,60},{32,6... | collective-permute-start | bytes 442376 | tf_op jit(solution)/shard_map/ppermute | solution.py:32
  116.6 18.2 %collective-permute-start.1 = (bf16[128,576]{0,1:T(8,128)(2,1)S(1)}, bf16[128,576]{0,1:T(8,128)(2,1)S(1)}, u32[]{:S(2)}, u32[]{:S(2)}) collective-permute-start(bf16[128,576]{0,1:T(8,128)(2,1)S(1)} %pad_maximum_fusion.4), channel_id=1, source_target_pairs={{0,28},{4,32},{8,36},{12,40},{16,44},{20,48},{24,52},{28,56},{32,6... | collective-permute-start | bytes 442376 | tf_op jit(solution)/shard_map/ppermute | solution.py:32
  119.5 18.2 %collective-permute-start.2 = (bf16[128,576]{0,1:T(8,128)(2,1)S(1)}, bf16[128,576]{0,1:T(8,128)(2,1)S(1)}, u32[]{:S(2)}, u32[]{:S(2)}) collective-permute-start(bf16[128,576]{0,1:T(8,128)(2,1)S(1)} %pad_maximum_fusion.4), channel_id=1, source_target_pairs={{0,24},{4,28},{8,32},{12,36},{16,40},{20,44},{24,48},{28,52},{32,5... | collective-permute-start | bytes 442376 | tf_op jit(solution)/shard_map/ppermute | solution.py:32
  123.0 18.2 %collective-permute-start.3 = (bf16[128,576]{0,1:T(8,128)(2,1)S(1)}, bf16[128,576]{0,1:T(8,128)(2,1)S(1)}, u32[]{:S(2)}, u32[]{:S(2)}) collective-permute-start(bf16[128,576]{0,1:T(8,128)(2,1)S(1)} %pad_maximum_fusion.4), channel_id=1, source_target_pairs={{0,20},{4,24},{8,28},{12,32},{16,36},{20,40},{24,44},{28,48},{32,5... | collective-permute-start | bytes 442376 | tf_op jit(solution)/shard_map/ppermute | solution.py:32
  126.0 15.2 %collective-permute-start.4 = (bf16[128,576]{0,1:T(8,128)(2,1)S(1)}, bf16[128,576]{0,1:T(8,128)(2,1)S(1)}, u32[]{:S(2)}, u32[]{:S(2)}) collective-permute-start(bf16[128,576]{0,1:T(8,128)(2,1)S(1)} %pad_maximum_fusion.4), channel_id=1, source_target_pairs={{0,16},{4,20},{8,24},{12,28},{16,32},{20,36},{24,40},{28,44},{32,4... | collective-permute-start | bytes 442376 | tf_op jit(solution)/shard_map/ppermute | solution.py:32
  133.3 11.3 %copy-start.25 = (f32[128,768]{0,1:T(8,128)}, f32[128,768]{0,1:T(8,128)S(1)}, u32[]{:S(2)}) copy-start(f32[128,768]{0,1:T(8,128)S(1)} %fusion.39) | copy-start | bytes 1179652
  133.4 8.7 copy-start.33
  133.4 7.9 collective-permute-start.5
  134.8 7.1 collective-permute-start.6
  137.7 4.3 collective-permute-start.7
  146.6 18.0 %copy-start.31 = (bf16[4,128,128]{2,1,0:T(8,128)(2,1)}, bf16[4,128,128]{2,1,0:T(8,128)(2,1)S(1)}, u32[]{:S(2)}) copy-start(bf16[4,128,128]{2,1,0:T(8,128)(2,1)S(1)} %fusion.78) | copy-start | bytes 393220
  164.7 54.6 %all-to-all-start = ((f32[4,128,2048]{2,1,0:T(8,128)}), f32[4,128,2048]{2,1,0:T(8,128)}, u32[]{:S(2)}, u32[]{:S(2)}) async-start(f32[4,128,2048]{2,1,0:T(8,128)} %broadcast_in_dim.53), calls=%async_computation | async-start | bytes 8388608 | tf_op jit(solution)/shard_map/all_to_all | solution.py:37
  169.7 188.0 %all-gather.18.cloned.1.call-start = ((), (), s32[]{:S(2)}) async-start(), calls=%async_computation.21 | async-start | bytes 7864320 | tf_op jit(solution)/shard_map/all_gather | solution.py:183
  224.9 41.5 %copy-start.52 = (f32[128]{0:T(128)}, f32[128]{0:T(128)S(1)}, u32[]{:S(2)}) copy-start(f32[128]{0:T(128)S(1)} %get-tuple-element.238) | copy-start | bytes 1540
  295.5 130.0 %all-gather.22.cloned.1.call-start = ((), (), s32[]{:S(2)}) async-start(), calls=%async_computation.25 | async-start | bytes 7864320 | tf_op jit(solution)/shard_map/all_gather | solution.py:183
  355.2 119.1 %all-gather.20.cloned.1.call-start = ((), (), s32[]{:S(2)}) async-start(), calls=%async_computation.23 | async-start | bytes 3244032 | tf_op jit(solution)/shard_map/all_gather | solution.py:221
  356.9 183.1 %reduce-scatter.18.cloned.1.call-start = ((), (), s32[]{:S(2)}) async-start(), calls=%async_computation.26 | async-start | bytes 7864320 | tf_op jit(solution)/shard_map/reduce_scatter | solution.py:187
  357.6 9.4 copy-start.63
  436.6 9.9 copy-start.21
  436.6 9.9 copy-start.19
  456.4 149.7 %reduce-scatter.14.cloned.1.call-start = ((), (), s32[]{:S(2)}) async-start(), calls=%async_computation.22 | async-start | bytes 7864320 | tf_op jit(solution)/shard_map/reduce_scatter | solution.py:187
  542.7 66.1 %all-to-all-start.4 = ((bf16[32,48,512]{2,1,0:T(8,128)(2,1)}), bf16[32,48,512]{2,1,0:T(8,128)(2,1)}, u32[]{:S(2)}, u32[]{:S(2)}) async-start(bf16[32,48,512]{2,1,0:T(8,128)(2,1)} %bitcast.193), calls=%async_computation.7 | async-start | bytes 3145728 | tf_op jit(solution)/shard_map/all_to_all | solution.py:179
  550.1 86.3 %reduce-scatter.20.cloned.1.call-start = ((), (), s32[]{:S(2)}) async-start(), calls=%async_computation.27 | async-start | bytes 655360 | tf_op jit(solution)/shard_map/reduce_scatter | solution.py:190
  608.9 30.5 %all-to-all-start.2 = ((bf16[32,48,512]{2,1,0:T(8,128)(2,1)}), bf16[32,48,512]{2,1,0:T(8,128)(2,1)}, u32[]{:S(2)}, u32[]{:S(2)}) async-start(bf16[32,48,512]{2,1,0:T(8,128)(2,1)} %bitcast.191), calls=%async_computation.3 | async-start | bytes 3145728 | tf_op jit(solution)/shard_map/all_to_all | solution.py:179
  616.2 40.8 %reduce-scatter.16.cloned.1.call-start = ((), (), s32[]{:S(2)}) async-start(), calls=%async_computation.24 | async-start | bytes 655360 | tf_op jit(solution)/shard_map/reduce_scatter | solution.py:190
  620.4 279.3 %reduce-scatter.26.cloned.1.call-start = ((), (), s32[]{:S(2)}) async-start(), calls=%async_computation.30 | async-start | bytes 3244032 | tf_op jit(solution)/shard_map/reduce_scatter | solution.py:545
  622.4 61.7 %copy-start.44 = (f32[4,128]{1,0:T(4,128)}, f32[4,128]{1,0:T(4,128)S(1)}, u32[]{:S(2)}) copy-start(f32[4,128]{1,0:T(4,128)S(1)} %log_add_fusion) | copy-start | bytes 6148
  641.4 36.1 %all-to-all-start.5 = ((f32[4,128,512]{2,1,0:T(8,128)}), f32[4,128,512]{2,1,0:T(8,128)}, u32[]{:S(2)}, u32[]{:S(2)}) async-start(f32[4,128,512]{2,1,0:T(8,128)} %broadcast_in_dim.54), calls=%async_computation.9 | async-start | bytes 2097152 | tf_op jit(solution)/shard_map/all_to_all | solution.py:37
  645.6 341.1 %reduce-scatter.22.cloned.1.call-start = ((), (), s32[]{:S(2)}) async-start(), calls=%async_computation.28 | async-start | bytes 1081344 | tf_op jit(solution)/shard_map/reduce_scatter | solution.py:523
  703.8 47.9 %copy-start.1 = (f32[1152,1024]{1,0:T(8,128)S(1)}, f32[1152,1024]{1,0:T(8,128)}, u32[]{:S(2)}) copy-start(f32[1152,1024]{1,0:T(8,128)} %copy.199) | copy-start | bytes 14155780
  704.0 16.1 %collective-permute-start.15 = (bf16[128,1088]{1,0:T(8,128)(2,1)S(1)}, bf16[128,1088]{1,0:T(8,128)(2,1)S(1)}, u32[]{:S(2)}, u32[]{:S(2)}) collective-permute-start(bf16[128,1088]{1,0:T(8,128)(2,1)S(1)} %get-tuple-element.206), channel_id=1, source_target_pairs={{32,0},{36,4},{40,8},{44,12},{48,16},{52,20},{56,24},{60,28},{64,3... | collective-permute-start | bytes 835592 | tf_op jit(solution)/shard_map/ppermute | solution.py:32
  705.6 21.9 %collective-permute-start.14 = (bf16[128,1088]{1,0:T(8,128)(2,1)S(1)}, bf16[128,1088]{1,0:T(8,128)(2,1)S(1)}, u32[]{:S(2)}, u32[]{:S(2)}) collective-permute-start(bf16[128,1088]{1,0:T(8,128)(2,1)S(1)} %get-tuple-element.207), channel_id=1, source_target_pairs={{28,0},{32,4},{36,8},{40,12},{44,16},{48,20},{52,24},{56,28},{60,3... | collective-permute-start | bytes 835592 | tf_op jit(solution)/shard_map/ppermute | solution.py:32
  706.9 23.8 %collective-permute-start.13 = (bf16[128,1088]{1,0:T(8,128)(2,1)S(1)}, bf16[128,1088]{1,0:T(8,128)(2,1)S(1)}, u32[]{:S(2)}, u32[]{:S(2)}) collective-permute-start(bf16[128,1088]{1,0:T(8,128)(2,1)S(1)} %get-tuple-element.208), channel_id=1, source_target_pairs={{24,0},{28,4},{32,8},{36,12},{40,16},{44,20},{48,24},{52,28},{56,3... | collective-permute-start | bytes 835592 | tf_op jit(solution)/shard_map/ppermute | solution.py:32
  708.2 23.9 %collective-permute-start.12 = (bf16[128,1088]{1,0:T(8,128)(2,1)S(1)}, bf16[128,1088]{1,0:T(8,128)(2,1)S(1)}, u32[]{:S(2)}, u32[]{:S(2)}) collective-permute-start(bf16[128,1088]{1,0:T(8,128)(2,1)S(1)} %get-tuple-element.209), channel_id=1, source_target_pairs={{20,0},{24,4},{28,8},{32,12},{36,16},{40,20},{44,24},{48,28},{52,3... | collective-permute-start | bytes 835592 | tf_op jit(solution)/shard_map/ppermute | solution.py:32
  709.5 22.6 %collective-permute-start.11 = (bf16[128,1088]{1,0:T(8,128)(2,1)S(1)}, bf16[128,1088]{1,0:T(8,128)(2,1)S(1)}, u32[]{:S(2)}, u32[]{:S(2)}) collective-permute-start(bf16[128,1088]{1,0:T(8,128)(2,1)S(1)} %get-tuple-element.210), channel_id=1, source_target_pairs={{16,0},{20,4},{24,8},{28,12},{32,16},{36,20},{40,24},{44,28},{48,3... | collective-permute-start | bytes 835592 | tf_op jit(solution)/shard_map/ppermute | solution.py:32
  720.1 12.0 %collective-permute-start.10 = (bf16[128,1088]{1,0:T(8,128)(2,1)S(1)}, bf16[128,1088]{1,0:T(8,128)(2,1)S(1)}, u32[]{:S(2)}, u32[]{:S(2)}) collective-permute-start(bf16[128,1088]{1,0:T(8,128)(2,1)S(1)} %get-tuple-element.211), channel_id=1, source_target_pairs={{12,0},{16,4},{20,8},{24,12},{28,16},{32,20},{36,24},{40,28},{44,3... | collective-permute-start | bytes 835592 | tf_op jit(solution)/shard_map/ppermute | solution.py:32
  727.5 24.2 %collective-permute-start.9 = (bf16[128,1088]{1,0:T(8,128)(2,1)S(1)}, bf16[128,1088]{1,0:T(8,128)(2,1)S(1)}, u32[]{:S(2)}, u32[]{:S(2)}) collective-permute-start(bf16[128,1088]{1,0:T(8,128)(2,1)S(1)} %get-tuple-element.212), channel_id=1, source_target_pairs={{8,0},{12,4},{16,8},{20,12},{24,16},{28,20},{32,24},{36,28},{40,32... | collective-permute-start | bytes 835592 | tf_op jit(solution)/shard_map/ppermute | solution.py:32
  730.7 21.4 %copy-start.17 = (bf16[128,512]{0,1:T(8,128)(2,1)S(1)}, bf16[128,512]{0,1:T(8,128)(2,1)}, u32[]{:S(2)}) copy-start(bf16[128,512]{0,1:T(8,128)(2,1)} %copy-done.16) | copy-start | bytes 393220
  730.7 21.0 %collective-permute-start.8 = (bf16[128,1088]{1,0:T(8,128)(2,1)S(1)}, bf16[128,1088]{1,0:T(8,128)(2,1)S(1)}, u32[]{:S(2)}, u32[]{:S(2)}) collective-permute-start(bf16[128,1088]{1,0:T(8,128)(2,1)S(1)} %get-tuple-element.205), channel_id=1, source_target_pairs={{4,0},{8,4},{12,8},{16,12},{20,16},{24,20},{28,24},{32,28},{36,32}... | collective-permute-start | bytes 835592 | tf_op jit(solution)/shard_map/ppermute | solution.py:32
  753.6 235.8 %reduce-scatter.24.cloned.1.call-start = ((), (), s32[]{:S(2)}) async-start(), calls=%async_computation.29 | async-start | bytes 2162688 | tf_op jit(solution)/shard_map/reduce_scatter | solution.py:526
  755.7 264.2 %reduce-scatter.30.cloned.1.call-start = ((), (), s32[]{:S(2)}) async-start(), calls=%async_computation.32 | async-start | bytes 6488064
  804.2 12.8 %all-to-all-start.7 = ((bf16[4,128,576]{1,2,0:T(8,128)(2,1)}), bf16[4,128,576]{1,2,0:T(8,128)(2,1)S(1)}, u32[]{:S(2)}, u32[]{:S(2)}) async-start(bf16[4,128,576]{1,2,0:T(8,128)(2,1)} %broadcast_in_dim.56), calls=%async_computation.11 | async-start | bytes 1179648 | tf_op jit(solution)/shard_map/all_to_all | solution.py:37
  807.7 9.4 copy-start.57
  807.7 9.4 copy-start.59
  807.7 9.6 copy-start.38
  822.6 31.3 %all-to-all-start.6 = ((bf16[4,128,2048]{2,1,0:T(8,128)(2,1)}), bf16[4,128,2048]{2,1,0:T(8,128)(2,1)}, u32[]{:S(2)}, u32[]{:S(2)}) async-start(bf16[4,128,2048]{2,1,0:T(8,128)(2,1)} %broadcast_in_dim.55), calls=%async_computation.10 | async-start | bytes 4194304 | tf_op jit(solution)/shard_map/all_to_all | solution.py:37
  827.2 281.5 %reduce-scatter.28.cloned.1.call-start = ((), (), s32[]{:S(2)}) async-start(), calls=%async_computation.31 | async-start | bytes 5947392
  901.3 16.0 %slice-start = ((s8[6291456]{0:T(1024)(128)(4,1)}), s8[4194304]{0:T(1024)(128)(4,1)S(1)}, s32[]{:S(2)}) async-start(s8[6291456]{0:T(1024)(128)(4,1)} %bitcast.223), calls=%async_computation.33 | async-start | bytes 8388608
  917.3 70.8 %copy-start.26 = (f32[128,2048]{1,0:T(8,128)S(1)}, f32[128,2048]{1,0:T(8,128)}, u32[]{:S(2)}) copy-start(f32[128,2048]{1,0:T(8,128)} %get-tuple-element.244) | copy-start | bytes 3145732
  917.3 70.8 %copy-start.60 = (f32[128]{0:T(128)S(1)}, f32[128]{0:T(128)}, u32[]{:S(2)}) copy-start(f32[128]{0:T(128)} %get-tuple-element.233) | copy-start | bytes 1540
  (41 other events, 144.5 us)
Sparse Core Ops, SparseCore 0:
  10.9 45.5 all-gather.11
  59.3 47.6 all-gather.9
  109.8 49.8 all-gather.13
  162.4 48.5 all-gather.15
  295.6 61.9 all-gather.17
  359.2 66.3 all-gather.21
  428.4 45.8 all-gather.19
  476.7 63.2 reduce-scatter.17
  542.4 63.6 reduce-scatter.13
  608.9 21.0 reduce-scatter.19
  632.4 22.2 reduce-scatter.15
  658.7 111.5 reduce-scatter.25
  774.2 74.8 reduce-scatter.21
  852.5 78.1 reduce-scatter.23
  934.2 85.6 reduce-scatter.29
  1024.0 84.6 reduce-scatter.27
where the time goes:
time: 1130 us; the launch traced here: 1120 us
  waiting for transfers between devices  456 us (40%)
  local copies, waits for them, and re-layouts  215 us (19%)
  matrix products  160 us (14%)
  blocking collectives  133 us (12%)
  other arithmetic  71.9 us (6%)
  starting transfers between devices  68.4 us (6%)
  between operations  16.4 us (1%)
    unnamed x18, waiting for transfers between devices  112 us
    all_gather x3, waiting for transfers between devices, in_one_piece(): result, at, done = (lax.all_gather(both, axis, axis=dim, tiled=True), 0, [])  101 us
    reduce_scatter x2, waiting for transfers between devices, ffn_reduce(): lax.psum_scatter(terms[0].astype(jnp.bfloat16), 'tensor', scatter_dimensi...  96.7 us
    unnamed x1, blocking collectives  63.7 us
    concatenate x2, local copies, waits for them, and re-layouts, in_one_piece_2(): both = jnp.concatenate(columns, axis=along)  60.8 us
    all_to_all x2, blocking collectives, part_move(): lax.all_to_all(rows, 'expert', split_axis=0, concat_axis=0, tiled=True)  53.8 us
    all_gather x2, waiting for transfers between devices, to_experts(): return lax.all_gather(part_move(piece), 'tensor', axis=1, tiled=True)  51.2 us
    scatter x1, local copies, waits for them, and re-layouts, body(): jnp.zeros((slot_count, model_width), jnp.bfloat16).at[slot_index]  40.6 us
  transfers between devices with their start and end apart: 38, of which 20 were waited for; matrix products, arithmetic and copies ran while one was open for 35% of the time, Pallas kernels for 0%

commit v1 on v0

v1 whole, which is shorter than its diff:
```python
import functools

import jax
import jax.numpy as jnp
from jax import lax
from jax.experimental import pallas as pl
from jax.experimental.pallas import tpu as pltpu
from jax.sharding import PartitionSpec as P

NOPE = 128
ROPE = 64
VH = 128
RANK = 512
WINDOW = 1024


epsilon = 1e-06
masked_score = -1e30
rope_base = 10000.0


MESH = pl.DeviceIdType.MESH
HBM = pl.BlockSpec(memory_space=pltpu.HBM)


def place():
    e = lax.axis_index("expert")
    return lax.axis_index("tensor"), e // 8, lax.rem(e // 2, 4), lax.rem(e, 2)


def at(x, z, c):
    return (x * 4 + z) * 2 + c


def wrap(v):
    return lax.rem(v + 4, 4)


def greet(peers):
    barrier = pltpu.get_barrier_semaphore()
    for peer in peers:
        pl.semaphore_signal(barrier, inc=1, device_id=peer, device_id_type=MESH)
    pl.semaphore_wait(barrier, len(peers))


def plane_gather_kernel(src, out, ssem, rsem, dssem, drsem, lsem):
    t, x, z, c = place()
    rows = src.shape[0]
    half, quarter = rows // 2, rows // 4
    sibling = (at(x, z, 1 - c), t)
    along_x = [(at(wrap(x - 1), z, c), t), (at(wrap(x + 1), z, c), t)]
    along_z = [(at(x, wrap(z - 1), c), t), (at(x, wrap(z + 1), c), t)]
    greet([sibling] + along_x + along_z)
    own = pltpu.make_async_copy(src, out.at[at(x, z, c)], lsem)
    own.start()
    sent = []

    def piece(h, j1, j2, part=None):
        if h == 0:
            index = at(wrap(x + j2), wrap(z + j1), c)
        else:
            index = at(wrap(x + j1), wrap(z + j2), c)
        if part is None:
            return index, pl.ds(h * half, half)
        return index, pl.ds(h * half + part * quarter, quarter)

    def send(h, slot, which, device, first):
        index, rows_of = which
        return pltpu.make_async_remote_copy(
            src_ref=src.at[rows_of] if first else out.at[index, rows_of],
            dst_ref=out.at[index, rows_of],
            send_sem=ssem.at[h, slot],
            recv_sem=rsem.at[h, slot],
            device_id=device,
            device_id_type=MESH,
        )

    def across(h, j1, j2):
        index, rows_of = piece(h, j1, j2)
        slot = (h * 4 + j1 % 4) * 4 + j2 % 4
        return pltpu.make_async_remote_copy(
            src_ref=src.at[rows_of] if j1 == 0 and j2 == 0 else out.at[index, rows_of],
            dst_ref=out.at[index, rows_of],
            send_sem=dssem.at[slot],
            recv_sem=drsem.at[slot],
            device_id=sibling,
            device_id_type=MESH,
        )

    def ring(h, stage):
        return along_z if (h == 0) == (stage == 1) else along_x

    def stage_one(h, kind):
        left, right = ring(h, 1)
        if kind == 0:
            return send(h, 0, piece(h, 0, 0), right, True)
        if kind == 1:
            return send(h, 1, piece(h, 0, 0), left, True)
        if kind == 2:
            return send(h, 2, piece(h, -1, 0, 0), right, False)
        return send(h, 3, piece(h, 1, 0, 1), left, False)

    def stage_two(h, j1, kind):
        left, right = ring(h, 2)
        slot = 4 + 4 * (j1 % 4) + kind
        if kind == 0:
            return send(h, slot, piece(h, j1, 0), right, j1 == 0)
        if kind == 1:
            return send(h, slot, piece(h, j1, 0), left, j1 == 0)
        if kind == 2:
            return send(h, slot, piece(h, j1, -1, 0), right, False)
        return send(h, slot, piece(h, j1, 1, 1), left, False)

    def go(copy):
        copy.start()
        sent.append(copy)

    for h in (0, 1):
        go(stage_one(h, 0))
        go(stage_one(h, 1))
        go(stage_two(h, 0, 0))
        go(stage_two(h, 0, 1))
        go(across(h, 0, 0))
    for h in (0, 1):
        for kind, j in ((0, -1), (1, 1)):
            stage_one(h, kind).wait_recv()
            go(stage_one(h, 2 + kind))
            go(stage_two(h, j, 0))
            go(stage_two(h, j, 1))
            go(across(h, j, 0))
    for h in (0, 1):
        for kind, j in ((0, -1), (1, 1)):
            stage_two(h, 0, kind).wait_recv()
            go(stage_two(h, 0, 2 + kind))
            go(across(h, 0, j))
    for h in (0, 1):
        stage_one(h, 2).wait_recv()
        stage_one(h, 3).wait_recv()
        go(stage_two(h, 2, 0))
        go(stage_two(h, 2, 1))
        go(across(h, 2, 0))
    for j1 in (-1, 1, 2):
        for h in (0, 1):
            for kind, j in ((0, -1), (1, 1)):
                stage_two(h, j1, kind).wait_recv()
                go(stage_two(h, j1, 2 + kind))
                go(across(h, j1, j))
    for j1 in (0, -1, 1, 2):
        for h in (0, 1):
            stage_two(h, j1, 2).wait_recv()
            stage_two(h, j1, 3).wait_recv()
            go(across(h, j1, 2))
    for h in (0, 1):
        for j1 in (0, -1, 1, 2):
            for j2 in (0, -1, 1, 2):
                across(h, j1, j2).wait_recv()
    for copy in sent:
        copy.wait_send()
    own.wait()


def plane_gather(rows, collective_id, name):
    grouped = rows.reshape(rows.shape[0] // 8, 8, rows.shape[1])
    gathered = pl.pallas_call(
        plane_gather_kernel,
        out_shape=jax.ShapeDtypeStruct((32, *grouped.shape), rows.dtype),
        in_specs=[HBM],
        out_specs=HBM,
        scratch_shapes=[
            pltpu.SemaphoreType.DMA((2, 20)),
            pltpu.SemaphoreType.DMA((2, 20)),
            pltpu.SemaphoreType.DMA((32,)),
            pltpu.SemaphoreType.DMA((32,)),
            pltpu.SemaphoreType.DMA,
        ],
        compiler_params=pltpu.CompilerParams(
            collective_id=collective_id, has_side_effects=True, vmem_limit_bytes=62 * 2**20
        ),
        cost_estimate=pl.CostEstimate(
            flops=0, bytes_accessed=64 * rows.size * rows.dtype.itemsize, transcendentals=0
        ),
        name=name,
    )(grouped)
    return gathered.reshape(32 * rows.shape[0], rows.shape[1])


class Line:
    def __init__(self, src, out, taken, ssem, rsem):
        e, t = lax.axis_index("expert"), lax.axis_index("tensor")
        self.src, self.out, self.taken, self.ssem, self.rsem = src, out, taken, ssem, rsem
        self.share, self.t = src.shape[0] // 4, t
        self.others = [(e, lax.rem(t + k, 4)) for k in (1, 2, 3)]

    def share_out(self, k):
        device = self.others[k - 1]
        return pltpu.make_async_remote_copy(
            src_ref=self.src.at[pl.ds(device[1] * self.share, self.share)],
            dst_ref=self.taken.at[k - 1],
            send_sem=self.ssem.at[0, k - 1],
            recv_sem=self.rsem.at[0, k - 1],
            device_id=device,
            device_id_type=MESH,
        )

    def pass_on(self, k):
        rows = pl.ds(self.t * self.share, self.share)
        return pltpu.make_async_remote_copy(
            src_ref=self.out.at[rows],
            dst_ref=self.out.at[rows],
            send_sem=self.ssem.at[1, k - 1],
            recv_sem=self.rsem.at[1, k - 1],
            device_id=self.others[k - 1],
            device_id_type=MESH,
        )

    def scatter(self):
        for k in (2, 1, 3):
            self.share_out(k).start()

    def add(self):
        for k in (2, 1, 3):
            self.share_out(k).wait_recv()

        def step(i, carry):
            total = self.src[self.t * self.share + i].astype(jnp.float32)
            for k in range(3):
                total = total + self.taken[k, i].astype(jnp.float32)
            self.out[self.t * self.share + i] = total.astype(self.out.dtype)
            return carry

        lax.fori_loop(0, self.share, step, 0)

    def gather(self):
        for k in (2, 1, 3):
            self.pass_on(k).start()

    def finish(self):
        for k in (2, 1, 3):
            self.pass_on(k).wait_recv()
        for k in (2, 1, 3):
            self.share_out(k).wait_send()
            self.pass_on(k).wait_send()


def line_sum_kernel(src, out, taken, ssem, rsem):
    line = Line(src, out, taken, ssem, rsem)
    greet(line.others)
    line.scatter()
    line.add()
    line.gather()
    line.finish()


def plane_sum_kernel(*refs, count, columns, beside):
    sources, refs = refs[:count], refs[count:]
    if beside:
        side_in, out, side_out, side_taken, side_ssem, side_rsem, *refs = refs
    else:
        out, *refs = refs
    mine, peer, one, two, last_one, last_two, lsem, pssem, prsem, ssem, rsem = refs
    t, x, z, c = place()
    groups = out.shape[0]
    half, quarter = groups // 2, groups // 4
    sibling = (at(x, z, 1 - c), t)
    along_x = [(at(wrap(x - 1), z, c), t), (at(wrap(x + 1), z, c), t)]
    along_z = [(at(x, wrap(z - 1), c), t), (at(x, wrap(z + 1), c), t)]
    if beside:
        line = Line(side_in, side_out, side_taken, side_ssem, side_rsem)
        greet([sibling] + along_x + along_z + line.others)
    else:
        greet([sibling] + along_x + along_z)
    order = (2, 1, 3, 0)
    sent = []

    def target(h, a, b, core):
        if h == 0:
            return at(wrap(x + a), wrap(z + b), core)
        return at(wrap(x + b), wrap(z + a), core)

    def outward(h, a, b):
        copies, start = [], 0
        for i, width in enumerate(columns):
            copies.append(
                pltpu.make_async_remote_copy(
                    src_ref=sources[i].at[target(h, a, b, 1 - c), pl.ds(h * half, half)],
                    dst_ref=peer.at[h, a, b, :, :, pl.ds(start, width)],
                    send_sem=pssem.at[i, h, a, b],
                    recv_sem=prsem.at[i, h, a, b],
                    device_id=sibling,
                    device_id_type=MESH,
                )
            )
            start += width
        return copies

    def inward(h, a, b):
        copies, start = [], 0
        for i, width in enumerate(columns):
            copies.append(
                pltpu.make_async_copy(
                    sources[i].at[target(h, a, b, c), pl.ds(h * half, half)],
                    mine.at[h, a, b, :, :, pl.ds(start, width)],
                    lsem.at[i, h, a, b],
                )
            )
            start += width
        return copies

    def hop(h, slot, src, dst, device):
        return pltpu.make_async_remote_copy(
            src_ref=src,
            dst_ref=dst,
            send_sem=ssem.at[h, slot],
            recv_sem=rsem.at[h, slot],
            device_id=device,
            device_id_type=MESH,
        )

    def ring(h, stage):
        return along_x if (h == 0) == (stage == 1) else along_z

    def first(h, b, side):
        return hop(
            h,
            4 * b + side,
            mine.at[h, 2, b, pl.ds(side * quarter, quarter)],
            one.at[h, b, side],
            ring(h, 1)[1 - side],
        )

    def second(h, b, side):
        return hop(
            h, 4 * b + 2 + side, mine.at[h, 1 + 2 * side, b], two.at[h, b, side], ring(h, 1)[1 - side]
        )

    def third(h, side):
        return hop(
            h,
            16 + side,
            mine.at[h, 0, 2, pl.ds(side * quarter, quarter)],
            last_one.at[h, side],
            ring(h, 2)[1 - side],
        )

    def fourth(h, side):
        return hop(
            h, 18 + side, mine.at[h, 0, 1 + 2 * side], last_two.at[h, side], ring(h, 2)[1 - side]
        )

    def go(copy):
        copy.start()
        sent.append(copy)

    def accumulate(into, sources_of, number):
        def step(i, carry):
            total = into[i].astype(jnp.float32)
            for source in sources_of:
                total = total + source[i].astype(jnp.float32)
            into[i] = total.astype(into.dtype)
            return carry

        lax.fori_loop(0, number, step, 0)

    spots = [(h, a, b) for a in order for b in order for h in (0, 1)]
    for spot in spots:
        for copy in inward(*spot):
            copy.start()
        for copy in outward(*spot):
            go(copy)

    if beside:
        line.scatter()

    def merge(h, a, b):
        for copy in inward(h, a, b):
            copy.wait()
        for copy in outward(h, a, b):
            copy.wait_recv()
        accumulate(mine.at[h, a, b], [peer.at[h, a, b]], half)

    for b in order:
        for h in (0, 1):
            merge(h, 2, b)
            for side in (0, 1):
                go(first(h, b, side))
    for side in (0, 1):
        for b in order:
            for h in (0, 1):
                a = 1 + 2 * side
                merge(h, a, b)
                first(h, b, side).wait_recv()
                accumulate(
                    mine.at[h, a, b, pl.ds(side * quarter, quarter)], [one.at[h, b, side]], quarter
                )
                go(second(h, b, side))

    if beside:
        line.add()
        line.gather()

    def gathered_here(h, b):
        merge(h, 0, b)
        for side in (0, 1):
            second(h, b, side).wait_recv()
        accumulate(mine.at[h, 0, b], [two.at[h, b, 0], two.at[h, b, 1]], half)

    for h in (0, 1):
        gathered_here(h, 2)
        for side in (0, 1):
            go(third(h, side))
    for side in (0, 1):
        b = 1 + 2 * side
        for h in (0, 1):
            gathered_here(h, b)
            third(h, side).wait_recv()
            accumulate(
                mine.at[h, 0, b, pl.ds(side * quarter, quarter)], [last_one.at[h, side]], quarter
            )
            go(fourth(h, side))
    for h in (0, 1):
        gathered_here(h, 0)
        for side in (0, 1):
            fourth(h, side).wait_recv()

        def finish(i, carry, h=h):
            total = mine[h, 0, 0, i].astype(jnp.float32)
            for side in (0, 1):
                total = total + last_two[h, side, i].astype(jnp.float32)
            out[h * half + i] = total
            return carry

        lax.fori_loop(0, half, finish, 0)
    for copy in sent:
        copy.wait_send()
    if beside:
        line.finish()


def plane_sum(parts, collective_id, name, beside=None):
    columns = tuple(part.shape[1] for part in parts)
    width = sum(columns)
    groups = parts[0].shape[0] // 256
    half, quarter = groups // 2, groups // 4
    low = jnp.bfloat16
    count = len(parts)
    vmem = pl.BlockSpec(memory_space=pltpu.VMEM)
    operands = [part.reshape(32, groups, 8, part.shape[1]) for part in parts]
    out_shape = [jax.ShapeDtypeStruct((groups, 8, width), jnp.float32)]
    side = []
    if beside is not None:
        lines, side_width = beside.shape
        operands.append(beside.reshape(lines // 8, 8, side_width))
        out_shape.append(jax.ShapeDtypeStruct((lines // 8, 8, side_width), beside.dtype))
        side = [
            pltpu.VMEM((3, lines // 32, 8, side_width), beside.dtype),
            pltpu.SemaphoreType.DMA((2, 3)),
            pltpu.SemaphoreType.DMA((2, 3)),
        ]
    results = pl.pallas_call(
        functools.partial(
            plane_sum_kernel, count=count, columns=columns, beside=beside is not None
        ),
        out_shape=out_shape,
        in_specs=[HBM] * count + [vmem] * (len(operands) - count),
        out_specs=[vmem] * len(out_shape),
        scratch_shapes=side
        + [
            pltpu.VMEM((2, 4, 4, half, 8, width), low),
            pltpu.VMEM((2, 4, 4, half, 8, width), low),
            pltpu.VMEM((2, 4, 2, quarter, 8, width), low),
            pltpu.VMEM((2, 4, 2, half, 8, width), low),
            pltpu.VMEM((2, 2, quarter, 8, width), low),
            pltpu.VMEM((2, 2, half, 8, width), low),
            pltpu.SemaphoreType.DMA((count, 2, 4, 4)),
            pltpu.SemaphoreType.DMA((count, 2, 4, 4)),
            pltpu.SemaphoreType.DMA((count, 2, 4, 4)),
            pltpu.SemaphoreType.DMA((2, 20)),
            pltpu.SemaphoreType.DMA((2, 20)),
        ],
        compiler_params=pltpu.CompilerParams(
            collective_id=collective_id, has_side_effects=True, vmem_limit_bytes=60 * 2**20
        ),
        cost_estimate=pl.CostEstimate(
            flops=0, bytes_accessed=256 * groups * width * 16, transcendentals=0
        ),
        name=name,
    )(*operands)
    summed = results[0].reshape(groups * 8, width)
    if beside is None:
        return summed
    return summed, results[1].reshape(beside.shape)


def line_sum(rows, collective_id, name):
    groups, width = rows.shape[0] // 8, rows.shape[1]
    vmem = pl.BlockSpec(memory_space=pltpu.VMEM)
    summed = pl.pallas_call(
        line_sum_kernel,
        out_shape=jax.ShapeDtypeStruct((groups, 8, width), rows.dtype),
        in_specs=[vmem],
        out_specs=vmem,
        scratch_shapes=[
            pltpu.VMEM((3, groups // 4, 8, width), rows.dtype),
            pltpu.SemaphoreType.DMA((2, 3)),
            pltpu.SemaphoreType.DMA((2, 3)),
        ],
        compiler_params=pltpu.CompilerParams(
            collective_id=collective_id, has_side_effects=True, vmem_limit_bytes=60 * 2**20
        ),
        cost_estimate=pl.CostEstimate(flops=0, bytes_accessed=40 * rows.size, transcendentals=0),
        name=name,
    )(rows.reshape(groups, 8, width))
    return summed.reshape(rows.shape)


def chip_at(x, z, c, distance):
    place_on = lax.rem(x * 4 + z + 16 + distance, 16)
    return place_on * 2 + c


def reach_back_kernel(src, out, lsem, ssem, rsem, pssem, prsem):
    t, x, z, c = place()
    sibling = (at(x, z, 1 - c), t)
    ahead = [(chip_at(x, z, c, k), t) for k in (1, 2, 3, 4)]
    behind = [(chip_at(x, z, c, -k), t) for k in (1, 2, 3, 4)]
    barrier = pltpu.get_barrier_semaphore()
    for peer in [sibling] + behind:
        pl.semaphore_signal(barrier, inc=1, device_id=peer, device_id_type=MESH)
    pl.semaphore_wait(barrier, 5)
    own = pltpu.make_async_copy(src, out.at[8], lsem)
    own.start()

    def far(k):
        return pltpu.make_async_remote_copy(
            src_ref=src,
            dst_ref=out.at[8 - 2 * k],
            send_sem=ssem.at[k - 1],
            recv_sem=rsem.at[k - 1],
            device_id=ahead[k - 1],
            device_id_type=MESH,
        )

    def near(i):
        return pltpu.make_async_remote_copy(
            src_ref=out.at[8 - 2 * (i + c)],
            dst_ref=out.at[7 - 2 * i],
            send_sem=pssem.at[i],
            recv_sem=prsem.at[i],
            device_id=sibling,
            device_id_type=MESH,
        )

    for k in (4, 3, 2, 1):
        far(k).start()
    own.wait()
    for k in (1, 2, 3, 4):
        far(k).wait_recv()
    for i in range(4):
        near(i).start()
    for i in range(4):
        near(i).wait()
    for k in (1, 2, 3, 4):
        far(k).wait_send()


def reach_back(rows, collective_id, name):
    groups, width = rows.shape[0] // 8, rows.shape[1]
    vmem = pl.BlockSpec(memory_space=pltpu.VMEM)
    keys = pl.pallas_call(
        reach_back_kernel,
        out_shape=jax.ShapeDtypeStruct((9, groups, 8, width), rows.dtype),
        in_specs=[vmem],
        out_specs=vmem,
        scratch_shapes=[
            pltpu.SemaphoreType.DMA,
            pltpu.SemaphoreType.DMA((4,)),
            pltpu.SemaphoreType.DMA((4,)),
            pltpu.SemaphoreType.DMA((4,)),
            pltpu.SemaphoreType.DMA((4,)),
        ],
        compiler_params=pltpu.CompilerParams(
            collective_id=collective_id, has_side_effects=True, vmem_limit_bytes=60 * 2**20
        ),
        cost_estimate=pl.CostEstimate(flops=0, bytes_accessed=200 * rows.size, transcendentals=0),
        name=name,
    )(rows.reshape(groups, 8, width))
    return keys.reshape(9 * rows.shape[0], width)


def send_back_kernel(src, out, held, near_in, far_in, lsem, ssem, rsem, pssem, prsem):
    t, x, z, c = place()
    groups = out.shape[0]
    sibling = (at(x, z, 1 - c), t)
    ahead = [(chip_at(x, z, c, k), t) for k in (1, 2, 3, 4)]
    behind = [(chip_at(x, z, c, -k), t) for k in (1, 2, 3, 4)]
    barrier = pltpu.get_barrier_semaphore()
    for peer in [sibling] + ahead:
        pl.semaphore_signal(barrier, inc=1, device_id=peer, device_id_type=MESH)
    pl.semaphore_wait(barrier, 5)

    def near(i):
        return pltpu.make_async_remote_copy(
            src_ref=src.at[7 - 2 * i],
            dst_ref=near_in.at[i],
            send_sem=pssem.at[i],
            recv_sem=prsem.at[i],
            device_id=sibling,
            device_id_type=MESH,
        )

    def far(k):
        return pltpu.make_async_remote_copy(
            src_ref=held.at[k],
            dst_ref=far_in.at[k - 1],
            send_sem=ssem.at[k - 1],
            recv_sem=rsem.at[k - 1],
            device_id=behind[k - 1],
            device_id_type=MESH,
        )

    for i in (3, 2, 1, 0):
        near(i).start()
    for i in (3, 2, 1, 0):
        near(i).wait_recv()
    for k in (4, 3, 2, 1, 0):

        def step(i, carry, k=k):
            total = src[8 - 2 * k, i].astype(jnp.float32)
            other = near_in[jnp.clip(k - c, 0, 3), i].astype(jnp.float32)
            covered = jnp.logical_and(k - c >= 0, k - c <= 3)
            total = total + jnp.where(covered, other, jnp.zeros_like(other))
            held[k, i] = total.astype(held.dtype)
            return carry

        lax.fori_loop(0, groups, step, 0)
        if k > 0:
            far(k).start()
    for k in (1, 2, 3, 4):
        far(k).wait_recv()

    def last(i, carry):
        total = held[0, i].astype(jnp.float32)
        for k in range(4):
            total = total + far_in[k, i].astype(jnp.float32)
        out[i] = total.astype(out.dtype)
        return carry

    lax.fori_loop(0, groups, last, 0)
    for k in (1, 2, 3, 4):
        far(k).wait_send()
    for i in range(4):
        near(i).wait_send()


def send_back(rows, collective_id, name):
    groups, width = rows.shape[0] // 72, rows.shape[1]
    vmem = pl.BlockSpec(memory_space=pltpu.VMEM)
    own = pl.pallas_call(
        send_back_kernel,
        out_shape=jax.ShapeDtypeStruct((groups, 8, width), rows.dtype),
        in_specs=[vmem],
        out_specs=vmem,
        scratch_shapes=[
            pltpu.VMEM((5, groups, 8, width), rows.dtype),
            pltpu.VMEM((4, groups, 8, width), rows.dtype),
            pltpu.VMEM((4, groups, 8, width), rows.dtype),
            pltpu.SemaphoreType.DMA,
            pltpu.SemaphoreType.DMA((4,)),
            pltpu.SemaphoreType.DMA((4,)),
            pltpu.SemaphoreType.DMA((4,)),
            pltpu.SemaphoreType.DMA((4,)),
        ],
        compiler_params=pltpu.CompilerParams(
            collective_id=collective_id, has_side_effects=True, vmem_limit_bytes=60 * 2**20
        ),
        cost_estimate=pl.CostEstimate(flops=0, bytes_accessed=20 * rows.size, transcendentals=0),
        name=name,
    )(rows.reshape(9, groups, 8, width))
    return own.reshape(8 * groups, width)


def contract(left_side, right_side, left_dim, right_dim):
    return lax.dot_general(
        left_side,
        right_side,
        (((left_dim,), (right_dim,)), ((), ())),
        preferred_element_type=jnp.float32,
    )


def experts_kernel(
    token_rows,
    grad_rows,
    gate_in,
    up_in,
    down_in,
    routed_out,
    back_out,
    gate_out,
    up_out,
    down_out,
    ranks,
    rows_x,
    rows_g,
    weights,
    dots,
    staged,
    gate_up,
    down,
    hidden,
    grads,
    sums_one,
    sums_two,
    in_sem,
    out_sem,
):
    step = pl.program_id(0)
    low = jnp.bfloat16
    units = down_in.shape[1]
    wide = down.shape[0]
    pair_slots = 48
    width = rows_x.shape[2]
    blocks = ranks.shape[0]
    count = rows_x.shape[1]
    part = 256

    def load(k, expert):
        source = (gate_in, up_in, down_in)[k].at[expert]
        return pltpu.make_async_copy(source, staged.at[k], in_sem.at[k])

    def store(k, expert):
        if k == 2:
            source = sums_two.at[pl.ds(0, units)]
        else:
            source = sums_one.at[pl.ds(k * wide, units)]
        target = (gate_out, up_out, down_out)[k].at[expert]
        return pltpu.make_async_copy(source, target, out_sem.at[k])

    def picks(block):
        row = lax.broadcasted_iota(jnp.int32, (pair_slots, 256), 0)
        column = lax.broadcasted_iota(jnp.int32, (pair_slots, 256), 1)
        second = row >= 24
        slot = jnp.where(second, row - 24, row).astype(jnp.float32)
        inside = second == (column >= 128)
        found = []
        for expert in (0, 1):
            rank = ranks[block, expert : expert + 1, :]
            found.append(jnp.logical_and(rank == slot, inside))
        return found

    @pl.when(step == 0)
    def _():
        for k in range(3):
            load(k, 0).start()

    def rank_slots(block):
        square = (128, 128)
        same = lax.broadcasted_iota(jnp.int32, square, 0) == lax.broadcasted_iota(
            jnp.int32, square, 1
        )
        turned = contract(
            jnp.where(same, 1.0, 0.0).astype(low), token_rows[0, :, width:], 1, 1
        )
        first = lax.broadcasted_iota(jnp.int32, (256, 256), 0)
        second = lax.broadcasted_iota(jnp.int32, (256, 256), 1)
        ahead = jnp.logical_and(first < second, (first >= 128) == (second >= 128))
        line = lax.broadcasted_iota(jnp.int32, (8, 256), 0)
        named = jnp.zeros((8, 256), jnp.float32)
        shares = jnp.zeros((8, 256), jnp.float32)
        for expert in (0, 1):
            number = (lax.axis_index("expert") * 2 + expert).astype(jnp.float32)
            match = turned[0:8] == number
            present = jnp.sum(jnp.where(match, 1.0, 0.0), 0, keepdims=True)
            share = jnp.sum(jnp.where(match, turned[8:16] + turned[16:24], 0.0), 0, keepdims=True)
            named = named + jnp.where(line == expert, present, 0.0)
            shares = shares + jnp.where(line == 2 + expert, share, 0.0)
        rank = contract(named.astype(low), jnp.where(ahead, 1.0, 0.0).astype(low), 1, 0)
        rank = jnp.where(named > 0.0, rank, -1.0)
        ranks[block] = jnp.where(line < 2, rank, shares)

    @pl.when(step < blocks)
    def _():
        rank_slots(step)
        found = picks(step)
        pick = jnp.concatenate([jnp.where(f, 1.0, 0.0) for f in found], 0).astype(low)
        from_x = contract(pick, token_rows[0, :, :width], 1, 0).astype(low)
        from_g = contract(pick, grad_rows[0], 1, 0).astype(low)
        here = pl.ds(pl.multiple_of(step * pair_slots, pair_slots), pair_slots)
        for expert in (0, 1):
            lines = slice(expert * pair_slots, (expert + 1) * pair_slots)
            rows_x[expert, here, :] = from_x[lines]
            rows_g[expert, here, :] = from_g[lines]
            shares = ranks[step, 2 + expert : 3 + expert, :]
            weight = jnp.sum(jnp.where(found[expert], shares, 0.0), 1, keepdims=True)
            weights[expert, here, :] = jnp.broadcast_to(weight, (pair_slots, 128))

    for expert in (0, 1):

        @pl.when(step == blocks + expert)
        def _(expert=expert):
            for k in range(3):
                load(k, expert).wait()
            nothing = jnp.zeros((wide - units, width), low)
            gate_up[pl.ds(units, wide - units), :] = nothing
            gate_up[pl.ds(wide + units, wide - units), :] = nothing
            down[pl.ds(units, wide - units), :] = nothing

            def cast(i, carry):
                rows = pl.ds(pl.multiple_of(i * 32, 32), 32)
                gate_up[rows, :] = staged[0, rows, :].astype(low)
                gate_up[pl.ds(pl.multiple_of(wide + i * 32, 32), 32), :] = staged[
                    1, rows, :
                ].astype(low)
                down[rows, :] = staged[2, rows, :].astype(low)
                return carry

            lax.fori_loop(0, units // 32, cast, 0)
            if expert == 0:
                for k in range(3):
                    load(k, 1).start()

            def middle(i, carry):
                rows = pl.ds(pl.multiple_of(i * part, part), part)
                before = contract(rows_x[expert, rows, :], gate_up[...], 1, 1)
                plain = contract(rows_g[expert, rows, :], down[...], 1, 1)
                weight = weights[expert, rows, :][:, 0:1]
                gate, up = before[:, :wide], before[:, wide:]
                sigmoid = 1.0 / (1.0 + jnp.exp(-gate))
                on = gate * sigmoid
                value = on * up
                hidden[rows, :] = (weight * value).astype(low)
                dot = jnp.sum(plain * value, 1, keepdims=True)
                mine = 64 + lax.axis_index("expert") * 2 + expert
                lane = lax.broadcasted_iota(jnp.int32, (part, 128), 1)
                dots[expert, rows, :] = jnp.where(lane == mine, dot, 0.0).astype(low)
                change = weight * plain
                grads[rows, :wide] = (change * up * (sigmoid * (1.0 + gate * (1.0 - sigmoid)))).astype(
                    low
                )
                grads[rows, wide:] = (change * on).astype(low)
                return carry

            lax.fori_loop(0, count // part, middle, 0)
            if expert == 1:
                for k in range(3):
                    store(k, 0).wait()

            def weight_grads(i, carry):
                columns = pl.ds(pl.multiple_of(i * part, part), part)
                sums_one[columns, :] = contract(grads[:, columns], rows_x[expert], 0, 0)
                return carry

            lax.fori_loop(0, 2 * wide // part, weight_grads, 0)
            for i in range(wide // 128):
                columns = pl.ds(i * 128, 128)
                sums_two[columns, :] = contract(hidden[:, columns], rows_g[expert], 0, 0)
            for k in range(3):
                store(k, expert).start()

            def results(i, carry):
                rows = pl.ds(pl.multiple_of(i * part, part), part)
                rows_x[expert, rows, :] = contract(hidden[rows, :], down[...], 1, 0).astype(low)
                rows_g[expert, rows, :] = contract(grads[rows, :], gate_up[...], 1, 0).astype(low)
                return carry

            lax.fori_loop(0, count // part, results, 0)

    @pl.when(step >= blocks + 2)
    def _():
        block = step - blocks - 2
        pick = jnp.concatenate([jnp.where(f, 1.0, 0.0) for f in picks(block)], 0).astype(low)
        here = pl.ds(pl.multiple_of(block * pair_slots, pair_slots), pair_slots)

        def both(ref):
            return jnp.concatenate([ref[0, here, :], ref[1, here, :]], 0)

        routed_out[0] = contract(pick, both(rows_x), 0, 0).astype(low)
        back_out[0, :, :width] = contract(pick, both(rows_g), 0, 0).astype(low)
        back_out[0, :, width:] = contract(pick, both(dots), 0, 0).astype(low)

    @pl.when(step == 2 * blocks + 1)
    def _():
        for k in range(3):
            store(k, 1).wait()


def experts(token_rows, grad_rows, gate, up, down):
    low = jnp.bfloat16
    blocks = token_rows.shape[0]
    local, units, width = down.shape
    wide = (units + 127) // 128 * 128
    count = blocks * 48
    last = blocks - 1

    def entering(i):
        return (jnp.minimum(i, last), 0, 0)

    def leaving(i):
        return (jnp.maximum(i - blocks - 2, 0), 0, 0)

    weight = jax.ShapeDtypeStruct((local, units, width), jnp.float32)
    return pl.pallas_call(
        experts_kernel,
        grid=(2 * blocks + 2,),
        out_shape=(
            jax.ShapeDtypeStruct((blocks, 256, width), low),
            jax.ShapeDtypeStruct((blocks, 256, width + 128), low),
            weight,
            weight,
            weight,
        ),
        in_specs=[
            pl.BlockSpec((1, 256, width + 128), entering),
            pl.BlockSpec((1, 256, width), entering),
            HBM,
            HBM,
            HBM,
        ],
        out_specs=(
            pl.BlockSpec((1, 256, width), leaving),
            pl.BlockSpec((1, 256, width + 128), leaving),
            HBM,
            HBM,
            HBM,
        ),
        scratch_shapes=[
            pltpu.VMEM((blocks, 8, 256), jnp.float32),
            pltpu.VMEM((local, count, width), low),
            pltpu.VMEM((local, count, width), low),
            pltpu.VMEM((local, count, 128), jnp.float32),
            pltpu.VMEM((local, count, 128), low),
            pltpu.VMEM((3, units, width), jnp.float32),
            pltpu.VMEM((2 * wide, width), low),
            pltpu.VMEM((wide, width), low),
            pltpu.VMEM((count, wide), low),
            pltpu.VMEM((count, 2 * wide), low),
            pltpu.VMEM((2 * wide, width), jnp.float32),
            pltpu.VMEM((wide, width), jnp.float32),
            pltpu.SemaphoreType.DMA((3,)),
            pltpu.SemaphoreType.DMA((3,)),
        ],
        compiler_params=pltpu.CompilerParams(
            dimension_semantics=("arbitrary",), vmem_limit_bytes=60 * 2**20
        ),
        cost_estimate=pl.CostEstimate(
            flops=18 * local * count * wide * width,
            bytes_accessed=100 * 2**20,
            transcendentals=local * count * wide,
        ),
        name="experts",
    )(token_rows, grad_rows, gate, up, down)


def rms_forward(values, gains):
    inverse = lax.rsqrt(jnp.mean(values * values, -1, keepdims=True) + epsilon)
    return (values * inverse * gains, inverse)


def rope_tables(positions):
    half_dim = ROPE // 2
    freqs = rope_base ** (-jnp.arange(half_dim, dtype=jnp.float32) / half_dim)
    angles = positions.astype(jnp.float32)[:, None] * freqs[None, :]
    return (jnp.cos(angles), jnp.sin(angles))


HEADS = 4
SCALE = (NOPE + ROPE) ** (-0.5)


def lanes(shape):
    return lax.broadcasted_iota(jnp.int32, shape, 1)


def turn_tables(cosine, sine_tab):
    lane = lanes(cosine.shape)
    kept = jnp.where(lane < 64, cosine, 0.0)
    crossed = jnp.where(lane < 32, -sine_tab, jnp.where(lane < 64, sine_tab, 0.0))
    return kept, crossed


def exchange_halves(values):
    shape = (128, 128)
    to = lanes(shape)
    from_lane = lax.broadcasted_iota(jnp.int32, shape, 0)
    other = jnp.where(to < 32, to + 32, jnp.where(to < 64, to - 32, to))
    swap = jnp.where(from_lane == other, 1.0, 0.0)
    return lax.dot_general(
        values,
        swap,
        (((1,), (0,)), ((), ())),
        precision=lax.Precision.HIGHEST,
        preferred_element_type=jnp.float32,
    )


def fold_matrix():
    shape = (128, 256)
    to = lanes(shape)
    wanted = jnp.where(to >= 128, 32, 0) + lax.rem(to, 32)
    return jnp.where(lax.broadcasted_iota(jnp.int32, shape, 0) == wanted, 1.0, 0.0).astype(
        jnp.bfloat16
    )


def head_lanes(values, head):
    lane = lanes(values.shape)
    inside = jnp.logical_and(lane >= 32 * head, lane < 32 * head + 32)
    return jnp.where(inside, values, jnp.zeros_like(values))


def pack_kernel(
    query,
    latent,
    gain_one,
    gain_two,
    gain_latent,
    output,
    expand,
    gate,
    router,
    up,
    down,
    attention_out,
    ffn_out,
):
    low = jnp.bfloat16
    shard = query.shape[0]
    for head in range(HEADS):
        start = 192 * head
        attention_out[:, 128 * head : 128 * head + 128] = query[:, start : start + 128].astype(low)
    for half in (0, 1):
        starts = [192 * head + 128 + 32 * half for head in range(HEADS)]
        pieces = [query[:, start : start + 32] for start in starts]
        to = 512 + 128 * half
        attention_out[:, to : to + 128] = jnp.concatenate(pieces, 1).astype(low)
    attention_out[:, 768:1280] = latent[:, :RANK].astype(low)
    row = lax.broadcasted_iota(jnp.int32, (shard, shard), 0)
    gains = jnp.where(row == 0, gain_one[...], 0.0)
    gains = jnp.where(row == 1, gain_two[...], gains)
    gains = jnp.where(row == 2, gain_latent[...], gains)
    attention_out[:, 1280:1408] = jnp.concatenate([latent[:, RANK:], gains], 1).astype(low)
    attention_out[:, 1408:1920] = output[...].astype(low)
    for j in range(4):
        attention_out[16 * j : 16 * j + 16, 1920:] = expand[:, 256 * j : 256 * j + 256].astype(low)
    gap = jnp.zeros((shard, 64), jnp.float32)
    for k, (wide, narrow) in enumerate(((gate, router[...]), (up, gap), (down, gap))):
        start = 768 * k
        ffn_out[:, start : start + 640] = wide[:, :640].astype(low)
        ffn_out[:, start + 640 : start + 768] = jnp.concatenate(
            [wide[:, 640:704], narrow], 1
        ).astype(low)


def project_kernel(
    hidden, weights, gain, gain_latent, cosine, sine_tab, normed_out, query_out, key_out, latent_out
):
    low = jnp.bfloat16
    normed = rms_forward(hidden[...].astype(jnp.float32), gain[...])[0].astype(low)
    normed_out[...] = normed
    query = contract(normed, weights[:, :768], 1, 0)
    first, second = query[:, 512:640], query[:, 640:768]
    cos, sin = cosine[...], sine_tab[...]
    query_out[:, :512] = query[:, :512].astype(low)
    query_out[:, 512:640] = (first * cos - second * sin).astype(low)
    query_out[:, 640:768] = (second * cos + first * sin).astype(low)
    latent = contract(normed, weights[:, 768:1408], 1, 0)
    latent_out[...] = latent[:, :RANK]
    key_out[:, :RANK] = rms_forward(latent[:, :RANK], gain_latent[...])[0].astype(low)
    rope = latent[:, RANK:]
    kept, crossed = turn_tables(cos, sin)
    key_out[:, RANK:] = (rope * kept + exchange_halves(rope) * crossed).astype(low)


def attend_kernel(
    keys,
    expand,
    query,
    own_segment,
    key_segment,
    wo_0,
    wo_1,
    wo_2,
    wo_3,
    out,
    attended,
    probs,
    expanded,
    key_rope,
):
    low = jnp.bfloat16
    rows = query.shape[0]
    count = keys.shape[0]
    fold = fold_matrix()

    def expand_rows(i, carry):
        part = pl.ds(pl.multiple_of(i * rows, rows), rows)
        expanded[part, :] = contract(keys[part, :RANK], expand[...], 1, 0).astype(low)
        key_rope[part, :] = contract(keys[part, RANK:], fold, 1, 0).astype(low)
        return carry

    lax.fori_loop(0, count // rows, expand_rows, 0)
    shape = (rows, count)
    distance = lax.broadcasted_iota(jnp.int32, shape, 0) + WINDOW - lanes(shape)
    allowed = jnp.logical_and(distance >= 0, distance < WINDOW)
    allowed = jnp.logical_and(allowed, own_segment[...] == key_segment[...])
    total = jnp.zeros(out.shape, jnp.float32)
    for head, wo in enumerate((wo_0, wo_1, wo_2, wo_3)):
        start = 256 * head
        scores = contract(query[:, 128 * head : 128 * head + 128], expanded[:, start : start + 128], 1, 1)
        scores += contract(head_lanes(query[:, 512:640], head), key_rope[:, :128], 1, 1)
        scores += contract(head_lanes(query[:, 640:768], head), key_rope[:, 128:], 1, 1)
        scores = jnp.where(allowed, scores * SCALE, masked_score)
        exponent = jnp.exp(scores - jnp.max(scores, 1, keepdims=True))
        share = exponent / jnp.sum(exponent, 1, keepdims=True)
        probs[head] = share
        mixed = contract(share.astype(low), expanded[:, start + 128 : start + 256], 1, 0).astype(low)
        attended[:, 128 * head : 128 * head + 128] = mixed
        total += contract(mixed, wo[...], 1, 1)
    out[...] = total.astype(low)


def route_kernel(hidden, attention, gain, router, routes, token_out, middle_out, gates_out):
    low = jnp.bfloat16
    middle = hidden[...].astype(jnp.float32) + attention[...].astype(jnp.float32)
    middle_out[...] = middle
    normed = rms_forward(middle, gain[...])[0].astype(low)
    width = normed.shape[1]
    token_out[:, :width] = normed
    logits = contract(normed, router[...], 1, 0)
    lane = lanes(logits.shape)
    named = [routes[:, r : r + 1] for r in range(6)]
    chosen = [
        jnp.sum(jnp.where(lane == number + 64, logits, 0.0), 1, keepdims=True) for number in named
    ]
    most = functools.reduce(jnp.maximum, chosen)
    exponents = [jnp.exp(value - most) for value in chosen]
    total = functools.reduce(jnp.add, exponents)
    extra = jnp.where(jnp.logical_or(lane == 6, lane == 7), 128.0, 0.0)
    gates = jnp.zeros(logits.shape, jnp.float32)
    for r in range(6):
        weight = exponents[r] / total
        high = weight.astype(low).astype(jnp.float32)
        extra += jnp.where(lane == r, named[r].astype(jnp.float32), 0.0)
        extra += jnp.where(lane == 8 + r, high, 0.0)
        extra += jnp.where(lane == 16 + r, weight - high, 0.0)
        gates += jnp.where(lane == r, weight, 0.0)
    token_out[:, width:] = extra.astype(low)
    gates_out[...] = gates


def shared_kernel(normed, cotangent, weights, part_out, back_out, grads_out):
    low = jnp.bfloat16
    gate = contract(normed[...], weights[:, :768], 1, 0)
    up = contract(normed[...], weights[:, 768:1536], 1, 0)
    sigmoid = 1.0 / (1.0 + jnp.exp(-gate))
    on = gate * sigmoid
    hidden = (on * up).astype(low)
    part_out[...] = contract(hidden, weights[:, 1536:], 1, 1)
    change = contract(cotangent[...], weights[:, 1536:], 1, 0)
    grad_gate = (change * up * (sigmoid * (1.0 + gate * (1.0 - sigmoid)))).astype(low)
    grad_up = (change * on).astype(low)
    back_out[...] = contract(grad_gate, weights[:, :768], 1, 1) + contract(
        grad_up, weights[:, 768:1536], 1, 1
    )

    def grads(i, carry):
        part = pl.ds(pl.multiple_of(i * 256, 256), 256)
        rows = normed[:, part]
        grads_out[part, :768] = contract(rows, grad_gate, 0, 0).astype(low)
        grads_out[part, 768:1536] = contract(rows, grad_up, 0, 0).astype(low)
        grads_out[part, 1536:] = contract(cotangent[:, part], hidden, 0, 0).astype(low)
        return carry

    lax.fori_loop(0, grads_out.shape[0] // 256, grads, 0)


def attend_back_kernel(
    back,
    middle,
    gain,
    gates,
    routes,
    router,
    cotangent,
    wo_0,
    wo_1,
    wo_2,
    wo_3,
    probs,
    expanded,
    key_rope,
    query,
    keys,
    expand,
    query_w,
    cosine,
    sine_tab,
    middle_out,
    attention_out,
    gain_out,
    logits_out,
    query_out,
    back_out,
    keys_out,
    expand_out,
    changes,
    ropes,
):
    low = jnp.bfloat16
    width = middle.shape[1]
    rows = middle.shape[0]
    lane = lanes((rows, 128))
    sums = back[:, width:].astype(jnp.float32)
    named = [routes[:, r : r + 1] for r in range(6)]
    weight = [gates[:, r : r + 1] for r in range(6)]
    change = [
        jnp.sum(jnp.where(lane == number + 64, sums, 0.0), 1, keepdims=True) for number in named
    ]
    inner = functools.reduce(jnp.add, [w * c for w, c in zip(weight, change)])
    logits = jnp.zeros((rows, 128), jnp.float32)
    for r in range(6):
        logits += jnp.where(lane == named[r] + 64, weight[r] * (change[r] - inner), 0.0)
    logits_low = logits.astype(low)
    logits_out[...] = logits_low
    grad_normed = back[:, :width].astype(jnp.float32) + contract(logits_low, router[...], 1, 1)
    values = middle[...]
    inverse = lax.rsqrt(jnp.mean(values * values, 1, keepdims=True) + epsilon)
    weighted = grad_normed * gain[...]
    aligned = jnp.mean(values * weighted, 1, keepdims=True)
    gain_out[...] = jnp.sum(grad_normed * values * inverse, 0, keepdims=True)
    grad_middle = (
        cotangent[...].astype(jnp.float32)
        + inverse * weighted
        - values * (inverse * inverse * inverse) * aligned
    )
    middle_out[...] = grad_middle
    grad_attn = grad_middle.astype(low)
    attention_out[...] = grad_attn
    first = jnp.zeros((rows, 128), jnp.float32)
    second = jnp.zeros((rows, 128), jnp.float32)
    for head, wo in enumerate((wo_0, wo_1, wo_2, wo_3)):
        start = 256 * head
        nope, value = slice(start, start + 128), slice(start + 128, start + 256)
        own = slice(128 * head, 128 * head + 128)
        grad_mixed = contract(grad_attn, wo[...], 1, 0).astype(low)
        share = probs[head]
        changes[:, value] = contract(share.astype(low), grad_mixed, 0, 0).astype(low)
        grad_share = contract(grad_mixed, expanded[:, value], 1, 1)
        grad_scores = share * (grad_share - jnp.sum(share * grad_share, 1, keepdims=True))
        grad_scores = grad_scores.astype(low)
        query_out[:, own] = (contract(grad_scores, expanded[:, nope], 1, 0) * SCALE).astype(low)
        both = contract(grad_scores, key_rope[...], 1, 0) * SCALE
        first += head_lanes(both[:, :128], head)
        second += head_lanes(both[:, 128:], head)
        changes[:, nope] = (contract(grad_scores, query[:, own], 0, 0) * SCALE).astype(low)
        from_first = contract(grad_scores, head_lanes(query[:, 512:640], head), 0, 0) * SCALE
        from_second = contract(grad_scores, head_lanes(query[:, 640:768], head), 0, 0) * SCALE
        if head == 0:
            ropes[:, :128] = from_first
            ropes[:, 128:] = from_second
        else:
            ropes[:, :128] += from_first
            ropes[:, 128:] += from_second
    cos, sin = cosine[...], sine_tab[...]
    query_out[:, 512:640] = (first * cos + second * sin).astype(low)
    query_out[:, 640:768] = (second * cos - first * sin).astype(low)
    back_out[...] = contract(query_out[...], query_w[...], 1, 1).astype(low)
    fold = fold_matrix()

    def key_rows(i, carry):
        part = pl.ds(pl.multiple_of(i * rows, rows), rows)
        keys_out[part, :RANK] = contract(changes[part, :], expand[...], 1, 1).astype(low)
        keys_out[part, RANK:] = contract(ropes[part, :].astype(low), fold, 1, 1).astype(low)
        return carry

    lax.fori_loop(0, keys.shape[0] // rows, key_rows, 0)
    for j in range(4):
        grad_expand = contract(keys[:, :RANK], changes[:, 256 * j : 256 * j + 256], 0, 0)
        expand_out[:, 16 * j : 16 * j + 16, :] = grad_expand.astype(low).reshape(32, 16, 256)


def finish_kernel(
    summed,
    latent,
    gain_latent,
    cosine,
    sine_tab,
    wl_0,
    wl_1,
    wl_2,
    wl_3,
    wl_4,
    hidden,
    gain,
    grad_middle,
    normed,
    grad_attn,
    normed_two,
    grad_logits,
    grad_query,
    attended,
    input_out,
    gain_out,
    gain_latent_out,
    grads_out,
    changes,
):
    low = jnp.bfloat16
    width = hidden.shape[1]
    grad_latent = summed[:, width : width + RANK].astype(jnp.float32)
    rope = summed[:, width + RANK :].astype(jnp.float32)
    values = latent[...]
    inverse = lax.rsqrt(jnp.mean(values * values, 1, keepdims=True) + epsilon)
    weighted = grad_latent * gain_latent[...]
    aligned = jnp.mean(values * weighted, 1, keepdims=True)
    gain_latent_out[...] = jnp.sum(grad_latent * values * inverse, 0, keepdims=True)
    changes[:, :RANK] = (
        inverse * weighted - values * (inverse * inverse * inverse) * aligned
    ).astype(low)
    kept, crossed = turn_tables(cosine[...], sine_tab[...])
    changes[:, RANK:] = (rope * kept - exchange_halves(rope) * crossed).astype(low)
    grad_normed = summed[:, :width].astype(jnp.float32)
    for j, wl in enumerate((wl_0, wl_1, wl_2, wl_3, wl_4)):
        grad_normed += contract(changes[:, 128 * j : 128 * j + 128], wl[...], 1, 1)
    values = hidden[...].astype(jnp.float32)
    inverse = lax.rsqrt(jnp.mean(values * values, 1, keepdims=True) + epsilon)
    weighted = grad_normed * gain[...]
    aligned = jnp.mean(values * weighted, 1, keepdims=True)
    gain_out[...] = jnp.sum(grad_normed * values * inverse, 0, keepdims=True)
    input_out[...] = (
        grad_middle[...] + inverse * weighted - values * (inverse * inverse * inverse) * aligned
    ).astype(low)

    def grads(i, carry):
        part = pl.ds(pl.multiple_of(i * 256, 256), 256)
        rows = normed[:, part]
        grads_out[part, :768] = contract(rows, grad_query[...], 0, 0).astype(low)
        grads_out[part, 768:1280] = contract(rows, changes[:, :RANK], 0, 0).astype(low)
        mixed = contract(rows, changes[:, RANK:], 0, 0)
        mixed += contract(normed_two[:, part], grad_logits[...], 0, 0)
        grads_out[part, 1280:1408] = mixed.astype(low)
        grads_out[part, 1408:] = contract(grad_attn[:, part], attended[...], 0, 0).astype(low)
        return carry

    lax.fori_loop(0, grads_out.shape[0] // 256, grads, 0)


def unpack_kernel(
    own,
    ffn,
    middle,
    layer,
    layer_out,
    query_out,
    latent_out,
    router_out,
    output_out,
    gains_out,
    expand_out,
    gate_out,
    up_out,
    down_out,
):
    layer_out[...] = (middle[...] + layer[...].astype(jnp.float32)).astype(layer_out.dtype)
    for head in range(HEADS):
        query_out[:, 192 * head : 192 * head + 128] = own[:, 128 * head : 128 * head + 128]
        for half in (0, 1):
            to, start = 192 * head + 128 + 32 * half, 512 + 128 * half + 32 * head
            query_out[:, to : to + 32] = own[:, start : start + 32]
    latent_out[...] = own[:, 768:1344]
    router_out[...] = own[:, 1344:1408]
    output_out[...] = own[:, 1408:1920]
    gains_out[...] = own[0:8, 1920:2048]
    for j in range(4):
        expand_out[:, 256 * j : 256 * j + 256] = own[16 * j : 16 * j + 16, 2048:2304]
    gate_out[...] = ffn[:, :704].astype(jnp.float32)
    up_out[...] = ffn[:, 768:1472].astype(jnp.float32)
    down_out[...] = ffn[:, 1536:2240].astype(jnp.float32)


def local_call(kernel, name, operands, out_shapes, scratch=()):
    arrays, specs = [], []
    for operand in operands:
        if isinstance(operand, tuple):
            array, block, index = operand
            specs.append(pl.BlockSpec(block, lambda i, index=index: index))
        else:
            array = operand
            zeros = (0,) * array.ndim
            specs.append(pl.BlockSpec(array.shape, lambda i, zeros=zeros: zeros))
        arrays.append(array)
    shapes = [jax.ShapeDtypeStruct(shape, dtype) for shape, dtype in out_shapes]
    return pl.pallas_call(
        kernel,
        grid=(1,),
        out_shape=shapes,
        in_specs=specs,
        out_specs=[
            pl.BlockSpec(shape.shape, lambda i, zeros=(0,) * len(shape.shape): zeros)
            for shape in shapes
        ],
        scratch_shapes=[pltpu.VMEM(shape, dtype) for shape, dtype in scratch],
        compiler_params=pltpu.CompilerParams(vmem_limit_bytes=60 * 2**20),
        name=name,
    )(*arrays)


def column_blocks(array, first, number):
    return [(array, (array.shape[0], 128), (0, first + j)) for j in range(number)]


def body(
    hidden_in,
    cotangent,
    segments,
    routes,
    attn_norm,
    w_query,
    w_latent,
    latent_norm,
    w_expand,
    w_output,
    ffn_norm,
    w_router,
    shared_gate,
    shared_up,
    shared_down,
    expert_gate,
    routed_expert_up,
    expert_down,
):
    tokens, model_width = hidden_in.shape
    devices = lax.axis_size("expert")
    own_index = lax.axis_index("expert")
    low = jnp.bfloat16
    full = jnp.float32
    shard = w_query.shape[0]

    attention_shard, ffn_shard = local_call(
        pack_kernel,
        "pack",
        (
            w_query,
            w_latent,
            attn_norm[None],
            ffn_norm[None],
            jnp.pad(latent_norm, (0, shard - latent_norm.shape[0]))[None],
            w_output.T,
            w_expand,
            shared_gate,
            w_router,
            shared_up,
            shared_down.T,
        ),
        (((shard, 2176), low), ((shard, 2304), low)),
    )
    ffn_all = lax.all_gather(ffn_shard, "expert", axis=0, tiled=True)
    grad_rows = lax.all_gather(cotangent, "expert", axis=0)
    attention_all = plane_gather(attention_shard, 1, "gather_attention")
    gains = attention_all.reshape(devices, shard, -1)[:, :8, 1344:1408].astype(full)
    gain_one = gains[:, 0].reshape(1, -1)
    gain_two = gains[:, 1].reshape(1, -1)
    gain_latent = gains[:, 2, : latent_norm.shape[0]].reshape(1, -1)
    expand_w = (
        attention_all[:, 1920:].reshape(devices, 4, 16, 256).swapaxes(1, 2).reshape(RANK, -1)
    )
    output_blocks = column_blocks(attention_all, 11, 4)
    latent_blocks = column_blocks(attention_all, 6, 5)
    router_block = column_blocks(ffn_all, 5, 1)[0]

    first_row = own_index * tokens
    row_index = first_row + jnp.arange(tokens, dtype=jnp.int32)
    own_segments = lax.dynamic_slice_in_dim(segments, first_row, tokens)
    doc_start = jnp.sum((segments[None, :] < own_segments[:, None]).astype(jnp.int32), 1)
    cosine, sine_tab = rope_tables(row_index - doc_start)
    cosine, sine_tab = jnp.tile(cosine, (1, 4)), jnp.tile(sine_tab, (1, 4))
    normed, queries, key_row, latent = local_call(
        project_kernel,
        "project",
        (
            hidden_in,
            (attention_all, (model_width, 1408), (0, 0)),
            gain_one,
            gain_latent,
            cosine,
            sine_tab,
        ),
        (
            ((tokens, model_width), low),
            ((tokens, 768), low),
            ((tokens, 640), low),
            ((tokens, RANK), full),
        ),
    )
    keys_all = reach_back(key_row, 2, "reach_back")
    key_count = keys_all.shape[0]
    key_segments = lax.dynamic_slice_in_dim(
        jnp.pad(segments, (key_count - tokens, 0), constant_values=-1), first_row, key_count
    )
    attn_part, attended, probs, expanded, key_rope = local_call(
        attend_kernel,
        "attend",
        (keys_all, expand_w, queries, own_segments[:, None], key_segments[None], *output_blocks),
        (
            ((tokens, model_width), low),
            ((tokens, HEADS * VH), low),
            ((HEADS, tokens, key_count), full),
            ((key_count, HEADS * (NOPE + VH)), low),
            ((key_count, 256), low),
        ),
    )
    attn_out = line_sum(attn_part, 3, "sum_heads")

    token_row, middle, gates = local_call(
        route_kernel,
        "route",
        (hidden_in, attn_out, gain_two, router_block, routes),
        (
            ((tokens, model_width + 128), low),
            ((tokens, model_width), full),
            ((tokens, 128), full),
        ),
    )
    token_rows = plane_gather(token_row, 4, "gather_tokens")
    token_row, token_rows = lax.optimization_barrier((token_row, token_rows))
    normed_two = (token_row, (tokens, model_width), (0, 0))

    shared_part, shared_back, ffn_grads = local_call(
        shared_kernel,
        "shared",
        (normed_two, cotangent, ffn_all),
        (
            ((tokens, model_width), full),
            ((tokens, model_width), full),
            (ffn_all.shape, low),
        ),
    )
    ffn_grads, token_rows = lax.optimization_barrier((ffn_grads, token_rows))
    own_ffn = lax.psum_scatter(ffn_grads, "expert", scatter_dimension=0, tiled=True)

    routed_part, back_part, out_egate, out_eup, out_edown = experts(
        token_rows.reshape(devices // 2, 2 * tokens, -1),
        grad_rows.reshape(devices // 2, 2 * tokens, -1),
        expert_gate.swapaxes(1, 2),
        routed_expert_up.swapaxes(1, 2),
        expert_down,
    )
    out_egate, out_eup = out_egate.swapaxes(1, 2), out_eup.swapaxes(1, 2)
    routed_own = lax.psum_scatter(
        routed_part.reshape(-1, model_width), "expert", scatter_dimension=0, tiled=True
    )
    layer_part = (routed_own.astype(full) + shared_part).astype(low)
    back_own = plane_sum((back_part.reshape(devices * tokens, -1),), 5, "sum_tokens")
    back_wide = back_own + jnp.pad(shared_back, ((0, 0), (0, 128)))
    back_all = line_sum(back_wide.astype(low), 6, "sum_units")

    (
        grad_middle,
        grad_attn,
        grad_gain_two,
        grad_logits,
        grad_query_pre,
        query_back,
        grad_keys,
        grad_expand,
    ) = local_call(
        attend_back_kernel,
        "attend_back",
        (
            back_all,
            middle,
            gain_two,
            gates,
            routes,
            router_block,
            cotangent,
            *output_blocks,
            probs,
            expanded,
            key_rope,
            queries,
            keys_all,
            expand_w,
            (attention_all, (model_width, 768), (0, 0)),
            cosine,
            sine_tab,
        ),
        (
            ((tokens, model_width), full),
            ((tokens, model_width), low),
            ((1, model_width), full),
            ((tokens, 128), low),
            ((tokens, 768), low),
            ((tokens, model_width), low),
            ((key_count, 640), low),
            ((devices, shard, 256), low),
        ),
        (((key_count, HEADS * (NOPE + VH)), low), ((key_count, 256), full)),
    )
    latent_part = send_back(grad_keys, 7, "send_back")
    summed = line_sum(jnp.concatenate([query_back, latent_part], 1), 8, "sum_inputs")
    grad_input, grad_gain_one, grad_gain_latent, many_grads = local_call(
        finish_kernel,
        "finish",
        (
            summed,
            latent,
            gain_latent,
            cosine,
            sine_tab,
            *latent_blocks,
            hidden_in,
            gain_one,
            grad_middle,
            normed,
            grad_attn,
            normed_two,
            grad_logits,
            grad_query_pre,
            attended,
        ),
        (
            ((tokens, model_width), low),
            ((1, model_width), full),
            ((1, RANK), full),
            ((model_width, 1920), low),
        ),
        (((tokens, 640), low),),
    )

    gain_grads = jnp.stack(
        [
            grad_gain_one.reshape(devices, shard),
            grad_gain_two.reshape(devices, shard),
            jnp.pad(
                grad_gain_latent.reshape(devices, -1), ((0, 0), (0, shard - latent_norm.shape[0]))
            ),
        ],
        1,
    ).astype(low)
    gain_grads = jnp.pad(gain_grads, ((0, 0), (0, shard - 3), (0, 128 - shard)))
    own, layer_sum = plane_sum(
        (many_grads, gain_grads.reshape(model_width, 128), grad_expand.reshape(model_width, 256)),
        9,
        "sum_attention",
        layer_part,
    )
    (
        layer_out,
        out_query,
        out_latent,
        out_router,
        out_output,
        out_gains,
        out_expand,
        out_sgate,
        out_sup,
        out_sdown,
    ) = local_call(
        unpack_kernel,
        "unpack",
        (own, own_ffn, middle, layer_sum),
        (
            ((tokens, model_width), low),
            (w_query.shape, full),
            (w_latent.shape, full),
            (w_router.shape, full),
            ((shard, w_output.shape[0]), full),
            ((8, 128), full),
            (w_expand.shape, full),
            (shared_gate.shape, full),
            (shared_up.shape, full),
            ((shard, shared_down.shape[0]), full),
        ),
    )
    return (
        layer_out,
        grad_input,
        out_gains[0, :shard],
        out_query,
        out_latent,
        out_gains[2, : latent_norm.shape[0]],
        out_expand,
        out_output.T,
        out_gains[1, :shard],
        out_router,
        out_sgate,
        out_sup,
        out_sdown.T,
        out_egate,
        out_eup,
        out_edown,
    )


def solution(mesh):
    in_specs = (
        P("expert", None),
        P("expert", None),
        P(),
        P("expert", None),
        P("expert"),
        P("expert", "tensor"),
        P("expert", None),
        P("expert"),
        P("expert", "tensor"),
        P("tensor", "expert"),
        P("expert"),
        P("expert", None),
        P("expert", "tensor"),
        P("expert", "tensor"),
        P("tensor", "expert"),
        P("expert", None, "tensor"),
        P("expert", None, "tensor"),
        P("expert", "tensor", None),
    )
    out_specs = (
        P("expert", None),
        P("expert", None),
        P("expert"),
        P("expert", "tensor"),
        P("expert", None),
        P("expert"),
        P("expert", "tensor"),
        P("tensor", "expert"),
        P("expert"),
        P("expert", None),
        P("expert", "tensor"),
        P("expert", "tensor"),
        P("tensor", "expert"),
        P("expert", None, "tensor"),
        P("expert", None, "tensor"),
        P("expert", "tensor", None),
    )
    return jax.shard_map(body, mesh=mesh, in_specs=in_specs, out_specs=out_specs, check_vma=False)
```

time: 1130 us -> 545 us (0.48)
  Pallas kernels: 0 us -> 481 us
  waiting for transfers between devices: 456 us -> 17.9 us
  local copies, waits for them, and re-layouts: 215 us -> 17.3 us
  matrix products: 160 us -> 0 us
  blocking collectives: 133 us -> 0 us
  starting transfers between devices: 68.4 us -> 0.16 us
  other arithmetic: 71.9 us -> 8.95 us
    pallas_call x0 -> x18, Pallas kernels: none -> 481 us  [the longest x2 115 us: plane_sum(): pl.pallas_call(functools.partial(plane_sum_kernel, count=count, columns=c...]
    all_gather x7 -> x2, waiting for transfers between devices: 174 us -> 0.02 us  [the longest x1 0.02 us: body(): ffn_all = lax.all_gather(ffn_shard, 'expert', axis=0, tiled=True)]
    dot_general x42 -> x0, matrix products: 160 us -> none  [the longest x8 29.5 us: product(): return jnp.dot(left_side, right_side, preferred_element_type=jnp.float32)]
    unnamed x18 -> x4, waiting for transfers between devices: 112 us -> 1.25 us
    reduce_scatter x7 -> x2, waiting for transfers between devices: 96.8 us -> 16.6 us  [the longest x1 16.6 us: body(): lax.psum_scatter(ffn_grads, 'expert', scatter_dimension=0, tiled=True)]
    unnamed x1 -> x0, blocking collectives: 63.7 us -> none
    concatenate x5 -> x0, local copies, waits for them, and re-layouts: 62.6 us -> none  [the longest x2 60.8 us: in_one_piece_2(): both = jnp.concatenate(columns, axis=along)]
    all_to_all x2 -> x0, blocking collectives: 53.8 us -> none  [part_move(): lax.all_to_all(rows, 'expert', split_axis=0, concat_axis=0, tiled=True)]
  transfers between devices with their start and end apart: 38 -> 4, of which waited for: 20 -> 1; matrix products, arithmetic and copies ran while one was open for 35% -> 4% of each run, Pallas kernels for 0% -> 75%
where the time goes in v1:
time: 545 us; the launch traced here: 540 us
  Pallas kernels  481 us (88%)
  waiting for transfers between devices  17.9 us (3%)
  local copies, waits for them, and re-layouts  17.3 us (3%)
  between operations  14.2 us (3%)
  other arithmetic  8.95 us (2%)
    pallas_call x2, Pallas kernels, plane_sum(): pl.pallas_call(functools.partial(plane_sum_kernel, count=count, columns=c...  115 us
    pallas_call x2, Pallas kernels, plane_gather(): pl.pallas_call(plane_gather_kernel, out_shape=jax.ShapeDtypeStruct((32, *...  100 us
    pallas_call x8, Pallas kernels, local_call(): pl.pallas_call(kernel, grid=(1,), out_shape=shapes, in_specs=specs, out_s...  72.4 us
    pallas_call x1, Pallas kernels, experts(): pl.pallas_call(experts_kernel, grid=(2 * blocks + 2,), out_shape=(jax.Sha...  69.9 us
    pallas_call x3, Pallas kernels, line_sum(): pl.pallas_call(line_sum_kernel, out_shape=jax.ShapeDtypeStruct((groups, 8...  63.5 us
    pallas_call x1, Pallas kernels, reach_back(): pl.pallas_call(reach_back_kernel, out_shape=jax.ShapeDtypeStruct((9, grou...  33.7 us
    pallas_call x1, Pallas kernels, send_back(): pl.pallas_call(send_back_kernel, out_shape=jax.ShapeDtypeStruct((groups,...  26.7 us
    reduce_scatter x1, waiting for transfers between devices, body(): lax.psum_scatter(ffn_grads, 'expert', scatter_dimension=0, tiled=True)  16.6 us
  transfers between devices with their start and end apart: 4, of which 1 were waited for; matrix products, arithmetic and copies ran while one was open for 4% of the time, Pallas kernels for 75%

profile of v1, /device:TPU:0, one launch (start us, length us, event | category | flops | bytes accessed | tf_op | source)
XLA Modules:
  0.0 539.6 jit_solution(17845428038822608883)
XLA Ops:
  7.2 0.0 all-gather.4.cloned.1.call-start
  7.2 1.2 pad_bitcast_fusion.2.gain_latent
  8.4 2.3 pack.1
  10.7 0.0 all-gather.4.cloned.1.call-update
  10.7 0.0 all-gather.6.cloned.1.call-start
  10.8 0.7 all-gather.6.cloned.1.call-update
  11.5 0.0 reduce-scatter.3.cloned.1.call-start
  11.5 0.8 dynamic_slice.6
  12.3 0.8 pad_dynamic-slice_fusion
  13.1 0.6 broadcast_in_dim.23.key_segment
  13.7 1.1 convert_reduce_fusion
  14.8 0.1 multiply_sine_fusion
  14.9 0.7 copy.55.sine_tab
  15.7 0.8 dynamic-slice_bitcast_fusion
  16.4 0.7 copy.57.own_segment
  17.2 1.4 copy.58.routes
  18.6 0.7 copy.54.cosine
  19.3 42.8 %gather_attention.1 = bf16[32,8,8,2176]{3,2,1,0:T(8,128)(2,1)} custom-call(bf16[8,8,2176]{2,1,0:T(8,128)(2,1)} %bitcast.106), custom_call_target="tpu_custom_call" | custom-call | bytes 17825792 | tf_op jit(solution)/shard_map/gather_attention/pallas_call | solution.py:164
  62.1 0.9 slice.32
  63.1 0.7 reshape_squeeze.10.gain_latent
  63.7 0.7 reshape_squeeze.11.gain
  64.4 0.7 reshape_squeeze.9.gain
  65.1 1.3 slice.35
  66.4 0.5 copy.56
  66.9 1.2 copy.67
  68.1 4.9 project.1
  73.0 33.7 %reach_back.1 = bf16[9,16,8,640]{3,2,1,0:T(8,128)(2,1)} custom-call(bf16[16,8,640]{2,1,0:T(8,128)(2,1)} %bitcast.110), custom_call_target="tpu_custom_call" | custom-call | bytes 16384000 | tf_op jit(solution)/shard_map/reach_back/pallas_call | solution.py:569
  106.7 10.8 %attend.1 = (bf16[128,2048]{1,0:T(8,128)(2,1)}, bf16[128,512]{1,0:T(8,128)(2,1)}, f32[4,128,1152]{2,1,0:T(8,128)}, bf16[1152,1024]{1,0:T(8,128)(2,1)}, bf16[1152,256]{1,0:T(8,128)(2,1)}) custom-call(bf16[1152,640]{1,0:T(8,128)(2,1)} %bitcast.89, bf16[512,1024]{1,0:T(8,128)(2,1)} %bitcast.91, bf16[128,768]{1,0:T(8,128)(2,1)} %get-tuple-element.68.query, ...), custom_call_target="tpu_custom_call" | custom-call | tf_op jit(solution)/shard_map/attend/pallas_call | solution.py:1393
  117.5 21.0 %sum_heads.1 = bf16[16,8,2048]{2,1,0:T(8,128)(2,1)} custom-call(bf16[16,8,2048]{2,1,0:T(8,128)(2,1)} %bitcast.105), custom_call_target="tpu_custom_call" | custom-call | bytes 10485760 | tf_op jit(solution)/shard_map/sum_heads/pallas_call | solution.py:497
  138.5 0.0 all-gather.4.cloned.1.call-done.router.weights
  138.5 3.1 route.1
  141.7 57.2 %gather_tokens.1 = bf16[32,16,8,2176]{3,2,1,0:T(8,128)(2,1)} custom-call(bf16[16,8,2176]{2,1,0:T(8,128)(2,1)} %bitcast.94), custom_call_target="tpu_custom_call" | custom-call | bytes 35651584 | tf_op jit(solution)/shard_map/gather_tokens/pallas_call | solution.py:164
  198.9 16.5 %shared.1 = (f32[128,2048]{1,0:T(8,128)}, f32[128,2048]{1,0:T(8,128)}, bf16[2048,2304]{1,0:T(8,128)(2,1)}) custom-call(bf16[128,2176]{1,0:T(8,128)(2,1)} %get-tuple-element.72.normed.normed_two, bf16[128,2048]{1,0:T(8,128)(2,1)} %cotangent.3, bf16[2048,2304]{1,0:T(8,128)(2,1)} %all-gather.4.cloned.1.call-done.router.weights), custom_call_target="tpu_custom_call" | custom-call | tf_op jit(solution)/shard_map/shared/pallas_call | solution.py:1393
  215.4 0.0 all-gather.6.cloned.1.call-done
  215.4 69.9 %experts.1 = (bf16[16,256,2048]{2,1,0:T(8,128)(2,1)}, bf16[16,256,2176]{2,1,0:T(8,128)(2,1)}, f32[2,352,2048]{2,1,0:T(8,128)}, f32[2,352,2048]{2,1,0:T(8,128)}, f32[2,352,2048]{2,1,0:T(8,128)}) custom-call(bf16[16,256,2176]{2,1,0:T(8,128)(2,1)} %bitcast.87, bf16[16,256,2048]{2,1,0:T(8,128)(2,1)} %bitcast.114, f32[2,352,2048]{2,1,0:T(8,128)} %bitcast.115, ...), custom_call_target="tpu_custom_call" | custom-call | flops 21743271936 | bytes 104857600 | tf_op jit(solution)/shard_map/experts/pallas_call | solution.py:902
  285.3 0.0 reduce-scatter.3.cloned.1.call-update
  285.4 0.0 reduce-scatter.5.cloned.1.call-start
  285.4 0.5 reduce-scatter.5.cloned.1.call-update
  285.9 0.0 copy-start.1
  286.0 57.7 %sum_tokens.1 = f32[16,8,2176]{2,1,0:T(8,128)} custom-call(bf16[32,16,8,2176]{3,2,1,0:T(8,128)(2,1)} %bitcast.86), custom_call_target="tpu_custom_call" | custom-call | bytes 142606336 | tf_op jit(solution)/shard_map/sum_tokens/pallas_call | solution.py:459
  343.7 0.0 copy-done.1
  343.7 2.2 fusion.1.src
  345.9 18.8 %sum_units.1 = bf16[16,8,2176]{2,1,0:T(8,128)(2,1)} custom-call(bf16[16,8,2176]{2,1,0:T(8,128)(2,1)} %fusion.1.src), custom_call_target="tpu_custom_call" | custom-call | bytes 11141120 | tf_op jit(solution)/shard_map/sum_units/pallas_call | solution.py:497
  364.6 19.7 %attend_back.1 = (f32[128,2048]{1,0:T(8,128)}, bf16[128,2048]{1,0:T(8,128)(2,1)}, f32[1,2048]{1,0:T(1,128)}, bf16[128,128]{1,0:T(8,128)(2,1)}, bf16[128,768]{1,0...) custom-call(bf16[128,2176]{1,0:T(8,128)(2,1)} %bitcast.98, ...), custom_call_target="tpu_custom_call" | custom-call | tf_op jit(solution)/shard_map/attend_back/pallas_call | solution.py:1393
  384.3 26.7 %send_back.1 = bf16[16,8,640]{2,1,0:T(8,128)(2,1)} custom-call(bf16[9,16,8,640]{3,2,1,0:T(8,128)(2,1)} %bitcast.100), custom_call_target="tpu_custom_call" | custom-call | bytes 14745600 | tf_op jit(solution)/shard_map/send_back/pallas_call | solution.py:658
  411.1 2.0 pad_maximum_fusion.src
  413.1 23.8 %sum_inputs.1 = bf16[16,8,2688]{2,1,0:T(8,128)(2,1)} custom-call(bf16[16,8,2688]{2,1,0:T(8,128)(2,1)} %pad_maximum_fusion.src), custom_call_target="tpu_custom_call" | custom-call | bytes 13762560 | tf_op jit(solution)/shard_map/sum_inputs/pallas_call | solution.py:497
  436.9 0.0 copy-start.2
  436.9 0.0 copy-start
  436.9 12.2 %finish.1 = (bf16[128,2048]{1,0:T(8,128)(2,1)}, f32[1,2048]{1,0:T(1,128)}, f32[1,512]{1,0:T(1,128)}, bf16[2048,1920]{1,0:T(8,128)(2,1)}) custom-call(bf16[128,2688]{1,0:T(8,128)(2,1)} %bitcast.97, f32[128,512]{1,0:T(8,128)} %get-tuple-element.85.latent, f32[1,512]{1,0:T(1,128)} %reshape_squeeze.10.gain_latent, f32[128,128]{1,0:T(8,128)} %copy.54.cosine, ...), custom_call_target="tpu_custom_call" | custom-call | tf_op jit(solution)/shard_map/finish/pallas_call | solution.py:1393
  449.1 0.7 convert_reduce_fusion.2
  449.9 0.1 stack_reshape.8
  449.9 0.0 copy-done.2
  450.0 0.1 stack_reshape.9
  450.1 0.7 convert_reduce_fusion.3
  450.8 0.1 reshape.200
  450.9 0.9 pad_bitcast_fusion.refs_1_
  451.8 0.0 copy-done
  451.8 2.0 fusion.2.refs_3_
  453.8 57.0 %sum_attention.1 = (f32[8,8,2304]{2,1,0:T(8,128)}, bf16[16,8,2048]{2,1,0:T(8,128)(2,1)}) custom-call(bf16[32,8,8,1920]{3,2,1,0:T(8,128)(2,1)} %bitcast.93, bf16[32,8,8,128]{3,2,1,0:T(8,128)(2,1)} %pad_bitcast_fusion.refs_1_, bf16[32,8,8,256]{3,2,1,0:T(8,128)(2,1)} %bitcast.101, bf16[16,8,2048]{2,1,0:T(8,128)(2,1)} %fusion.2.refs_3_), custom_call_target="tpu_custom_call" | custom-call | bytes 75497472 | tf_op jit(solution)/shard_map/sum_attention/pallas_call | solution.py:459
  510.8 16.6 %reduce-scatter.5.cloned.1.call-done.ffn = bf16[64,2304]{1,0:T(8,128)(2,1)} async-done(((bf16[2048,2304]{1,0:T(8,128)(2,1)}), bf16[64,2304]{1,0:T(8,128)(2,1)}) %reduce-scatter.5.cloned.1.call-update) | async-done | bytes 294928 | tf_op jit(solution)/shard_map/reduce_scatter | solution.py:1539
  527.5 2.9 unpack.1
  530.3 1.2 slice_bitcast_fusion.1
  531.5 1.3 slice_bitcast_fusion
  (12 shorter events, 0.1 us)
Async XLA Ops:
  7.2 131.4 %all-gather.4.cloned.1.call-start = ((), (), s32[]{:S(2)}) async-start(), calls=%async_computation.2 | async-start | bytes 9732096 | tf_op jit(solution)/shard_map/all_gather | solution.py:1457
  10.7 204.6 %all-gather.6.cloned.1.call-start = ((), (), s32[]{:S(2)}) async-start(), calls=%async_computation.5 | async-start | bytes 17301504 | tf_op jit(solution)/shard_map/all_gather | solution.py:1458
  11.5 440.3 %reduce-scatter.3.cloned.1.call-start = ((), (), s32[]{:S(2)}) async-start(), calls=%async_computation.3 | async-start | bytes 17301504 | tf_op jit(solution)/shard_map/reduce_scatter | solution.py:1549
  285.4 242.1 %reduce-scatter.5.cloned.1.call-start = ((), (), s32[]{:S(2)}) async-start(), calls=%async_computation.4 | async-start | bytes 9732096 | tf_op jit(solution)/shard_map/reduce_scatter | solution.py:1539
  285.9 57.7 %copy-start.1 = (f32[128,2048]{1,0:T(8,128)S(1)}, f32[128,2048]{1,0:T(8,128)}, u32[]{:S(2)}) copy-start(f32[128,2048]{1,0:T(8,128)} %get-tuple-element.77) | copy-start | bytes 3145732
  436.9 13.1 %copy-start.2 = (f32[1,2048]{1,0:T(1,128)S(1)}, f32[1,2048]{1,0:T(1,128)}, u32[]{:S(2)}) copy-start(f32[1,2048]{1,0:T(1,128)} %get-tuple-element.94) | copy-start | bytes 24580
  436.9 14.9 %copy-start = (f32[128,2048]{1,0:T(8,128)S(1)}, f32[128,2048]{1,0:T(8,128)}, u32[]{:S(2)}) copy-start(f32[128,2048]{1,0:T(8,128)} %get-tuple-element.98) | copy-start | bytes 3145732
Sparse Core Ops, SparseCore 0:
  10.9 63.9 all-gather.3
  77.1 80.1 all-gather.5
  285.5 125.1 reduce-scatter.2
  414.3 113.1 reduce-scatter.4

commit v2 on v1

--- a/solution.py
+++ b/solution.py
@@ -37,10 +37,18 @@
 
 
 def greet(peers):
+    call(peers)
+    hear(peers)
+
+
+def call(peers):
     barrier = pltpu.get_barrier_semaphore()
     for peer in peers:
         pl.semaphore_signal(barrier, inc=1, device_id=peer, device_id_type=MESH)
-    pl.semaphore_wait(barrier, len(peers))
+
+
+def hear(peers):
+    pl.semaphore_wait(pltpu.get_barrier_semaphore(), len(peers))
 
 
 def plane_gather_kernel(src, out, ssem, rsem, dssem, drsem, lsem):
@@ -184,12 +192,17 @@
     return gathered.reshape(32 * rows.shape[0], rows.shape[1])
 
 
+def line_peers():
+    e, t = lax.axis_index("expert"), lax.axis_index("tensor")
+    return [(e, lax.rem(t + k, 4)) for k in (1, 2, 3)]
+
+
 class Line:
     def __init__(self, src, out, taken, ssem, rsem):
-        e, t = lax.axis_index("expert"), lax.axis_index("tensor")
+        t = lax.axis_index("tensor")
         self.src, self.out, self.taken, self.ssem, self.rsem = src, out, taken, ssem, rsem
         self.share, self.t = src.shape[0] // 4, t
-        self.others = [(e, lax.rem(t + k, 4)) for k in (1, 2, 3)]
+        self.others = line_peers()
 
     def share_out(self, k):
         device = self.others[k - 1]
@@ -251,60 +264,42 @@
     line.finish()
 
 
-def plane_sum_kernel(*refs, count, columns, beside):
-    sources, refs = refs[:count], refs[count:]
-    if beside:
-        side_in, out, side_out, side_taken, side_ssem, side_rsem, *refs = refs
-    else:
-        out, *refs = refs
-    mine, peer, one, two, last_one, last_two, lsem, pssem, prsem, ssem, rsem = refs
+PLANE_STEPS = 1 + 8 + 16 + 2 + 4 + 2
+
+
+def plane_sum_steps(source, emit, scratch):
+    mine, peer, one, two, last_one, last_two, lsem, pssem, prsem, ssem, rsem = scratch
     t, x, z, c = place()
-    groups = out.shape[0]
+    groups = mine.shape[2]
     half, quarter = groups // 2, groups // 4
     sibling = (at(x, z, 1 - c), t)
     along_x = [(at(wrap(x - 1), z, c), t), (at(wrap(x + 1), z, c), t)]
     along_z = [(at(x, wrap(z - 1), c), t), (at(x, wrap(z + 1), c), t)]
-    if beside:
-        line = Line(side_in, side_out, side_taken, side_ssem, side_rsem)
-        greet([sibling] + along_x + along_z + line.others)
-    else:
-        greet([sibling] + along_x + along_z)
     order = (2, 1, 3, 0)
     sent = []
 
-    def target(h, a, b, core):
+    def view(ref, h, a, b):
         if h == 0:
-            return at(wrap(x + a), wrap(z + b), core)
-        return at(wrap(x + b), wrap(z + a), core)
-
-    def outward(h, a, b):
-        copies, start = [], 0
-        for i, width in enumerate(columns):
-            copies.append(
-                pltpu.make_async_remote_copy(
-                    src_ref=sources[i].at[target(h, a, b, 1 - c), pl.ds(h * half, half)],
-                    dst_ref=peer.at[h, a, b, :, :, pl.ds(start, width)],
-                    send_sem=pssem.at[i, h, a, b],
-                    recv_sem=prsem.at[i, h, a, b],
-                    device_id=sibling,
-                    device_id_type=MESH,
-                )
-            )
-            start += width
-        return copies
-
-    def inward(h, a, b):
-        copies, start = [], 0
-        for i, width in enumerate(columns):
-            copies.append(
-                pltpu.make_async_copy(
-                    sources[i].at[target(h, a, b, c), pl.ds(h * half, half)],
-                    mine.at[h, a, b, :, :, pl.ds(start, width)],
-                    lsem.at[i, h, a, b],
-                )
-            )
-            start += width
-        return copies
+            return ref.at[a, b, pl.ds(0, half)]
+        return ref.at[b, a, pl.ds(half, half)]
+
+    def target(dx, dz, core):
+        return at(wrap(x + dx), wrap(z + dz), core)
+
+    def outward(dx, dz):
+        return pltpu.make_async_remote_copy(
+            src_ref=source.at[target(dx, dz, 1 - c)],
+            dst_ref=peer.at[dx, dz],
+            send_sem=pssem.at[dx, dz],
+            recv_sem=prsem.at[dx, dz],
+            device_id=sibling,
+            device_id_type=MESH,
+        )
+
+    def inward(dx, dz):
+        return pltpu.make_async_copy(
+            source.at[target(dx, dz, c)], mine.at[dx, dz], lsem.at[dx, dz]
+        )
 
     def hop(h, slot, src, dst, device):
         return pltpu.make_async_remote_copy(
@@ -323,28 +318,28 @@
         return hop(
             h,
             4 * b + side,
-            mine.at[h, 2, b, pl.ds(side * quarter, quarter)],
+            view(mine, h, 2, b).at[pl.ds(side * quarter, quarter)],
             one.at[h, b, side],
             ring(h, 1)[1 - side],
         )
 
     def second(h, b, side):
         return hop(
-            h, 4 * b + 2 + side, mine.at[h, 1 + 2 * side, b], two.at[h, b, side], ring(h, 1)[1 - side]
+            h, 4 * b + 2 + side, view(mine, h, 1 + 2 * side, b), two.at[h, b, side], ring(h, 1)[1 - side]
         )
 
     def third(h, side):
         return hop(
             h,
             16 + side,
-            mine.at[h, 0, 2, pl.ds(side * quarter, quarter)],
+            view(mine, h, 0, 2).at[pl.ds(side * quarter, quarter)],
             last_one.at[h, side],
             ring(h, 2)[1 - side],
         )
 
     def fourth(h, side):
         return hop(
-            h, 18 + side, mine.at[h, 0, 1 + 2 * side], last_two.at[h, side], ring(h, 2)[1 - side]
+            h, 18 + side, view(mine, h, 0, 1 + 2 * side), last_two.at[h, side], ring(h, 2)[1 - side]
         )
 
     def go(copy):
@@ -361,28 +356,30 @@
 
         lax.fori_loop(0, number, step, 0)
 
-    spots = [(h, a, b) for a in order for b in order for h in (0, 1)]
+    spots = [(2, 2), (2, 1), (1, 2), (2, 3), (3, 2), (2, 0), (0, 2), (1, 1)]
+    spots += [(1, 3), (3, 1), (3, 3), (1, 0), (0, 1), (3, 0), (0, 3), (0, 0)]
     for spot in spots:
-        for copy in inward(*spot):
-            copy.start()
-        for copy in outward(*spot):
-            go(copy)
-
-    if beside:
-        line.scatter()
+        inward(*spot).start()
+        go(outward(*spot))
+    merged = set()
+
+    yield
 
     def merge(h, a, b):
-        for copy in inward(h, a, b):
-            copy.wait()
-        for copy in outward(h, a, b):
-            copy.wait_recv()
-        accumulate(mine.at[h, a, b], [peer.at[h, a, b]], half)
+        spot = (a, b) if h == 0 else (b, a)
+        if spot in merged:
+            return
+        merged.add(spot)
+        inward(*spot).wait()
+        outward(*spot).wait_recv()
+        accumulate(mine.at[spot[0], spot[1]], [peer.at[spot[0], spot[1]]], groups)
 
     for b in order:
         for h in (0, 1):
             merge(h, 2, b)
             for side in (0, 1):
                 go(first(h, b, side))
+            yield
     for side in (0, 1):
         for b in order:
             for h in (0, 1):
@@ -390,153 +387,197 @@
                 merge(h, a, b)
                 first(h, b, side).wait_recv()
                 accumulate(
-                    mine.at[h, a, b, pl.ds(side * quarter, quarter)], [one.at[h, b, side]], quarter
+                    view(mine, h, a, b).at[pl.ds(side * quarter, quarter)],
+                    [one.at[h, b, side]],
+                    quarter,
                 )
                 go(second(h, b, side))
-
-    if beside:
-        line.add()
-        line.gather()
+                yield
 
     def gathered_here(h, b):
         merge(h, 0, b)
         for side in (0, 1):
             second(h, b, side).wait_recv()
-        accumulate(mine.at[h, 0, b], [two.at[h, b, 0], two.at[h, b, 1]], half)
+        accumulate(view(mine, h, 0, b), [two.at[h, b, 0], two.at[h, b, 1]], half)
 
     for h in (0, 1):
         gathered_here(h, 2)
         for side in (0, 1):
             go(third(h, side))
+        yield
     for side in (0, 1):
         b = 1 + 2 * side
         for h in (0, 1):
             gathered_here(h, b)
             third(h, side).wait_recv()
             accumulate(
-                mine.at[h, 0, b, pl.ds(side * quarter, quarter)], [last_one.at[h, side]], quarter
+                view(mine, h, 0, b).at[pl.ds(side * quarter, quarter)],
+                [last_one.at[h, side]],
+                quarter,
             )
             go(fourth(h, side))
+            yield
     for h in (0, 1):
         gathered_here(h, 0)
         for side in (0, 1):
             fourth(h, side).wait_recv()
 
         def finish(i, carry, h=h):
-            total = mine[h, 0, 0, i].astype(jnp.float32)
+            total = mine[0, 0, h * half + i].astype(jnp.float32)
             for side in (0, 1):
                 total = total + last_two[h, side, i].astype(jnp.float32)
-            out[h * half + i] = total
+            emit(h * half + i, total)
             return carry
 
         lax.fori_loop(0, half, finish, 0)
+        yield
     for copy in sent:
         copy.wait_send()
-    if beside:
-        line.finish()
-
-
-def plane_sum(parts, collective_id, name, beside=None):
-    columns = tuple(part.shape[1] for part in parts)
-    width = sum(columns)
-    groups = parts[0].shape[0] // 256
+
+
+def plane_peers():
+    t, x, z, c = place()
+    return [
+        (at(x, z, 1 - c), t),
+        (at(wrap(x - 1), z, c), t),
+        (at(wrap(x + 1), z, c), t),
+        (at(x, wrap(z - 1), c), t),
+        (at(x, wrap(z + 1), c), t),
+    ]
+
+
+def plane_scratch(groups, width):
     half, quarter = groups // 2, groups // 4
     low = jnp.bfloat16
-    count = len(parts)
+    return [
+        pltpu.VMEM((4, 4, groups, 8, width), low),
+        pltpu.VMEM((4, 4, groups, 8, width), low),
+        pltpu.VMEM((2, 4, 2, quarter, 8, width), low),
+        pltpu.VMEM((2, 4, 2, half, 8, width), low),
+        pltpu.VMEM((2, 2, quarter, 8, width), low),
+        pltpu.VMEM((2, 2, half, 8, width), low),
+        pltpu.SemaphoreType.DMA((4, 4)),
+        pltpu.SemaphoreType.DMA((4, 4)),
+        pltpu.SemaphoreType.DMA((4, 4)),
+        pltpu.SemaphoreType.DMA((2, 20)),
+        pltpu.SemaphoreType.DMA((2, 20)),
+    ]
+
+
+def line_scratch(groups, width):
+    return [
+        pltpu.VMEM((3, groups // 4, 8, width), jnp.bfloat16),
+        pltpu.SemaphoreType.DMA((2, 3)),
+        pltpu.SemaphoreType.DMA((2, 3)),
+    ]
+
+
+def advance(task, number):
+    for _ in range(number):
+        next(task, None)
+
+
+def by_expert(part, groups):
+    return part.reshape(32, groups, 8, part.shape[1])
+
+
+def by_group(part):
+    return part.reshape(part.shape[0] // 8, 8, part.shape[1])
+
+
+def communicate(kernel, collective_id, name, operands, where, out_shapes, scratch, moved):
     vmem = pl.BlockSpec(memory_space=pltpu.VMEM)
-    operands = [part.reshape(32, groups, 8, part.shape[1]) for part in parts]
-    out_shape = [jax.ShapeDtypeStruct((groups, 8, width), jnp.float32)]
-    side = []
-    if beside is not None:
-        lines, side_width = beside.shape
-        operands.append(beside.reshape(lines // 8, 8, side_width))
-        out_shape.append(jax.ShapeDtypeStruct((lines // 8, 8, side_width), beside.dtype))
-        side = [
-            pltpu.VMEM((3, lines // 32, 8, side_width), beside.dtype),
-            pltpu.SemaphoreType.DMA((2, 3)),
-            pltpu.SemaphoreType.DMA((2, 3)),
-        ]
-    results = pl.pallas_call(
-        functools.partial(
-            plane_sum_kernel, count=count, columns=columns, beside=beside is not None
-        ),
-        out_shape=out_shape,
-        in_specs=[HBM] * count + [vmem] * (len(operands) - count),
-        out_specs=[vmem] * len(out_shape),
-        scratch_shapes=side
-        + [
-            pltpu.VMEM((2, 4, 4, half, 8, width), low),
-            pltpu.VMEM((2, 4, 4, half, 8, width), low),
-            pltpu.VMEM((2, 4, 2, quarter, 8, width), low),
-            pltpu.VMEM((2, 4, 2, half, 8, width), low),
-            pltpu.VMEM((2, 2, quarter, 8, width), low),
-            pltpu.VMEM((2, 2, half, 8, width), low),
-            pltpu.SemaphoreType.DMA((count, 2, 4, 4)),
-            pltpu.SemaphoreType.DMA((count, 2, 4, 4)),
-            pltpu.SemaphoreType.DMA((count, 2, 4, 4)),
-            pltpu.SemaphoreType.DMA((2, 20)),
-            pltpu.SemaphoreType.DMA((2, 20)),
-        ],
+    shapes = [jax.ShapeDtypeStruct(shape, dtype) for shape, dtype in out_shapes]
+    return pl.pallas_call(
+        kernel,
+        out_shape=shapes,
+        in_specs=[vmem if inside else HBM for inside in where],
+        out_specs=[vmem] * len(shapes),
+        scratch_shapes=scratch,
         compiler_params=pltpu.CompilerParams(
             collective_id=collective_id, has_side_effects=True, vmem_limit_bytes=60 * 2**20
         ),
-        cost_estimate=pl.CostEstimate(
-            flops=0, bytes_accessed=256 * groups * width * 16, transcendentals=0
-        ),
+        cost_estimate=pl.CostEstimate(flops=0, bytes_accessed=moved, transcendentals=0),
         name=name,
     )(*operands)
-    summed = results[0].reshape(groups * 8, width)
-    if beside is None:
-        return summed
-    return summed, results[1].reshape(beside.shape)
-
-
-def line_sum(rows, collective_id, name):
-    groups, width = rows.shape[0] // 8, rows.shape[1]
-    vmem = pl.BlockSpec(memory_space=pltpu.VMEM)
-    summed = pl.pallas_call(
-        line_sum_kernel,
-        out_shape=jax.ShapeDtypeStruct((groups, 8, width), rows.dtype),
-        in_specs=[vmem],
-        out_specs=vmem,
-        scratch_shapes=[
-            pltpu.VMEM((3, groups // 4, 8, width), rows.dtype),
-            pltpu.SemaphoreType.DMA((2, 3)),
-            pltpu.SemaphoreType.DMA((2, 3)),
-        ],
-        compiler_params=pltpu.CompilerParams(
-            collective_id=collective_id, has_side_effects=True, vmem_limit_bytes=60 * 2**20
-        ),
-        cost_estimate=pl.CostEstimate(flops=0, bytes_accessed=40 * rows.size, transcendentals=0),
-        name=name,
-    )(rows.reshape(groups, 8, width))
-    return summed.reshape(rows.shape)
-
-
-def chip_at(x, z, c, distance):
-    place_on = lax.rem(x * 4 + z + 16 + distance, 16)
-    return place_on * 2 + c
-
-
-def reach_back_kernel(src, out, lsem, ssem, rsem, pssem, prsem):
+
+
+def sum_tokens_kernel(source, shared, out, held, taken, line_ssem, line_rsem, *scratch):
+    half = out.shape[0] // 2
+
+    def emit(i, total):
+        held[i] = (total + shared[i]).astype(held.dtype)
+
+    greet(plane_peers() + line_peers())
+    plane = plane_sum_steps(source, emit, scratch)
+    lines = []
+    for h in (0, 1):
+        rows = pl.ds(h * half, half)
+        lines.append(
+            Line(held.at[rows], out.at[rows], taken.at[h], line_ssem.at[h], line_rsem.at[h])
+        )
+    advance(plane, PLANE_STEPS - 1)
+    lines[0].scatter()
+    advance(plane, 1)
+    lines[1].scatter()
+    for line in lines:
+        line.add()
+        line.gather()
+    for line in lines:
+        line.finish()
+    advance(plane, 1)
+
+
+def sum_tokens(part, shared, collective_id):
+    groups, width = part.shape[0] // 256, part.shape[1]
+    (summed,) = communicate(
+        sum_tokens_kernel,
+        collective_id,
+        "sum_tokens",
+        (by_expert(part, groups), by_group(shared)),
+        (False, True),
+        (((groups, 8, width), jnp.bfloat16),),
+        [
+            pltpu.VMEM((groups, 8, width), jnp.bfloat16),
+            pltpu.VMEM((2, 3, groups // 8, 8, width), jnp.bfloat16),
+            pltpu.SemaphoreType.DMA((2, 2, 3)),
+            pltpu.SemaphoreType.DMA((2, 2, 3)),
+        ]
+        + plane_scratch(groups, width),
+        16 * part.size,
+    )
+    return summed.reshape(8 * groups, width)
+
+
+def reach_back_peers():
+    t, x, z, c = place()
+    along = [(at(x, wrap(z - r), c), t) for r in (1, 2, 3)]
+    return [(at(x, z, 1 - c), t), (at(wrap(x - 1), z, c), t)] + along
+
+
+def reach_back_run(src, out, lsem, ssem, rsem, pssem, prsem):
     t, x, z, c = place()
     sibling = (at(x, z, 1 - c), t)
-    ahead = [(chip_at(x, z, c, k), t) for k in (1, 2, 3, 4)]
-    behind = [(chip_at(x, z, c, -k), t) for k in (1, 2, 3, 4)]
-    barrier = pltpu.get_barrier_semaphore()
-    for peer in [sibling] + behind:
-        pl.semaphore_signal(barrier, inc=1, device_id=peer, device_id_type=MESH)
-    pl.semaphore_wait(barrier, 5)
     own = pltpu.make_async_copy(src, out.at[8], lsem)
     own.start()
 
-    def far(k):
+    def onward():
         return pltpu.make_async_remote_copy(
             src_ref=src,
-            dst_ref=out.at[8 - 2 * k],
-            send_sem=ssem.at[k - 1],
-            recv_sem=rsem.at[k - 1],
-            device_id=ahead[k - 1],
+            dst_ref=out.at[0],
+            send_sem=ssem.at[3],
+            recv_sem=rsem.at[3],
+            device_id=(at(wrap(x + 1), z, c), t),
+            device_id_type=MESH,
+        )
+
+    def along(r, source):
+        return pltpu.make_async_remote_copy(
+            src_ref=source,
+            dst_ref=out.at[8 - 2 * r],
+            send_sem=ssem.at[r - 1],
+            recv_sem=rsem.at[r - 1],
+            device_id=(at(x, wrap(z + r), c), t),
             device_id_type=MESH,
         )
 
@@ -550,53 +591,42 @@
             device_id_type=MESH,
         )
 
-    for k in (4, 3, 2, 1):
-        far(k).start()
+    onward().start()
+    for r in (2, 1, 3):
+
+        @pl.when(z + r < 4)
+        def _(r=r):
+            along(r, src).start()
+
     own.wait()
-    for k in (1, 2, 3, 4):
-        far(k).wait_recv()
+    onward().wait_recv()
+    for r in (2, 3, 1):
+
+        @pl.when(z + r >= 4)
+        def _(r=r):
+            along(r, out.at[0]).start()
+
+    for r in (1, 3, 2):
+        along(r, src).wait_recv()
     for i in range(4):
         near(i).start()
     for i in range(4):
         near(i).wait()
-    for k in (1, 2, 3, 4):
-        far(k).wait_send()
-
-
-def reach_back(rows, collective_id, name):
-    groups, width = rows.shape[0] // 8, rows.shape[1]
-    vmem = pl.BlockSpec(memory_space=pltpu.VMEM)
-    keys = pl.pallas_call(
-        reach_back_kernel,
-        out_shape=jax.ShapeDtypeStruct((9, groups, 8, width), rows.dtype),
-        in_specs=[vmem],
-        out_specs=vmem,
-        scratch_shapes=[
-            pltpu.SemaphoreType.DMA,
-            pltpu.SemaphoreType.DMA((4,)),
-            pltpu.SemaphoreType.DMA((4,)),
-            pltpu.SemaphoreType.DMA((4,)),
-            pltpu.SemaphoreType.DMA((4,)),
-        ],
-        compiler_params=pltpu.CompilerParams(
-            collective_id=collective_id, has_side_effects=True, vmem_limit_bytes=60 * 2**20
-        ),
-        cost_estimate=pl.CostEstimate(flops=0, bytes_accessed=200 * rows.size, transcendentals=0),
-        name=name,
-    )(rows.reshape(groups, 8, width))
-    return keys.reshape(9 * rows.shape[0], width)
-
-
-def send_back_kernel(src, out, held, near_in, far_in, lsem, ssem, rsem, pssem, prsem):
+    onward().wait_send()
+    for r in (1, 2, 3):
+        along(r, src).wait_send()
+
+
+def chip_at(x, z, c, distance):
+    place_on = lax.rem(x * 4 + z + 16 + distance, 16)
+    return place_on * 2 + c
+
+
+def send_back_steps(src, out, held, near_in, far_in, ssem, rsem, pssem, prsem):
     t, x, z, c = place()
     groups = out.shape[0]
     sibling = (at(x, z, 1 - c), t)
-    ahead = [(chip_at(x, z, c, k), t) for k in (1, 2, 3, 4)]
     behind = [(chip_at(x, z, c, -k), t) for k in (1, 2, 3, 4)]
-    barrier = pltpu.get_barrier_semaphore()
-    for peer in [sibling] + ahead:
-        pl.semaphore_signal(barrier, inc=1, device_id=peer, device_id_type=MESH)
-    pl.semaphore_wait(barrier, 5)
 
     def near(i):
         return pltpu.make_async_remote_copy(
@@ -620,6 +650,7 @@
 
     for i in (3, 2, 1, 0):
         near(i).start()
+    yield
     for i in (3, 2, 1, 0):
         near(i).wait_recv()
     for k in (4, 3, 2, 1, 0):
@@ -635,6 +666,7 @@
         lax.fori_loop(0, groups, step, 0)
         if k > 0:
             far(k).start()
+    yield
     for k in (1, 2, 3, 4):
         far(k).wait_recv()
 
@@ -646,37 +678,11 @@
         return carry
 
     lax.fori_loop(0, groups, last, 0)
+    yield
     for k in (1, 2, 3, 4):
         far(k).wait_send()
     for i in range(4):
         near(i).wait_send()
-
-
-def send_back(rows, collective_id, name):
-    groups, width = rows.shape[0] // 72, rows.shape[1]
-    vmem = pl.BlockSpec(memory_space=pltpu.VMEM)
-    own = pl.pallas_call(
-        send_back_kernel,
-        out_shape=jax.ShapeDtypeStruct((groups, 8, width), rows.dtype),
-        in_specs=[vmem],
-        out_specs=vmem,
-        scratch_shapes=[
-            pltpu.VMEM((5, groups, 8, width), rows.dtype),
-            pltpu.VMEM((4, groups, 8, width), rows.dtype),
-            pltpu.VMEM((4, groups, 8, width), rows.dtype),
-            pltpu.SemaphoreType.DMA,
-            pltpu.SemaphoreType.DMA((4,)),
-            pltpu.SemaphoreType.DMA((4,)),
-            pltpu.SemaphoreType.DMA((4,)),
-            pltpu.SemaphoreType.DMA((4,)),
-        ],
-        compiler_params=pltpu.CompilerParams(
-            collective_id=collective_id, has_side_effects=True, vmem_limit_bytes=60 * 2**20
-        ),
-        cost_estimate=pl.CostEstimate(flops=0, bytes_accessed=20 * rows.size, transcendentals=0),
-        name=name,
-    )(rows.reshape(9, groups, 8, width))
-    return own.reshape(8 * groups, width)
 
 
 def contract(left_side, right_side, left_dim, right_dim):
@@ -967,6 +973,10 @@
 SCALE = (NOPE + ROPE) ** (-0.5)
 
 
+def in_groups(values):
+    return values.reshape(values.shape[0] // 8, 8, values.shape[1])
+
+
 def lanes(shape):
     return lax.broadcasted_iota(jnp.int32, shape, 1)
 
@@ -1052,9 +1062,23 @@
 
 
 def project_kernel(
-    hidden, weights, gain, gain_latent, cosine, sine_tab, normed_out, query_out, key_out, latent_out
+    hidden,
+    weights,
+    gain,
+    gain_latent,
+    cosine,
+    sine_tab,
+    normed_out,
+    query_out,
+    latent_out,
+    keys_out,
+    key_row,
+    landed,
+    *scratch,
 ):
     low = jnp.bfloat16
+    peers = reach_back_peers()
+    call(peers)
     normed = rms_forward(hidden[...].astype(jnp.float32), gain[...])[0].astype(low)
     normed_out[...] = normed
     query = contract(normed, weights[:, :768], 1, 0)
@@ -1065,10 +1089,15 @@
     query_out[:, 640:768] = (second * cos + first * sin).astype(low)
     latent = contract(normed, weights[:, 768:1408], 1, 0)
     latent_out[...] = latent[:, :RANK]
-    key_out[:, :RANK] = rms_forward(latent[:, :RANK], gain_latent[...])[0].astype(low)
+    compressed = rms_forward(latent[:, :RANK], gain_latent[...])[0]
+    key_row[:, :, :RANK] = in_groups(compressed).astype(low)
     rope = latent[:, RANK:]
     kept, crossed = turn_tables(cos, sin)
-    key_out[:, RANK:] = (rope * kept + exchange_halves(rope) * crossed).astype(low)
+    turned = rope * kept + exchange_halves(rope) * crossed
+    key_row[:, :, RANK:] = in_groups(turned).astype(low)
+    hear(peers)
+    reach_back_run(key_row, landed, *scratch)
+    keys_out[...] = landed[...]
 
 
 def attend_kernel(
@@ -1086,8 +1115,13 @@
     probs,
     expanded,
     key_rope,
+    held,
+    landed,
+    *scratch,
 ):
     low = jnp.bfloat16
+    peers = line_peers()
+    call(peers)
     rows = query.shape[0]
     count = keys.shape[0]
     fold = fold_matrix()
@@ -1103,7 +1137,7 @@
     distance = lax.broadcasted_iota(jnp.int32, shape, 0) + WINDOW - lanes(shape)
     allowed = jnp.logical_and(distance >= 0, distance < WINDOW)
     allowed = jnp.logical_and(allowed, own_segment[...] == key_segment[...])
-    total = jnp.zeros(out.shape, jnp.float32)
+    total = jnp.zeros((rows, wo_0.shape[0]), jnp.float32)
     for head, wo in enumerate((wo_0, wo_1, wo_2, wo_3)):
         start = 256 * head
         scores = contract(query[:, 128 * head : 128 * head + 128], expanded[:, start : start + 128], 1, 1)
@@ -1116,7 +1150,14 @@
         mixed = contract(share.astype(low), expanded[:, start + 128 : start + 256], 1, 0).astype(low)
         attended[:, 128 * head : 128 * head + 128] = mixed
         total += contract(mixed, wo[...], 1, 1)
-    out[...] = total.astype(low)
+    held[...] = in_groups(total).astype(low)
+    hear(peers)
+    line = Line(held, landed, *scratch)
+    line.scatter()
+    line.add()
+    line.gather()
+    line.finish()
+    out[...] = landed[...]
 
 
 def route_kernel(hidden, attention, gain, router, routes, token_out, middle_out, gates_out):
@@ -1159,9 +1200,11 @@
     change = contract(cotangent[...], weights[:, 1536:], 1, 0)
     grad_gate = (change * up * (sigmoid * (1.0 + gate * (1.0 - sigmoid)))).astype(low)
     grad_up = (change * on).astype(low)
-    back_out[...] = contract(grad_gate, weights[:, :768], 1, 1) + contract(
+    width = normed.shape[1]
+    back_out[:, :width] = contract(grad_gate, weights[:, :768], 1, 1) + contract(
         grad_up, weights[:, 768:1536], 1, 1
     )
+    back_out[:, width:] = jnp.zeros((normed.shape[0], 128), jnp.float32)
 
     def grads(i, carry):
         part = pl.ds(pl.multiple_of(i * 256, 256), 256)
@@ -1195,18 +1238,37 @@
     query_w,
     cosine,
     sine_tab,
+    normed,
+    attended,
     middle_out,
     attention_out,
     gain_out,
     logits_out,
+    own_out,
+    query_sum_out,
+    latent_sum_out,
+    changes,
+    ropes,
     query_out,
     back_out,
     keys_out,
-    expand_out,
-    changes,
-    ropes,
+    grads_out,
+    held,
+    near_in,
+    far_in,
+    ssem,
+    rsem,
+    pssem,
+    prsem,
+    latent,
+    landed_one,
+    landed_two,
+    *scratch,
 ):
     low = jnp.bfloat16
+    t, x, z, c = place()
+    peers = plane_peers() + line_peers() + [(chip_at(x, z, c, k), t) for k in (1, 2, 3, 4)]
+    call(peers)
     width = middle.shape[1]
     rows = middle.shape[0]
     lane = lanes((rows, 128))
@@ -1264,23 +1326,64 @@
     cos, sin = cosine[...], sine_tab[...]
     query_out[:, 512:640] = (first * cos + second * sin).astype(low)
     query_out[:, 640:768] = (second * cos - first * sin).astype(low)
-    back_out[...] = contract(query_out[...], query_w[...], 1, 1).astype(low)
+    back_out[...] = in_groups(contract(query_out[...], query_w[...], 1, 1)).astype(low)
     fold = fold_matrix()
 
     def key_rows(i, carry):
         part = pl.ds(pl.multiple_of(i * rows, rows), rows)
-        keys_out[part, :RANK] = contract(changes[part, :], expand[...], 1, 1).astype(low)
-        keys_out[part, RANK:] = contract(ropes[part, :].astype(low), fold, 1, 1).astype(low)
+        compressed = contract(changes[part, :], expand[...], 1, 1)
+        keys_out[i, :, :, :RANK] = in_groups(compressed).astype(low)
+        rope = contract(ropes[part, :].astype(low), fold, 1, 1)
+        keys_out[i, :, :, RANK:] = in_groups(rope).astype(low)
         return carry
 
     lax.fori_loop(0, keys.shape[0] // rows, key_rows, 0)
+    hear(peers)
+    back = send_back_steps(keys_out, latent, held, near_in, far_in, ssem, rsem, pssem, prsem)
+    advance(back, 1)
+    line_one = Line(back_out, landed_one, *scratch[:3])
+    line_two = Line(latent, landed_two, *scratch[3:6])
+    line_one.scatter()
+    advance(back, 1)
     for j in range(4):
         grad_expand = contract(keys[:, :RANK], changes[:, 256 * j : 256 * j + 256], 0, 0)
-        expand_out[:, 16 * j : 16 * j + 16, :] = grad_expand.astype(low).reshape(32, 16, 256)
+        grads_out[:, 2 * j : 2 * j + 2, :, 1280:] = grad_expand.reshape(32, 2, 8, 256).astype(low)
+
+    def grads(i, carry):
+        part = pl.ds(pl.multiple_of(i * 256, 256), 256)
+        some = pl.ds(i * 4, 4)
+        of_query = contract(normed[:, part], query_out[...], 0, 0)
+        grads_out[some, :, :, :768] = of_query.reshape(4, 8, 8, 768).astype(low)
+        of_output = contract(attention_out[:, part], attended[...], 0, 0)
+        grads_out[some, :, :, 768:1280] = of_output.reshape(4, 8, 8, 512).astype(low)
+        return carry
+
+    lax.fori_loop(0, width // 256, grads, 0)
+    line_one.add()
+    line_one.gather()
+
+    def emit(i, total):
+        own_out[i] = total
+
+    plane = plane_sum_steps(grads_out, emit, scratch[6:])
+    advance(plane, 5)
+    advance(back, 1)
+    line_two.scatter()
+    advance(plane, 8)
+    line_two.add()
+    line_two.gather()
+    advance(plane, PLANE_STEPS - 13)
+    line_one.finish()
+    query_sum_out[...] = landed_one[...]
+    line_two.finish()
+    latent_sum_out[...] = landed_two[...]
+    advance(back, 1)
+    advance(plane, 1)
 
 
 def finish_kernel(
-    summed,
+    query_sum,
+    latent_sum,
     latent,
     gain_latent,
     cosine,
@@ -1294,59 +1397,89 @@
     gain,
     grad_middle,
     normed,
-    grad_attn,
     normed_two,
     grad_logits,
-    grad_query,
-    attended,
+    gain_two_grad,
+    layer,
     input_out,
-    gain_out,
-    gain_latent_out,
+    own_out,
+    layer_out,
+    changes,
     grads_out,
-    changes,
+    landed,
+    *scratch,
 ):
     low = jnp.bfloat16
-    width = hidden.shape[1]
-    grad_latent = summed[:, width : width + RANK].astype(jnp.float32)
-    rope = summed[:, width + RANK :].astype(jnp.float32)
+    peers = plane_peers() + line_peers()
+    call(peers)
+    grad_latent = latent_sum[:, :RANK].astype(jnp.float32)
+    rope = latent_sum[:, RANK:].astype(jnp.float32)
     values = latent[...]
     inverse = lax.rsqrt(jnp.mean(values * values, 1, keepdims=True) + epsilon)
     weighted = grad_latent * gain_latent[...]
     aligned = jnp.mean(values * weighted, 1, keepdims=True)
-    gain_latent_out[...] = jnp.sum(grad_latent * values * inverse, 0, keepdims=True)
+    gain_latent_grad = jnp.sum(grad_latent * values * inverse, 0, keepdims=True)
     changes[:, :RANK] = (
         inverse * weighted - values * (inverse * inverse * inverse) * aligned
     ).astype(low)
     kept, crossed = turn_tables(cosine[...], sine_tab[...])
     changes[:, RANK:] = (rope * kept - exchange_halves(rope) * crossed).astype(low)
-    grad_normed = summed[:, :width].astype(jnp.float32)
+    grad_normed = query_sum[...].astype(jnp.float32)
+    width = hidden.shape[1]
     for j, wl in enumerate((wl_0, wl_1, wl_2, wl_3, wl_4)):
         grad_normed += contract(changes[:, 128 * j : 128 * j + 128], wl[...], 1, 1)
     values = hidden[...].astype(jnp.float32)
     inverse = lax.rsqrt(jnp.mean(values * values, 1, keepdims=True) + epsilon)
     weighted = grad_normed * gain[...]
     aligned = jnp.mean(values * weighted, 1, keepdims=True)
-    gain_out[...] = jnp.sum(grad_normed * values * inverse, 0, keepdims=True)
+    gain_grad = jnp.sum(grad_normed * values * inverse, 0, keepdims=True)
     input_out[...] = (
         grad_middle[...] + inverse * weighted - values * (inverse * inverse * inverse) * aligned
     ).astype(low)
 
     def grads(i, carry):
         part = pl.ds(pl.multiple_of(i * 256, 256), 256)
+        some = pl.ds(i * 4, 4)
         rows = normed[:, part]
-        grads_out[part, :768] = contract(rows, grad_query[...], 0, 0).astype(low)
-        grads_out[part, 768:1280] = contract(rows, changes[:, :RANK], 0, 0).astype(low)
+        of_latent = contract(rows, changes[:, :RANK], 0, 0)
+        grads_out[some, :, :, :RANK] = of_latent.reshape(4, 8, 8, RANK).astype(low)
         mixed = contract(rows, changes[:, RANK:], 0, 0)
         mixed += contract(normed_two[:, part], grad_logits[...], 0, 0)
-        grads_out[part, 1280:1408] = mixed.astype(low)
-        grads_out[part, 1408:] = contract(grad_attn[:, part], attended[...], 0, 0).astype(low)
+        grads_out[some, :, :, RANK : RANK + 128] = mixed.reshape(4, 8, 8, 128).astype(low)
         return carry
 
-    lax.fori_loop(0, grads_out.shape[0] // 256, grads, 0)
+    lax.fori_loop(0, width // 256, grads, 0)
+    grads_out[:, 1:, :, RANK + 128 :] = jnp.zeros((32, 7, 8, 128), low)
+    line_number = lax.broadcasted_iota(jnp.int32, (8, 128), 0)
+    gain_two = gain_two_grad[...]
+    for e in range(32):
+        block = jnp.zeros((8, 128), jnp.float32)
+        for row, (values, size) in enumerate(
+            ((gain_grad, 64), (gain_two, 64), (gain_latent_grad, 16))
+        ):
+            piece = values[:, size * e : size * e + size]
+            piece = jnp.concatenate([piece, jnp.zeros((1, 128 - size), jnp.float32)], 1)
+            block = jnp.where(line_number == row, piece, block)
+        grads_out[e, 0, :, RANK + 128 :] = block.astype(low)
+    hear(peers)
+    line = Line(layer, landed, *scratch[:3])
+    line.scatter()
+
+    def emit(i, total):
+        own_out[i] = total
+
+    plane = plane_sum_steps(grads_out, emit, scratch[3:])
+    advance(plane, 10)
+    line.add()
+    line.gather()
+    advance(plane, PLANE_STEPS)
+    line.finish()
+    layer_out[...] = landed[...]
 
 
 def unpack_kernel(
     own,
+    last,
     ffn,
     middle,
     layer,
@@ -1367,12 +1500,12 @@
         for half in (0, 1):
             to, start = 192 * head + 128 + 32 * half, 512 + 128 * half + 32 * head
             query_out[:, to : to + 32] = own[:, start : start + 32]
-    latent_out[...] = own[:, 768:1344]
-    router_out[...] = own[:, 1344:1408]
-    output_out[...] = own[:, 1408:1920]
-    gains_out[...] = own[0:8, 1920:2048]
+    latent_out[...] = last[:, :576]
+    router_out[...] = last[:, 576:640]
+    output_out[...] = own[:, 768:1280]
+    gains_out[...] = last[0:8, 640:768]
     for j in range(4):
-        expand_out[:, 256 * j : 256 * j + 256] = own[16 * j : 16 * j + 16, 2048:2304]
+        expand_out[:, 256 * j : 256 * j + 256] = own[16 * j : 16 * j + 16, 1280:1536]
     gate_out[...] = ffn[:, :704].astype(jnp.float32)
     up_out[...] = ffn[:, 768:1472].astype(jnp.float32)
     down_out[...] = ffn[:, 1536:2240].astype(jnp.float32)
@@ -1401,6 +1534,39 @@
         ],
         scratch_shapes=[pltpu.VMEM(shape, dtype) for shape, dtype in scratch],
         compiler_params=pltpu.CompilerParams(vmem_limit_bytes=60 * 2**20),
+        name=name,
+    )(*arrays)
+
+
+def joint_call(kernel, collective_id, name, operands, out_shapes, scratch, moved):
+    arrays, specs = [], []
+    for operand in operands:
+        if isinstance(operand, tuple):
+            array, block, index = operand
+        else:
+            array, block, index = operand, operand.shape, (0,) * operand.ndim
+        specs.append(
+            pl.BlockSpec(block, lambda i, index=index: index, pipeline_mode=pl.Buffered(1))
+        )
+        arrays.append(array)
+    return pl.pallas_call(
+        kernel,
+        grid=(1,),
+        out_shape=[jax.ShapeDtypeStruct(shape, dtype) for shape, dtype in out_shapes],
+        in_specs=specs,
+        out_specs=[
+            pl.BlockSpec(
+                shape,
+                lambda i, zeros=(0,) * len(shape): zeros,
+                pipeline_mode=pl.Buffered(1),
+            )
+            for shape, _ in out_shapes
+        ],
+        scratch_shapes=scratch,
+        compiler_params=pltpu.CompilerParams(
+            collective_id=collective_id, has_side_effects=True, vmem_limit_bytes=60 * 2**20
+        ),
+        cost_estimate=pl.CostEstimate(flops=0, bytes_accessed=moved, transcendentals=0),
         name=name,
     )(*arrays)
 
@@ -1474,8 +1640,10 @@
     doc_start = jnp.sum((segments[None, :] < own_segments[:, None]).astype(jnp.int32), 1)
     cosine, sine_tab = rope_tables(row_index - doc_start)
     cosine, sine_tab = jnp.tile(cosine, (1, 4)), jnp.tile(sine_tab, (1, 4))
-    normed, queries, key_row, latent = local_call(
+    key_count = 9 * tokens
+    normed, queries, latent, keys_all = joint_call(
         project_kernel,
+        2,
         "project",
         (
             hidden_in,
@@ -1488,28 +1656,41 @@
         (
             ((tokens, model_width), low),
             ((tokens, 768), low),
-            ((tokens, 640), low),
             ((tokens, RANK), full),
+            ((9, tokens // 8, 8, 640), low),
         ),
-    )
-    keys_all = reach_back(key_row, 2, "reach_back")
-    key_count = keys_all.shape[0]
+        [
+            pltpu.VMEM((tokens // 8, 8, 640), low),
+            pltpu.VMEM((9, tokens // 8, 8, 640), low),
+            pltpu.SemaphoreType.DMA,
+            pltpu.SemaphoreType.DMA((4,)),
+            pltpu.SemaphoreType.DMA((4,)),
+            pltpu.SemaphoreType.DMA((4,)),
+            pltpu.SemaphoreType.DMA((4,)),
+        ],
+        2**25,
+    )
+    keys_all = keys_all.reshape(key_count, 640)
     key_segments = lax.dynamic_slice_in_dim(
         jnp.pad(segments, (key_count - tokens, 0), constant_values=-1), first_row, key_count
     )
-    attn_part, attended, probs, expanded, key_rope = local_call(
+    attn_out, attended, probs, expanded, key_rope = joint_call(
         attend_kernel,
+        3,
         "attend",
         (keys_all, expand_w, queries, own_segments[:, None], key_segments[None], *output_blocks),
         (
-            ((tokens, model_width), low),
+            ((tokens // 8, 8, model_width), low),
             ((tokens, HEADS * VH), low),
             ((HEADS, tokens, key_count), full),
             ((key_count, HEADS * (NOPE + VH)), low),
             ((key_count, 256), low),
         ),
-    )
-    attn_out = line_sum(attn_part, 3, "sum_heads")
+        [pltpu.VMEM((tokens // 8, 8, model_width), low)] * 2
+        + line_scratch(tokens // 8, model_width),
+        2**25,
+    )
+    attn_out = attn_out.reshape(tokens, model_width)
 
     token_row, middle, gates = local_call(
         route_kernel,
@@ -1521,8 +1702,6 @@
             ((tokens, 128), full),
         ),
     )
-    token_rows = plane_gather(token_row, 4, "gather_tokens")
-    token_row, token_rows = lax.optimization_barrier((token_row, token_rows))
     normed_two = (token_row, (tokens, model_width), (0, 0))
 
     shared_part, shared_back, ffn_grads = local_call(
@@ -1531,12 +1710,13 @@
         (normed_two, cotangent, ffn_all),
         (
             ((tokens, model_width), full),
-            ((tokens, model_width), full),
+            ((tokens, model_width + 128), full),
             (ffn_all.shape, low),
         ),
     )
-    ffn_grads, token_rows = lax.optimization_barrier((ffn_grads, token_rows))
     own_ffn = lax.psum_scatter(ffn_grads, "expert", scatter_dimension=0, tiled=True)
+    token_row, _ = lax.optimization_barrier((token_row, ffn_grads))
+    token_rows = plane_gather(token_row, 4, "gather_tokens")
 
     routed_part, back_part, out_egate, out_eup, out_edown = experts(
         token_rows.reshape(devices // 2, 2 * tokens, -1),
@@ -1546,25 +1726,24 @@
         expert_down,
     )
     out_egate, out_eup = out_egate.swapaxes(1, 2), out_eup.swapaxes(1, 2)
+    routed_part, own_ffn = lax.optimization_barrier((routed_part, own_ffn))
     routed_own = lax.psum_scatter(
         routed_part.reshape(-1, model_width), "expert", scatter_dimension=0, tiled=True
     )
     layer_part = (routed_own.astype(full) + shared_part).astype(low)
-    back_own = plane_sum((back_part.reshape(devices * tokens, -1),), 5, "sum_tokens")
-    back_wide = back_own + jnp.pad(shared_back, ((0, 0), (0, 128)))
-    back_all = line_sum(back_wide.astype(low), 6, "sum_units")
+    back_all = sum_tokens(back_part.reshape(devices * tokens, -1), shared_back, 5)
 
     (
         grad_middle,
         grad_attn,
         grad_gain_two,
         grad_logits,
-        grad_query_pre,
-        query_back,
-        grad_keys,
-        grad_expand,
-    ) = local_call(
+        own,
+        query_sum,
+        latent_sum,
+    ) = joint_call(
         attend_back_kernel,
+        7,
         "attend_back",
         (
             back_all,
@@ -1584,26 +1763,51 @@
             (attention_all, (model_width, 768), (0, 0)),
             cosine,
             sine_tab,
+            normed,
+            attended,
         ),
         (
             ((tokens, model_width), full),
             ((tokens, model_width), low),
             ((1, model_width), full),
             ((tokens, 128), low),
-            ((tokens, 768), low),
-            ((tokens, model_width), low),
-            ((key_count, 640), low),
-            ((devices, shard, 256), low),
+            ((shard // 8, 8, 1536), full),
+            ((tokens // 8, 8, model_width), low),
+            ((tokens // 8, 8, 640), low),
         ),
-        (((key_count, HEADS * (NOPE + VH)), low), ((key_count, 256), full)),
-    )
-    latent_part = send_back(grad_keys, 7, "send_back")
-    summed = line_sum(jnp.concatenate([query_back, latent_part], 1), 8, "sum_inputs")
-    grad_input, grad_gain_one, grad_gain_latent, many_grads = local_call(
+        [
+            pltpu.VMEM((key_count, HEADS * (NOPE + VH)), low),
+            pltpu.VMEM((key_count, 256), full),
+            pltpu.VMEM((tokens, 768), low),
+            pltpu.VMEM((tokens // 8, 8, model_width), low),
+            pltpu.VMEM((9, tokens // 8, 8, 640), low),
+            pltpu.VMEM((devices, shard // 8, 8, 1536), low),
+            pltpu.VMEM((5, tokens // 8, 8, 640), low),
+            pltpu.VMEM((4, tokens // 8, 8, 640), low),
+            pltpu.VMEM((4, tokens // 8, 8, 640), low),
+            pltpu.SemaphoreType.DMA((4,)),
+            pltpu.SemaphoreType.DMA((4,)),
+            pltpu.SemaphoreType.DMA((4,)),
+            pltpu.SemaphoreType.DMA((4,)),
+            pltpu.VMEM((tokens // 8, 8, 640), low),
+            pltpu.VMEM((tokens // 8, 8, model_width), low),
+            pltpu.VMEM((tokens // 8, 8, 640), low),
+        ]
+        + line_scratch(tokens // 8, model_width)
+        + line_scratch(tokens // 8, 640)
+        + plane_scratch(shard // 8, 1536),
+        2**26,
+    )
+    own = own.reshape(shard, 1536)
+    query_sum = query_sum.reshape(tokens, model_width)
+    latent_sum = latent_sum.reshape(tokens, 640)
+    grad_input, own_last, layer_sum = joint_call(
         finish_kernel,
+        9,
         "finish",
         (
-            summed,
+            query_sum,
+            latent_sum,
             latent,
             gain_latent,
             cosine,
@@ -1613,38 +1817,27 @@
             gain_one,
             grad_middle,
             normed,
-            grad_attn,
             normed_two,
             grad_logits,
-            grad_query_pre,
-            attended,
+            grad_gain_two,
+            layer_part.reshape(tokens // 8, 8, model_width),
         ),
         (
             ((tokens, model_width), low),
-            ((1, model_width), full),
-            ((1, RANK), full),
-            ((model_width, 1920), low),
+            ((shard // 8, 8, 768), full),
+            ((tokens // 8, 8, model_width), low),
         ),
-        (((tokens, 640), low),),
-    )
-
-    gain_grads = jnp.stack(
         [
-            grad_gain_one.reshape(devices, shard),
-            grad_gain_two.reshape(devices, shard),
-            jnp.pad(
-                grad_gain_latent.reshape(devices, -1), ((0, 0), (0, shard - latent_norm.shape[0]))
-            ),
-        ],
-        1,
-    ).astype(low)
-    gain_grads = jnp.pad(gain_grads, ((0, 0), (0, shard - 3), (0, 128 - shard)))
-    own, layer_sum = plane_sum(
-        (many_grads, gain_grads.reshape(model_width, 128), grad_expand.reshape(model_width, 256)),
-        9,
-        "sum_attention",
-        layer_part,
-    )
+            pltpu.VMEM((tokens, 640), low),
+            pltpu.VMEM((devices, shard // 8, 8, 768), low),
+            pltpu.VMEM((tokens // 8, 8, model_width), low),
+        ]
+        + line_scratch(tokens // 8, model_width)
+        + plane_scratch(shard // 8, 768),
+        2**25,
+    )
+    own_last = own_last.reshape(shard, 768)
+    layer_sum = layer_sum.reshape(tokens, model_width)
     (
         layer_out,
         out_query,
@@ -1659,7 +1852,7 @@
     ) = local_call(
         unpack_kernel,
         "unpack",
-        (own, own_ffn, middle, layer_sum),
+        (own, own_last, own_ffn, middle, layer_sum),
         (
             ((tokens, model_width), low),
             (w_query.shape, full),

time: 545 us -> 453 us (0.83)
  Pallas kernels: 481 us -> 412 us
  waiting for transfers between devices: 17.9 us -> 0.83 us
  other arithmetic: 8.95 us -> 3.2 us
    pallas_call x8 -> x4, Pallas kernels: 72.4 us -> 25.6 us  [local_call(): pl.pallas_call(kernel, grid=(1,), out_shape=shapes, in_specs=specs, out_s...]
    pallas_call x7 -> x5, Pallas kernels: 239 us -> 220 us  [the longest x4 147 us: joint_call(): pl.pallas_call(kernel, grid=(1,), out_shape=[jax.ShapeDtypeStruct(shape,...]
    reduce_scatter x1, waiting for transfers between devices: 16.6 us -> 0.02 us  [body(): lax.psum_scatter(ffn_grads, 'expert', scatter_dimension=0, tiled=True)]
  transfers between devices with their start and end apart: 4 -> 4, of which waited for: 1 -> 0; matrix products, arithmetic and copies ran while one was open for 4% -> 3% of each run, Pallas kernels for 75% -> 84%
where the time goes in v2:
time: 453 us; the launch traced here: 448 us
  Pallas kernels  412 us (91%)
  local copies, waits for them, and re-layouts  18 us (4%)
  between operations  14.4 us (3%)
    pallas_call x4, Pallas kernels, joint_call(): pl.pallas_call(kernel, grid=(1,), out_shape=[jax.ShapeDtypeStruct(shape,...  147 us
    pallas_call x2, Pallas kernels, plane_gather(): pl.pallas_call(plane_gather_kernel, out_shape=jax.ShapeDtypeStruct((32, *...  95.5 us
    pallas_call x1, Pallas kernels, communicate(): pl.pallas_call(kernel, out_shape=shapes, in_specs=[vmem if inside else HB...  73 us
    pallas_call x1, Pallas kernels, experts(): pl.pallas_call(experts_kernel, grid=(2 * blocks + 2,), out_shape=(jax.Sha...  70.3 us
    pallas_call x4, Pallas kernels, local_call(): pl.pallas_call(kernel, grid=(1,), out_shape=shapes, in_specs=specs, out_s...  25.6 us
  transfers between devices with their start and end apart: 4, of which 0 were waited for; matrix products, arithmetic and copies ran while one was open for 3% of the time, Pallas kernels for 84%

profile of v2, /device:TPU:0, one launch (start us, length us, event | category | flops | bytes accessed | tf_op | source)
XLA Modules:
  0.0 448.4 jit_solution(7833935260046842260)
XLA Ops:
  7.2 0.0 all-gather.4.cloned.1.call-start
  7.2 1.2 pad_bitcast_fusion.gain_latent
  8.4 2.3 pack.1
  10.7 0.0 all-gather.4.cloned.1.call-update
  10.7 0.0 all-gather.6.cloned.1.call-start
  10.8 0.7 all-gather.6.cloned.1.call-update
  11.5 0.0 reduce-scatter.3.cloned.1.call-start
  11.6 0.8 dynamic_slice.6
  12.3 0.8 pad_dynamic-slice_fusion
  13.1 0.6 broadcast_in_dim.23.key_segment
  13.7 1.1 convert_reduce_fusion
  14.8 0.1 multiply_sine_fusion
  14.9 0.7 copy.52.sine_tab
  15.7 0.8 dynamic-slice_bitcast_fusion
  16.4 0.7 copy.54.own_segment
  17.2 1.4 copy.55.routes
  18.6 0.7 copy.51.cosine
  19.3 42.8 %gather_attention.1 = bf16[32,8,8,2176]{3,2,1,0:T(8,128)(2,1)} custom-call(bf16[8,8,2176]{2,1,0:T(8,128)(2,1)} %bitcast.86), custom_call_target="tpu_custom_call" | custom-call | bytes 17825792 | tf_op jit(solution)/shard_map/gather_attention/pallas_call | solution.py:172
  62.1 0.9 slice.32
  63.1 0.7 reshape_squeeze.10.gain_latent
  63.7 0.7 reshape_squeeze.11.gain
  64.4 0.7 reshape_squeeze.9.gain
  65.1 1.3 slice.35
  66.4 0.5 copy.53
  66.9 1.2 copy.62
  68.1 24.6 %project.1 = (bf16[128,2048]{1,0:T(8,128)(2,1)}, bf16[128,768]{1,0:T(8,128)(2,1)}, f32[128,512]{1,0:T(8,128)}, bf16[9,16,8,640]{3,2,1,0:T(8,128)(2,1)}) custom-call(bf16[128,2048]{1,0:T(8,128)(2,1)} %hidden.5, bf16[2048,2176]{1,0:T(8,128)(2,1)} %bitcast.55, f32[1,2048]{1,0:T(1,128)} %reshape_squeeze.9.gain, f32[1,512]{1,0:T(1,128)} %reshape_squeeze.10.gain_latent, ...), custom_call_target="tpu_custom_call" | custom-call | bytes 33554432 | tf_op jit(solution)/shard_map/project/pallas_call | solution.py:1552
  92.8 29.3 %attend.1 = (bf16[16,8,2048]{2,1,0:T(8,128)(2,1)}, bf16[128,512]{1,0:T(8,128)(2,1)}, f32[4,128,1152]{2,1,0:T(8,128)}, bf16[1152,1024]{1,0:T(8,128)(2,1)}, bf16[1152,256]{1,0:T(8,128)(2,1)}) custom-call(bf16[1152,640]{1,0:T(8,128)(2,1)} %bitcast.75, bf16[512,1024]{1,0:T(8,128)(2,1)} %bitcast.73, bf16[128,768]{1,0:T(8,128)(2,1)} %get-tuple-element.62.query, ...), custom_call_target="tpu_custom_call" | custom-call | bytes 33554432 | tf_op jit(solution)/shard_map/attend/pallas_call | solution.py:1552
  122.1 0.0 all-gather.4.cloned.1.call-done.router.weights
  122.2 3.4 route.1
  125.5 16.9 %shared.1 = (f32[128,2048]{1,0:T(8,128)}, f32[128,2176]{1,0:T(8,128)}, bf16[2048,2304]{1,0:T(8,128)(2,1)}) custom-call(bf16[128,2176]{1,0:T(8,128)(2,1)} %get-tuple-element.67.normed.normed_two, bf16[128,2048]{1,0:T(8,128)(2,1)} %cotangent.3, bf16[2048,2304]{1,0:T(8,128)(2,1)} %all-gather.4.cloned.1.call-done.router.weights), custom_call_target="tpu_custom_call" | custom-call | tf_op jit(solution)/shard_map/shared/pallas_call | solution.py:1526
  142.5 0.0 reduce-scatter.3.cloned.1.call-update
  142.5 0.0 reduce-scatter.5.cloned.1.call-start
  142.5 52.7 %gather_tokens.1 = bf16[32,16,8,2176]{3,2,1,0:T(8,128)(2,1)} custom-call(bf16[16,8,2176]{2,1,0:T(8,128)(2,1)} %bitcast.77), custom_call_target="tpu_custom_call" | custom-call | bytes 35651584 | tf_op jit(solution)/shard_map/gather_tokens/pallas_call | solution.py:172
  195.3 0.0 all-gather.6.cloned.1.call-done
  195.3 70.3 %experts.1 = (bf16[16,256,2048]{2,1,0:T(8,128)(2,1)}, bf16[16,256,2176]{2,1,0:T(8,128)(2,1)}, f32[2,352,2048]{2,1,0:T(8,128)}, f32[2,352,2048]{2,1,0:T(8,128)}, f32[2,352,2048]{2,1,0:T(8,128)}) custom-call(bf16[16,256,2176]{2,1,0:T(8,128)(2,1)} %bitcast.71, bf16[16,256,2048]{2,1,0:T(8,128)(2,1)} %bitcast.95, f32[2,352,2048]{2,1,0:T(8,128)} %bitcast.96, ...), custom_call_target="tpu_custom_call" | custom-call | flops 21743271936 | bytes 104857600 | tf_op jit(solution)/shard_map/experts/pallas_call | solution.py:908
  265.6 0.0 reduce-scatter.3.cloned.1.call-done.ffn
  265.6 0.0 reduce-scatter.5.cloned.1.call-update
  265.6 73.0 %sum_tokens.1 = bf16[16,8,2176]{2,1,0:T(8,128)(2,1)} custom-call(bf16[32,16,8,2176]{3,2,1,0:T(8,128)(2,1)} %bitcast.70, f32[16,8,2176]{2,1,0:T(8,128)} %bitcast.81), custom_call_target="tpu_custom_call" | custom-call | bytes 142606336 | tf_op jit(solution)/shard_map/sum_tokens/pallas_call | solution.py:491
  338.7 0.0 copy-start
  338.7 63.4 %attend_back.1 = (f32[128,2048]{1,0:T(8,128)}, bf16[128,2048]{1,0:T(8,128)(2,1)}, f32[1,2048]{1,0:T(1,128)}, bf16[128,128]{1,0:T(8,128)(2,1)}, f32[8,8,1536]{2,1...) custom-call(bf16[128,2176]{1,0:T(8,128)(2,1)} %bitcast.80, f32[128,2048]{1,0:T(8,128)} %get-tuple-element.70.middle, ...), custom_call_target="tpu_custom_call" | custom-call | bytes 67108864 | tf_op jit(solution)/shard_map/attend_back/pallas_call | solution.py:1552
  402.1 0.0 reduce-scatter.5.cloned.1.call-done
  402.1 0.0 copy-done
  402.2 1.9 fusion.layer
  404.1 30.0 %finish.1 = (bf16[128,2048]{1,0:T(8,128)(2,1)}, f32[8,8,768]{2,1,0:T(8,128)}, bf16[16,8,2048]{2,1,0:T(8,128)(2,1)}) custom-call(bf16[128,2048]{1,0:T(8,128)(2,1)} %bitcast.82, bf16[128,640]{1,0:T(8,128)(2,1)} %bitcast.91, f32[128,512]{1,0:T(8,128)} %get-tuple-element.80.latent, f32[1,512]{1,0:T(1,128)} %reshape_squeeze.10.gain_latent, ...), custom_call_target="tpu_custom_call" | custom-call | bytes 33554432 | tf_op jit(solution)/shard_map/finish/pallas_call | solution.py:1552
  434.1 2.9 unpack.1
  437.1 1.2 slice_bitcast_fusion.1
  438.3 1.3 slice_bitcast_fusion
  439.5 1.9 copy.65
  (7 shorter events, 0.1 us)
Async XLA Ops:
  7.2 115.0 %all-gather.4.cloned.1.call-start = ((), (), s32[]{:S(2)}) async-start(), calls=%async_computation.2 | async-start | bytes 9732096 | tf_op jit(solution)/shard_map/all_gather | solution.py:1623
  10.7 184.5 %all-gather.6.cloned.1.call-start = ((), (), s32[]{:S(2)}) async-start(), calls=%async_computation.5 | async-start | bytes 17301504 | tf_op jit(solution)/shard_map/all_gather | solution.py:1624
  11.5 254.1 %reduce-scatter.3.cloned.1.call-start = ((), (), s32[]{:S(2)}) async-start(), calls=%async_computation.3 | async-start | bytes 9732096 | tf_op jit(solution)/shard_map/reduce_scatter | solution.py:1717
  142.5 259.7 %reduce-scatter.5.cloned.1.call-start = ((), (), s32[]{:S(2)}) async-start(), calls=%async_computation.4 | async-start | bytes 17301504 | tf_op jit(solution)/shard_map/reduce_scatter | solution.py:1730
  338.7 63.5 %copy-start = (f32[128,2048]{1,0:T(8,128)S(1)}, f32[128,2048]{1,0:T(8,128)}, u32[]{:S(2)}) copy-start(f32[128,2048]{1,0:T(8,128)} %get-tuple-element.86) | copy-start | bytes 3145732
Sparse Core Ops, SparseCore 0:
  10.9 63.9 all-gather.3
  77.1 72.4 all-gather.5
  153.3 99.3 reduce-scatter.2
  265.7 125.2 reduce-scatter.4

commit v3 on v2

--- a/solution.py
+++ b/solution.py
@@ -962,15 +962,14 @@
     return (values * inverse * gains, inverse)
 
 
-def rope_tables(positions):
-    half_dim = ROPE // 2
-    freqs = rope_base ** (-jnp.arange(half_dim, dtype=jnp.float32) / half_dim)
-    angles = positions.astype(jnp.float32)[:, None] * freqs[None, :]
-    return (jnp.cos(angles), jnp.sin(angles))
-
-
 HEADS = 4
 SCALE = (NOPE + ROPE) ** (-0.5)
+
+
+def column(row):
+    shape = (128, 128)
+    same = lax.broadcasted_iota(jnp.int32, shape, 0) == lanes(shape)
+    return jnp.sum(jnp.where(same, row.astype(jnp.float32), 0.0), 1, keepdims=True)
 
 
 def in_groups(values):
@@ -1047,7 +1046,8 @@
     row = lax.broadcasted_iota(jnp.int32, (shard, shard), 0)
     gains = jnp.where(row == 0, gain_one[...], 0.0)
     gains = jnp.where(row == 1, gain_two[...], gains)
-    gains = jnp.where(row == 2, gain_latent[...], gains)
+    rest = jnp.zeros((1, shard - gain_latent.shape[1]), jnp.float32)
+    gains = jnp.where(row == 2, jnp.concatenate([gain_latent[...], rest], 1), gains)
     attention_out[:, 1280:1408] = jnp.concatenate([latent[:, RANK:], gains], 1).astype(low)
     attention_out[:, 1408:1920] = output[...].astype(low)
     for j in range(4):
@@ -1064,14 +1064,17 @@
 def project_kernel(
     hidden,
     weights,
-    gain,
-    gain_latent,
-    cosine,
-    sine_tab,
+    segments,
+    frequencies,
     normed_out,
     query_out,
     latent_out,
     keys_out,
+    cosine_out,
+    sine_out,
+    gain_one_out,
+    gain_two_out,
+    gain_latent_out,
     key_row,
     landed,
     *scratch,
@@ -1079,17 +1082,34 @@
     low = jnp.bfloat16
     peers = reach_back_peers()
     call(peers)
-    normed = rms_forward(hidden[...].astype(jnp.float32), gain[...])[0].astype(low)
+    own_index = lax.axis_index("expert")
+    rows = hidden.shape[0]
+    own = column(segments[pl.ds(own_index, 1), :])
+    before = jnp.zeros((rows, 128), jnp.float32)
+    for i in range(segments.shape[0]):
+        before += jnp.where(segments[i : i + 1, :].astype(jnp.float32) < own, 1.0, 0.0)
+    start = jnp.sum(before, 1, keepdims=True)
+    index = (lax.broadcasted_iota(jnp.int32, (rows, 1), 0) + own_index * rows).astype(jnp.float32)
+    angles = (index - start) * frequencies[...]
+    cos, sin = jnp.cos(angles), jnp.sin(angles)
+    cosine_out[...] = cos
+    sine_out[...] = sin
+    gains = [
+        weights[64 * e : 64 * e + 16, 1280:1408].astype(jnp.float32) for e in range(32)
+    ]
+    gain_one_out[...] = jnp.concatenate([block[0:1, 64:128] for block in gains], 1)
+    gain_two_out[...] = jnp.concatenate([block[1:2, 64:128] for block in gains], 1)
+    gain_latent_out[...] = jnp.concatenate([block[2:3, 64:80] for block in gains], 1)
+    normed = rms_forward(hidden[...].astype(jnp.float32), gain_one_out[...])[0].astype(low)
     normed_out[...] = normed
     query = contract(normed, weights[:, :768], 1, 0)
     first, second = query[:, 512:640], query[:, 640:768]
-    cos, sin = cosine[...], sine_tab[...]
     query_out[:, :512] = query[:, :512].astype(low)
     query_out[:, 512:640] = (first * cos - second * sin).astype(low)
     query_out[:, 640:768] = (second * cos + first * sin).astype(low)
     latent = contract(normed, weights[:, 768:1408], 1, 0)
     latent_out[...] = latent[:, :RANK]
-    compressed = rms_forward(latent[:, :RANK], gain_latent[...])[0]
+    compressed = rms_forward(latent[:, :RANK], gain_latent_out[...])[0]
     key_row[:, :, :RANK] = in_groups(compressed).astype(low)
     rope = latent[:, RANK:]
     kept, crossed = turn_tables(cos, sin)
@@ -1102,10 +1122,10 @@
 
 def attend_kernel(
     keys,
-    expand,
+    expand_0,
+    expand_1,
     query,
-    own_segment,
-    key_segment,
+    segments,
     wo_0,
     wo_1,
     wo_2,
@@ -1115,6 +1135,7 @@
     probs,
     expanded,
     key_rope,
+    expand,
     held,
     landed,
     *scratch,
@@ -1125,6 +1146,18 @@
     rows = query.shape[0]
     count = keys.shape[0]
     fold = fold_matrix()
+    for k, block in enumerate((expand_0, expand_1)):
+        for j in range(4):
+            part = block[...].reshape(32, 64, 128)[:, 16 * j : 16 * j + 16, :]
+            expand[:, 256 * j + 128 * k : 256 * j + 128 * k + 128] = part.reshape(RANK, 128)
+    own_index = lax.axis_index("expert")
+    own_segment = column(segments[pl.ds(own_index, 1), :])
+    key_segments = []
+    for j in range(9):
+        where = own_index - 8 + j
+        row = segments[pl.ds(jnp.maximum(where, 0), 1), :].astype(jnp.float32)
+        key_segments.append(jnp.where(where >= 0, row, -1.0))
+    key_segment = jnp.concatenate(key_segments, 1)
 
     def expand_rows(i, carry):
         part = pl.ds(pl.multiple_of(i * rows, rows), rows)
@@ -1136,7 +1169,7 @@
     shape = (rows, count)
     distance = lax.broadcasted_iota(jnp.int32, shape, 0) + WINDOW - lanes(shape)
     allowed = jnp.logical_and(distance >= 0, distance < WINDOW)
-    allowed = jnp.logical_and(allowed, own_segment[...] == key_segment[...])
+    allowed = jnp.logical_and(allowed, own_segment == key_segment)
     total = jnp.zeros((rows, wo_0.shape[0]), jnp.float32)
     for head, wo in enumerate((wo_0, wo_1, wo_2, wo_3)):
         start = 256 * head
@@ -1168,8 +1201,8 @@
     width = normed.shape[1]
     token_out[:, :width] = normed
     logits = contract(normed, router[...], 1, 0)
-    lane = lanes(logits.shape)
-    named = [routes[:, r : r + 1] for r in range(6)]
+    lane = lanes(logits.shape).astype(jnp.float32)
+    named = [column(routes[r : r + 1, :]) for r in range(6)]
     chosen = [
         jnp.sum(jnp.where(lane == number + 64, logits, 0.0), 1, keepdims=True) for number in named
     ]
@@ -1181,7 +1214,7 @@
     for r in range(6):
         weight = exponents[r] / total
         high = weight.astype(low).astype(jnp.float32)
-        extra += jnp.where(lane == r, named[r].astype(jnp.float32), 0.0)
+        extra += jnp.where(lane == r, named[r], 0.0)
         extra += jnp.where(lane == 8 + r, high, 0.0)
         extra += jnp.where(lane == 16 + r, weight - high, 0.0)
         gates += jnp.where(lane == r, weight, 0.0)
@@ -1271,9 +1304,9 @@
     call(peers)
     width = middle.shape[1]
     rows = middle.shape[0]
-    lane = lanes((rows, 128))
+    lane = lanes((rows, 128)).astype(jnp.float32)
     sums = back[:, width:].astype(jnp.float32)
-    named = [routes[:, r : r + 1] for r in range(6)]
+    named = [column(routes[r : r + 1, :]) for r in range(6)]
     weight = [gates[:, r : r + 1] for r in range(6)]
     change = [
         jnp.sum(jnp.where(lane == number + 64, sums, 0.0), 1, keepdims=True) for number in named
@@ -1326,25 +1359,6 @@
     cos, sin = cosine[...], sine_tab[...]
     query_out[:, 512:640] = (first * cos + second * sin).astype(low)
     query_out[:, 640:768] = (second * cos - first * sin).astype(low)
-    back_out[...] = in_groups(contract(query_out[...], query_w[...], 1, 1)).astype(low)
-    fold = fold_matrix()
-
-    def key_rows(i, carry):
-        part = pl.ds(pl.multiple_of(i * rows, rows), rows)
-        compressed = contract(changes[part, :], expand[...], 1, 1)
-        keys_out[i, :, :, :RANK] = in_groups(compressed).astype(low)
-        rope = contract(ropes[part, :].astype(low), fold, 1, 1)
-        keys_out[i, :, :, RANK:] = in_groups(rope).astype(low)
-        return carry
-
-    lax.fori_loop(0, keys.shape[0] // rows, key_rows, 0)
-    hear(peers)
-    back = send_back_steps(keys_out, latent, held, near_in, far_in, ssem, rsem, pssem, prsem)
-    advance(back, 1)
-    line_one = Line(back_out, landed_one, *scratch[:3])
-    line_two = Line(latent, landed_two, *scratch[3:6])
-    line_one.scatter()
-    advance(back, 1)
     for j in range(4):
         grad_expand = contract(keys[:, :RANK], changes[:, 256 * j : 256 * j + 256], 0, 0)
         grads_out[:, 2 * j : 2 * j + 2, :, 1280:] = grad_expand.reshape(32, 2, 8, 256).astype(low)
@@ -1359,20 +1373,42 @@
         return carry
 
     lax.fori_loop(0, width // 256, grads, 0)
+
+    def emit(i, total):
+        own_out[i] = total
+
+    hear(peers)
+    plane = plane_sum_steps(grads_out, emit, scratch[6:])
+    advance(plane, 1)
+    fold = fold_matrix()
+
+    def key_rows(i, carry):
+        part = pl.ds(pl.multiple_of(i * rows, rows), rows)
+        compressed = contract(changes[part, :], expand[...], 1, 1)
+        keys_out[i, :, :, :RANK] = in_groups(compressed).astype(low)
+        rope = contract(ropes[part, :].astype(low), fold, 1, 1)
+        keys_out[i, :, :, RANK:] = in_groups(rope).astype(low)
+        return carry
+
+    lax.fori_loop(0, keys.shape[0] // rows, key_rows, 0)
+    back = send_back_steps(keys_out, latent, held, near_in, far_in, ssem, rsem, pssem, prsem)
+    advance(back, 1)
+    advance(plane, 2)
+    back_out[...] = in_groups(contract(query_out[...], query_w[...], 1, 1)).astype(low)
+    line_one = Line(back_out, landed_one, *scratch[:3])
+    line_two = Line(latent, landed_two, *scratch[3:6])
+    line_one.scatter()
+    advance(back, 1)
+    advance(plane, 6)
     line_one.add()
     line_one.gather()
-
-    def emit(i, total):
-        own_out[i] = total
-
-    plane = plane_sum_steps(grads_out, emit, scratch[6:])
-    advance(plane, 5)
+    advance(plane, 4)
     advance(back, 1)
     line_two.scatter()
     advance(plane, 8)
     line_two.add()
     line_two.gather()
-    advance(plane, PLANE_STEPS - 13)
+    advance(plane, PLANE_STEPS - 21)
     line_one.finish()
     query_sum_out[...] = landed_one[...]
     line_two.finish()
@@ -1410,8 +1446,9 @@
     *scratch,
 ):
     low = jnp.bfloat16
-    peers = plane_peers() + line_peers()
-    call(peers)
+    greet(plane_peers() + line_peers())
+    line = Line(layer, landed, *scratch[:3])
+    line.scatter()
     grad_latent = latent_sum[:, :RANK].astype(jnp.float32)
     rope = latent_sum[:, RANK:].astype(jnp.float32)
     values = latent[...]
@@ -1461,15 +1498,12 @@
             piece = jnp.concatenate([piece, jnp.zeros((1, 128 - size), jnp.float32)], 1)
             block = jnp.where(line_number == row, piece, block)
         grads_out[e, 0, :, RANK + 128 :] = block.astype(low)
-    hear(peers)
-    line = Line(layer, landed, *scratch[:3])
-    line.scatter()
 
     def emit(i, total):
         own_out[i] = total
 
     plane = plane_sum_steps(grads_out, emit, scratch[3:])
-    advance(plane, 10)
+    advance(plane, 1)
     line.add()
     line.gather()
     advance(plane, PLANE_STEPS)
@@ -1483,7 +1517,9 @@
     ffn,
     middle,
     layer,
+    grad_in,
     layer_out,
+    grad_in_out,
     query_out,
     latent_out,
     router_out,
@@ -1495,6 +1531,7 @@
     down_out,
 ):
     layer_out[...] = (middle[...] + layer[...].astype(jnp.float32)).astype(layer_out.dtype)
+    grad_in_out[...] = grad_in[...]
     for head in range(HEADS):
         query_out[:, 192 * head : 192 * head + 128] = own[:, 128 * head : 128 * head + 128]
         for half in (0, 1):
@@ -1597,7 +1634,6 @@
 ):
     tokens, model_width = hidden_in.shape
     devices = lax.axis_size("expert")
-    own_index = lax.axis_index("expert")
     low = jnp.bfloat16
     full = jnp.float32
     shard = w_query.shape[0]
@@ -1610,7 +1646,7 @@
             w_latent,
             attn_norm[None],
             ffn_norm[None],
-            jnp.pad(latent_norm, (0, shard - latent_norm.shape[0]))[None],
+            latent_norm[None],
             w_output.T,
             w_expand,
             shared_gate,
@@ -1623,41 +1659,45 @@
     ffn_all = lax.all_gather(ffn_shard, "expert", axis=0, tiled=True)
     grad_rows = lax.all_gather(cotangent, "expert", axis=0)
     attention_all = plane_gather(attention_shard, 1, "gather_attention")
-    gains = attention_all.reshape(devices, shard, -1)[:, :8, 1344:1408].astype(full)
-    gain_one = gains[:, 0].reshape(1, -1)
-    gain_two = gains[:, 1].reshape(1, -1)
-    gain_latent = gains[:, 2, : latent_norm.shape[0]].reshape(1, -1)
-    expand_w = (
-        attention_all[:, 1920:].reshape(devices, 4, 16, 256).swapaxes(1, 2).reshape(RANK, -1)
-    )
     output_blocks = column_blocks(attention_all, 11, 4)
     latent_blocks = column_blocks(attention_all, 6, 5)
     router_block = column_blocks(ffn_all, 5, 1)[0]
 
-    first_row = own_index * tokens
-    row_index = first_row + jnp.arange(tokens, dtype=jnp.int32)
-    own_segments = lax.dynamic_slice_in_dim(segments, first_row, tokens)
-    doc_start = jnp.sum((segments[None, :] < own_segments[:, None]).astype(jnp.int32), 1)
-    cosine, sine_tab = rope_tables(row_index - doc_start)
-    cosine, sine_tab = jnp.tile(cosine, (1, 4)), jnp.tile(sine_tab, (1, 4))
+    segment_rows = segments.reshape(devices, tokens)
+    half_dim = ROPE // 2
+    frequencies = rope_base ** (-jnp.arange(half_dim, dtype=full) / half_dim)
+    frequencies = jnp.tile(frequencies, HEADS)[None]
     key_count = 9 * tokens
-    normed, queries, latent, keys_all = joint_call(
+    (
+        normed,
+        queries,
+        latent,
+        keys_all,
+        cosine,
+        sine_tab,
+        gain_one,
+        gain_two,
+        gain_latent,
+    ) = joint_call(
         project_kernel,
         2,
         "project",
         (
             hidden_in,
             (attention_all, (model_width, 1408), (0, 0)),
-            gain_one,
-            gain_latent,
-            cosine,
-            sine_tab,
+            segment_rows,
+            frequencies,
         ),
         (
             ((tokens, model_width), low),
             ((tokens, 768), low),
             ((tokens, RANK), full),
             ((9, tokens // 8, 8, 640), low),
+            ((tokens, 128), full),
+            ((tokens, 128), full),
+            ((1, model_width), full),
+            ((1, model_width), full),
+            ((1, RANK), full),
         ),
         [
             pltpu.VMEM((tokens // 8, 8, 640), low),
@@ -1671,20 +1711,24 @@
         2**25,
     )
     keys_all = keys_all.reshape(key_count, 640)
-    key_segments = lax.dynamic_slice_in_dim(
-        jnp.pad(segments, (key_count - tokens, 0), constant_values=-1), first_row, key_count
-    )
-    attn_out, attended, probs, expanded, key_rope = joint_call(
+    attn_out, attended, probs, expanded, key_rope, expand_w = joint_call(
         attend_kernel,
         3,
         "attend",
-        (keys_all, expand_w, queries, own_segments[:, None], key_segments[None], *output_blocks),
+        (
+            keys_all,
+            *column_blocks(attention_all, 15, 2),
+            queries,
+            segment_rows,
+            *output_blocks,
+        ),
         (
             ((tokens // 8, 8, model_width), low),
             ((tokens, HEADS * VH), low),
             ((HEADS, tokens, key_count), full),
             ((key_count, HEADS * (NOPE + VH)), low),
             ((key_count, 256), low),
+            ((RANK, HEADS * (NOPE + VH)), low),
         ),
         [pltpu.VMEM((tokens // 8, 8, model_width), low)] * 2
         + line_scratch(tokens // 8, model_width),
@@ -1692,10 +1736,11 @@
     )
     attn_out = attn_out.reshape(tokens, model_width)
 
+    route_rows = routes.T
     token_row, middle, gates = local_call(
         route_kernel,
         "route",
-        (hidden_in, attn_out, gain_two, router_block, routes),
+        (hidden_in, attn_out, gain_two, router_block, route_rows),
         (
             ((tokens, model_width + 128), low),
             ((tokens, model_width), full),
@@ -1750,7 +1795,7 @@
             middle,
             gain_two,
             gates,
-            routes,
+            route_rows,
             router_block,
             cotangent,
             *output_blocks,
@@ -1840,6 +1885,7 @@
     layer_sum = layer_sum.reshape(tokens, model_width)
     (
         layer_out,
+        grad_input,
         out_query,
         out_latent,
         out_router,
@@ -1852,8 +1898,9 @@
     ) = local_call(
         unpack_kernel,
         "unpack",
-        (own, own_last, own_ffn, middle, layer_sum),
+        (own, own_last, own_ffn, middle, layer_sum, grad_input),
         (
+            ((tokens, model_width), low),
             ((tokens, model_width), low),
             (w_query.shape, full),
             (w_latent.shape, full),

time: 453 us -> 479 us (1.057)
  Pallas kernels: 412 us -> 450 us
  local copies, waits for them, and re-layouts: 18 us -> 3.07 us
    pallas_call x4, Pallas kernels: 147 us -> 161 us  [joint_call(): pl.pallas_call(kernel, grid=(1,), out_shape=[jax.ShapeDtypeStruct(shape,...]
    pallas_call x2, Pallas kernels: 95.5 us -> 107 us  [plane_gather(): pl.pallas_call(plane_gather_kernel, out_shape=jax.ShapeDtypeStruct((32, *...]
    pallas_call x1, Pallas kernels: 73 us -> 83.9 us  [communicate(): pl.pallas_call(kernel, out_shape=shapes, in_specs=[vmem if inside else HB...]
  transfers between devices with their start and end apart: 4 -> 4, of which waited for: 0 -> 1; matrix products, arithmetic and copies ran while one was open for 3% -> 0% of each run, Pallas kernels for 84% -> 87%
where the time goes in v3:
time: 479 us; the launch traced here: 473 us
  Pallas kernels  450 us (94%)
  between operations  14.1 us (3%)
    pallas_call x4, Pallas kernels, joint_call(): pl.pallas_call(kernel, grid=(1,), out_shape=[jax.ShapeDtypeStruct(shape,...  161 us
    pallas_call x2, Pallas kernels, plane_gather(): pl.pallas_call(plane_gather_kernel, out_shape=jax.ShapeDtypeStruct((32, *...  107 us
    pallas_call x1, Pallas kernels, communicate(): pl.pallas_call(kernel, out_shape=shapes, in_specs=[vmem if inside else HB...  83.9 us
    pallas_call x1, Pallas kernels, experts(): pl.pallas_call(experts_kernel, grid=(2 * blocks + 2,), out_shape=(jax.Sha...  70.7 us
    pallas_call x4, Pallas kernels, local_call(): pl.pallas_call(kernel, grid=(1,), out_shape=shapes, in_specs=specs, out_s...  26.8 us
  transfers between devices with their start and end apart: 4, of which 1 were waited for; matrix products, arithmetic and copies ran while one was open for 0% of the time, Pallas kernels for 87%

profile of v3, /device:TPU:0, one launch (start us, length us, event | category | flops | bytes accessed | tf_op | source)
XLA Modules:
  0.0 473.1 jit_solution(11032429851578300707)
XLA Ops:
  7.2 0.0 all-gather.4.cloned.1.call-start
  7.2 2.3 pack.1
  9.6 0.0 all-gather.4.cloned.1.call-update
  9.6 0.0 all-gather.6.cloned.1.call-start
  9.6 0.7 all-gather.6.cloned.1.call-update
  10.3 0.0 reduce-scatter.3.cloned.1.call-start
  10.4 0.6 broadcast_in_dim_tile.3.frequencies
  11.0 38.8 %gather_attention.1 = bf16[32,8,8,2176]{3,2,1,0:T(8,128)(2,1)} custom-call(bf16[8,8,2176]{2,1,0:T(8,128)(2,1)} %bitcast.66), custom_call_target="tpu_custom_call" | custom-call | bytes 17825792 | tf_op jit(solution)/shard_map/gather_attention/pallas_call | solution.py:172
  49.8 31.0 %project.1 = (bf16[128,2048]{1,0:T(8,128)(2,1)}, bf16[128,768]{1,0:T(8,128)(2,1)}, f32[128,512]{1,0:T(8,128)}, bf16[9,16,8,640]{3,2,1,0:T(8,128)(2,1)}, f32[128,...) custom-call(bf16[128,2048]{1,0:T(8,128)(2,1)} %hidden.5, ...), custom_call_target="tpu_custom_call" | custom-call | bytes 33554432 | tf_op jit(solution)/shard_map/project/pallas_call | solution.py:1589
  80.8 29.9 %attend.1 = (bf16[16,8,2048]{2,1,0:T(8,128)(2,1)}, bf16[128,512]{1,0:T(8,128)(2,1)}, f32[4,128,1152]{2,1,0:T(8,128)}, bf16[1152,1024]{1,0:T(8,128)(2,1)}, bf16[1...) custom-call(bf16[1152,640]{1,0:T(8,128)(2,1)} %bitcast.57, bf16[2048,2176]{1,0:T(8,128)(2,1)} %bitcast.38, ...), custom_call_target="tpu_custom_call" | custom-call | bytes 33554432 | tf_op jit(solution)/shard_map/attend/pallas_call | solution.py:1589
  110.7 0.0 all-gather.4.cloned.1.call-done.router.weights
  110.7 3.0 route.1
  113.7 18.1 %shared.1 = (f32[128,2048]{1,0:T(8,128)}, f32[128,2176]{1,0:T(8,128)}, bf16[2048,2304]{1,0:T(8,128)(2,1)}) custom-call(bf16[128,2176]{1,0:T(8,128)(2,1)} %get-tuple-element.75.normed.normed_two, bf16[128,2048]{1,0:T(8,128)(2,1)} %cotangent.3, bf16[2048,2304]{1,0:T(8,128)(2,1)} %all-gather.4.cloned.1.call-done.router.weights), custom_call_target="tpu_custom_call" | custom-call | tf_op jit(solution)/shard_map/shared/pallas_call | solution.py:1563
  131.9 0.0 reduce-scatter.3.cloned.1.call-update
  131.9 0.3 reduce-scatter.5.cloned.1.call-start
  132.2 68.1 %gather_tokens.1 = bf16[32,16,8,2176]{3,2,1,0:T(8,128)(2,1)} custom-call(bf16[16,8,2176]{2,1,0:T(8,128)(2,1)} %bitcast.59), custom_call_target="tpu_custom_call" | custom-call | bytes 35651584 | tf_op jit(solution)/shard_map/gather_tokens/pallas_call | solution.py:172
  200.3 0.0 all-gather.6.cloned.1.call-done
  200.4 70.7 %experts.1 = (bf16[16,256,2048]{2,1,0:T(8,128)(2,1)}, bf16[16,256,2176]{2,1,0:T(8,128)(2,1)}, f32[2,352,2048]{2,1,0:T(8,128)}, f32[2,352,2048]{2,1,0:T(8,128)}, f32[2,352,2048]{2,1,0:T(8,128)}) custom-call(bf16[16,256,2176]{2,1,0:T(8,128)(2,1)} %bitcast.55, bf16[16,256,2048]{2,1,0:T(8,128)(2,1)} %bitcast.78, f32[2,352,2048]{2,1,0:T(8,128)} %bitcast.79, ...), custom_call_target="tpu_custom_call" | custom-call | flops 21743271936 | bytes 104857600 | tf_op jit(solution)/shard_map/experts/pallas_call | solution.py:908
  271.1 3.2 reduce-scatter.3.cloned.1.call-done.ffn
  274.3 0.0 reduce-scatter.5.cloned.1.call-update
  274.4 83.9 %sum_tokens.1 = bf16[16,8,2176]{2,1,0:T(8,128)(2,1)} custom-call(bf16[32,16,8,2176]{3,2,1,0:T(8,128)(2,1)} %bitcast.54, f32[16,8,2176]{2,1,0:T(8,128)} %bitcast.61), custom_call_target="tpu_custom_call" | custom-call | bytes 142606336 | tf_op jit(solution)/shard_map/sum_tokens/pallas_call | solution.py:491
  358.2 0.0 copy-start
  358.2 67.3 %attend_back.1 = (f32[128,2048]{1,0:T(8,128)}, bf16[128,2048]{1,0:T(8,128)(2,1)}, f32[1,2048]{1,0:T(1,128)}, bf16[128,128]{1,0:T(8,128)(2,1)}, f32[8,8,1536]{2,1...) custom-call(bf16[128,2176]{1,0:T(8,128)(2,1)} %bitcast.60, f32[128,2048]{1,0:T(8,128)} %get-tuple-element.78.middle, ...), custom_call_target="tpu_custom_call" | custom-call | bytes 67108864 | tf_op jit(solution)/shard_map/attend_back/pallas_call | solution.py:1589
  425.6 0.0 reduce-scatter.5.cloned.1.call-done
  425.6 0.0 copy-done
  425.6 1.9 fusion.layer
  427.5 33.1 %finish.1 = (bf16[128,2048]{1,0:T(8,128)(2,1)}, f32[8,8,768]{2,1,0:T(8,128)}, bf16[16,8,2048]{2,1,0:T(8,128)(2,1)}) custom-call(bf16[128,2048]{1,0:T(8,128)(2,1)} %bitcast.62, bf16[128,640]{1,0:T(8,128)(2,1)} %bitcast.69, f32[128,512]{1,0:T(8,128)} %get-tuple-element.91.latent, f32[1,512]{1,0:T(1,128)} %get-tuple-element.92.gain_latent, ...), custom_call_target="tpu_custom_call" | custom-call | bytes 33554432 | tf_op jit(solution)/shard_map/finish/pallas_call | solution.py:1589
  460.6 3.3 unpack.1
  463.9 1.2 slice_bitcast_fusion.1
  465.1 1.3 slice_bitcast_fusion
  (2 shorter events, 0.0 us)
Async XLA Ops:
  7.2 103.5 %all-gather.4.cloned.1.call-start = ((), (), s32[]{:S(2)}) async-start(), calls=%async_computation.2 | async-start | bytes 9732096 | tf_op jit(solution)/shard_map/all_gather | solution.py:1659
  9.6 190.8 %all-gather.6.cloned.1.call-start = ((), (), s32[]{:S(2)}) async-start(), calls=%async_computation.5 | async-start | bytes 17301504 | tf_op jit(solution)/shard_map/all_gather | solution.py:1660
  10.3 264.0 %reduce-scatter.3.cloned.1.call-start = ((), (), s32[]{:S(2)}) async-start(), calls=%async_computation.3 | async-start | bytes 9732096 | tf_op jit(solution)/shard_map/reduce_scatter | solution.py:1762
  131.9 293.7 %reduce-scatter.5.cloned.1.call-start = ((), (), s32[]{:S(2)}) async-start(), calls=%async_computation.4 | async-start | bytes 17301504 | tf_op jit(solution)/shard_map/reduce_scatter | solution.py:1775
  358.2 67.4 %copy-start = (f32[128,2048]{1,0:T(8,128)S(1)}, f32[128,2048]{1,0:T(8,128)}, u32[]{:S(2)}) copy-start(f32[128,2048]{1,0:T(8,128)} %get-tuple-element.99) | copy-start | bytes 3145732
Sparse Core Ops, SparseCore 0:
  10.8 68.4 all-gather.3
  81.6 89.0 all-gather.5
  174.5 99.7 reduce-scatter.2
  278.6 124.5 reduce-scatter.4

commit v4 on v2

--- a/solution.py
+++ b/solution.py
@@ -1359,14 +1359,15 @@
         return carry
 
     lax.fori_loop(0, width // 256, grads, 0)
+
+    def emit(i, total):
+        own_out[i] = total
+
+    plane = plane_sum_steps(grads_out, emit, scratch[6:])
+    advance(plane, 1)
     line_one.add()
     line_one.gather()
-
-    def emit(i, total):
-        own_out[i] = total
-
-    plane = plane_sum_steps(grads_out, emit, scratch[6:])
-    advance(plane, 5)
+    advance(plane, 4)
     advance(back, 1)
     line_two.scatter()
     advance(plane, 8)
@@ -1400,13 +1401,15 @@
     normed_two,
     grad_logits,
     gain_two_grad,
-    layer,
+    routed,
+    shared,
     input_out,
     own_out,
     layer_out,
     changes,
     grads_out,
     landed,
+    layer,
     *scratch,
 ):
     low = jnp.bfloat16
@@ -1461,6 +1464,7 @@
             piece = jnp.concatenate([piece, jnp.zeros((1, 128 - size), jnp.float32)], 1)
             block = jnp.where(line_number == row, piece, block)
         grads_out[e, 0, :, RANK + 128 :] = block.astype(low)
+    layer[...] = (routed[...].astype(jnp.float32) + shared[...]).astype(low)
     hear(peers)
     line = Line(layer, landed, *scratch[:3])
     line.scatter()
@@ -1483,18 +1487,23 @@
     ffn,
     middle,
     layer,
+    grad_in,
     layer_out,
+    grad_in_out,
     query_out,
     latent_out,
     router_out,
     output_out,
-    gains_out,
+    gain_one_out,
+    gain_two_out,
+    gain_latent_out,
     expand_out,
     gate_out,
     up_out,
     down_out,
 ):
     layer_out[...] = (middle[...] + layer[...].astype(jnp.float32)).astype(layer_out.dtype)
+    grad_in_out[...] = grad_in[...]
     for head in range(HEADS):
         query_out[:, 192 * head : 192 * head + 128] = own[:, 128 * head : 128 * head + 128]
         for half in (0, 1):
@@ -1503,7 +1512,9 @@
     latent_out[...] = last[:, :576]
     router_out[...] = last[:, 576:640]
     output_out[...] = own[:, 768:1280]
-    gains_out[...] = last[0:8, 640:768]
+    gain_one_out[...] = last[0:1, 640:704]
+    gain_two_out[...] = last[1:2, 640:704]
+    gain_latent_out[...] = last[2:3, 640:656]
     for j in range(4):
         expand_out[:, 256 * j : 256 * j + 256] = own[16 * j : 16 * j + 16, 1280:1536]
     gate_out[...] = ffn[:, :704].astype(jnp.float32)
@@ -1730,7 +1741,6 @@
     routed_own = lax.psum_scatter(
         routed_part.reshape(-1, model_width), "expert", scatter_dimension=0, tiled=True
     )
-    layer_part = (routed_own.astype(full) + shared_part).astype(low)
     back_all = sum_tokens(back_part.reshape(devices * tokens, -1), shared_back, 5)
 
     (
@@ -1820,7 +1830,8 @@
             normed_two,
             grad_logits,
             grad_gain_two,
-            layer_part.reshape(tokens // 8, 8, model_width),
+            by_group(routed_own),
+            by_group(shared_part),
         ),
         (
             ((tokens, model_width), low),
@@ -1831,6 +1842,7 @@
             pltpu.VMEM((tokens, 640), low),
             pltpu.VMEM((devices, shard // 8, 8, 768), low),
             pltpu.VMEM((tokens // 8, 8, model_width), low),
+            pltpu.VMEM((tokens // 8, 8, model_width), low),
         ]
         + line_scratch(tokens // 8, model_width)
         + plane_scratch(shard // 8, 768),
@@ -1840,11 +1852,14 @@
     layer_sum = layer_sum.reshape(tokens, model_width)
     (
         layer_out,
+        grad_input,
         out_query,
         out_latent,
         out_router,
         out_output,
-        out_gains,
+        out_gain_one,
+        out_gain_two,
+        out_gain_latent,
         out_expand,
         out_sgate,
         out_sup,
@@ -1852,14 +1867,17 @@
     ) = local_call(
         unpack_kernel,
         "unpack",
-        (own, own_last, own_ffn, middle, layer_sum),
+        (own, own_last, own_ffn, middle, layer_sum, grad_input),
         (
+            ((tokens, model_width), low),
             ((tokens, model_width), low),
             (w_query.shape, full),
             (w_latent.shape, full),
             (w_router.shape, full),
             ((shard, w_output.shape[0]), full),
-            ((8, 128), full),
+            ((1, shard), full),
+            ((1, shard), full),
+            ((1, latent_norm.shape[0]), full),
             (w_expand.shape, full),
             (shared_gate.shape, full),
             (shared_up.shape, full),
@@ -1869,13 +1887,13 @@
     return (
         layer_out,
         grad_input,
-        out_gains[0, :shard],
+        out_gain_one.reshape(-1),
         out_query,
         out_latent,
-        out_gains[2, : latent_norm.shape[0]],
+        out_gain_latent.reshape(-1),
         out_expand,
         out_output.T,
-        out_gains[1, :shard],
+        out_gain_two.reshape(-1),
         out_router,
         out_sgate,
         out_sup,

time: 453 us -> 447 us (0.987)
  transfers between devices with their start and end apart: 4 -> 4, of which waited for: 0 -> 0; matrix products, arithmetic and copies ran while one was open for 3% -> 3% of each run, Pallas kernels for 84% -> 85%
where the time goes in v4:
time: 447 us; the launch traced here: 443 us
  Pallas kernels  413 us (92%)
  between operations  14.4 us (3%)
  local copies, waits for them, and re-layouts  13.7 us (3%)
    pallas_call x4, Pallas kernels, joint_call(): pl.pallas_call(kernel, grid=(1,), out_shape=[jax.ShapeDtypeStruct(shape,...  148 us
    pallas_call x2, Pallas kernels, plane_gather(): pl.pallas_call(plane_gather_kernel, out_shape=jax.ShapeDtypeStruct((32, *...  95.4 us
    pallas_call x1, Pallas kernels, communicate(): pl.pallas_call(kernel, out_shape=shapes, in_specs=[vmem if inside else HB...  73 us
    pallas_call x1, Pallas kernels, experts(): pl.pallas_call(experts_kernel, grid=(2 * blocks + 2,), out_shape=(jax.Sha...  70.3 us
    pallas_call x4, Pallas kernels, local_call(): pl.pallas_call(kernel, grid=(1,), out_shape=shapes, in_specs=specs, out_s...  25.9 us
  transfers between devices with their start and end apart: 4, of which 0 were waited for; matrix products, arithmetic and copies ran while one was open for 3% of the time, Pallas kernels for 85%

profile of v4, /device:TPU:0, one launch (start us, length us, event | category | flops | bytes accessed | tf_op | source)
XLA Modules:
  0.0 442.9 jit_solution(8605084949275560366)
XLA Ops:
  7.2 0.0 all-gather.4.cloned.1.call-start
  7.2 1.2 pad_bitcast_fusion.gain_latent
  8.4 2.3 pack.1
  10.7 0.0 all-gather.4.cloned.1.call-update
  10.7 0.0 all-gather.6.cloned.1.call-start
  10.8 0.7 all-gather.6.cloned.1.call-update
  11.5 0.0 reduce-scatter.3.cloned.1.call-start
  11.6 0.8 dynamic_slice.6
  12.3 0.8 pad_dynamic-slice_fusion
  13.1 0.6 broadcast_in_dim.23.key_segment
  13.7 1.1 convert_reduce_fusion
  14.8 0.1 multiply_sine_fusion
  14.9 0.7 copy.52.sine_tab
  15.7 0.8 dynamic-slice_bitcast_fusion
  16.4 0.7 copy.54.own_segment
  17.2 1.4 copy.55.routes
  18.6 0.7 copy.51.cosine
  19.3 42.8 %gather_attention.1 = bf16[32,8,8,2176]{3,2,1,0:T(8,128)(2,1)} custom-call(bf16[8,8,2176]{2,1,0:T(8,128)(2,1)} %bitcast.85), custom_call_target="tpu_custom_call" | custom-call | bytes 17825792 | tf_op jit(solution)/shard_map/gather_attention/pallas_call | solution.py:172
  62.1 0.9 slice.20
  63.1 0.7 reshape_squeeze.10.gain_latent
  63.7 0.7 reshape_squeeze.11.gain
  64.4 0.7 reshape_squeeze.9.gain
  65.1 1.3 slice.23
  66.4 0.5 copy.53
  66.9 1.2 copy.62
  68.1 24.7 %project.1 = (bf16[128,2048]{1,0:T(8,128)(2,1)}, bf16[128,768]{1,0:T(8,128)(2,1)}, f32[128,512]{1,0:T(8,128)}, bf16[9,16,8,640]{3,2,1,0:T(8,128)(2,1)}) custom-call(bf16[128,2048]{1,0:T(8,128)(2,1)} %hidden.5, bf16[2048,2176]{1,0:T(8,128)(2,1)} %bitcast.52, f32[1,2048]{1,0:T(1,128)} %reshape_squeeze.9.gain, f32[1,512]{1,0:T(1,128)} %reshape_squeeze.10.gain_latent, ...), custom_call_target="tpu_custom_call" | custom-call | bytes 33554432 | tf_op jit(solution)/shard_map/project/pallas_call | solution.py:1563
  92.8 29.4 %attend.1 = (bf16[16,8,2048]{2,1,0:T(8,128)(2,1)}, bf16[128,512]{1,0:T(8,128)(2,1)}, f32[4,128,1152]{2,1,0:T(8,128)}, bf16[1152,1024]{1,0:T(8,128)(2,1)}, bf16[1152,256]{1,0:T(8,128)(2,1)}) custom-call(bf16[1152,640]{1,0:T(8,128)(2,1)} %bitcast.72, bf16[512,1024]{1,0:T(8,128)(2,1)} %bitcast.70, bf16[128,768]{1,0:T(8,128)(2,1)} %get-tuple-element.65.query, ...), custom_call_target="tpu_custom_call" | custom-call | bytes 33554432 | tf_op jit(solution)/shard_map/attend/pallas_call | solution.py:1563
  122.2 0.0 all-gather.4.cloned.1.call-done.router.weights
  122.2 3.4 route.1
  125.6 16.9 %shared.1 = (f32[128,2048]{1,0:T(8,128)}, f32[128,2176]{1,0:T(8,128)}, bf16[2048,2304]{1,0:T(8,128)(2,1)}) custom-call(bf16[128,2176]{1,0:T(8,128)(2,1)} %get-tuple-element.70.normed.normed_two, bf16[128,2048]{1,0:T(8,128)(2,1)} %cotangent.3, bf16[2048,2304]{1,0:T(8,128)(2,1)} %all-gather.4.cloned.1.call-done.router.weights), custom_call_target="tpu_custom_call" | custom-call | tf_op jit(solution)/shard_map/shared/pallas_call | solution.py:1537
  142.5 0.0 reduce-scatter.3.cloned.1.call-update
  142.5 0.0 reduce-scatter.5.cloned.1.call-start
  142.6 52.6 %gather_tokens.1 = bf16[32,16,8,2176]{3,2,1,0:T(8,128)(2,1)} custom-call(bf16[16,8,2176]{2,1,0:T(8,128)(2,1)} %bitcast.74), custom_call_target="tpu_custom_call" | custom-call | bytes 35651584 | tf_op jit(solution)/shard_map/gather_tokens/pallas_call | solution.py:172
  195.2 0.0 all-gather.6.cloned.1.call-done
  195.3 70.3 %experts.1 = (bf16[16,256,2048]{2,1,0:T(8,128)(2,1)}, bf16[16,256,2176]{2,1,0:T(8,128)(2,1)}, f32[2,352,2048]{2,1,0:T(8,128)}, f32[2,352,2048]{2,1,0:T(8,128)}, f32[2,352,2048]{2,1,0:T(8,128)}) custom-call(bf16[16,256,2176]{2,1,0:T(8,128)(2,1)} %bitcast.68, bf16[16,256,2048]{2,1,0:T(8,128)(2,1)} %bitcast.94, f32[2,352,2048]{2,1,0:T(8,128)} %bitcast.95, ...), custom_call_target="tpu_custom_call" | custom-call | flops 21743271936 | bytes 104857600 | tf_op jit(solution)/shard_map/experts/pallas_call | solution.py:908
  265.5 0.0 reduce-scatter.3.cloned.1.call-done.ffn
  265.6 0.0 reduce-scatter.5.cloned.1.call-update
  265.6 73.0 %sum_tokens.1 = bf16[16,8,2176]{2,1,0:T(8,128)(2,1)} custom-call(bf16[32,16,8,2176]{3,2,1,0:T(8,128)(2,1)} %bitcast.67, f32[16,8,2176]{2,1,0:T(8,128)} %bitcast.78), custom_call_target="tpu_custom_call" | custom-call | bytes 142606336 | tf_op jit(solution)/shard_map/sum_tokens/pallas_call | solution.py:491
  338.6 63.5 %attend_back.1 = (f32[128,2048]{1,0:T(8,128)}, bf16[128,2048]{1,0:T(8,128)(2,1)}, f32[1,2048]{1,0:T(1,128)}, bf16[128,128]{1,0:T(8,128)(2,1)}, f32[8,8,1536]{2,1...) custom-call(bf16[128,2176]{1,0:T(8,128)(2,1)} %bitcast.77, f32[128,2048]{1,0:T(8,128)} %get-tuple-element.73.middle, ...), custom_call_target="tpu_custom_call" | custom-call | bytes 67108864 | tf_op jit(solution)/shard_map/attend_back/pallas_call | solution.py:1563
  402.1 0.0 reduce-scatter.5.cloned.1.call-done
  402.1 30.5 %finish.1 = (bf16[128,2048]{1,0:T(8,128)(2,1)}, f32[8,8,768]{2,1,0:T(8,128)}, bf16[16,8,2048]{2,1,0:T(8,128)(2,1)}) custom-call(bf16[128,2048]{1,0:T(8,128)(2,1)} %bitcast.81, bf16[128,640]{1,0:T(8,128)(2,1)} %bitcast.90, f32[128,512]{1,0:T(8,128)} %get-tuple-element.83.latent, f32[1,512]{1,0:T(1,128)} %reshape_squeeze.10.gain_latent, ...), custom_call_target="tpu_custom_call" | custom-call | bytes 33554432 | tf_op jit(solution)/shard_map/finish/pallas_call | solution.py:1563
  432.7 3.2 unpack.1
  (7 shorter events, 0.1 us)
Async XLA Ops:
  7.2 115.0 %all-gather.4.cloned.1.call-start = ((), (), s32[]{:S(2)}) async-start(), calls=%async_computation.2 | async-start | bytes 9732096 | tf_op jit(solution)/shard_map/all_gather | solution.py:1634
  10.7 184.5 %all-gather.6.cloned.1.call-start = ((), (), s32[]{:S(2)}) async-start(), calls=%async_computation.5 | async-start | bytes 17301504 | tf_op jit(solution)/shard_map/all_gather | solution.py:1635
  11.5 254.1 %reduce-scatter.3.cloned.1.call-start = ((), (), s32[]{:S(2)}) async-start(), calls=%async_computation.3 | async-start | bytes 9732096 | tf_op jit(solution)/shard_map/reduce_scatter | solution.py:1728
  142.5 259.6 %reduce-scatter.5.cloned.1.call-start = ((), (), s32[]{:S(2)}) async-start(), calls=%async_computation.4 | async-start | bytes 17301504 | tf_op jit(solution)/shard_map/reduce_scatter | solution.py:1741
Sparse Core Ops, SparseCore 0:
  10.9 63.9 all-gather.3
  77.1 72.4 all-gather.5
  153.3 99.4 reduce-scatter.2
  265.7 125.7 reduce-scatter.4

commit v5 on v4

--- a/solution.py
+++ b/solution.py
@@ -973,6 +973,12 @@
 SCALE = (NOPE + ROPE) ** (-0.5)
 
 
+def column(row):
+    shape = (128, 128)
+    same = lax.broadcasted_iota(jnp.int32, shape, 0) == lanes(shape)
+    return jnp.sum(jnp.where(same, row.astype(jnp.float32), 0.0), 1, keepdims=True)
+
+
 def in_groups(values):
     return values.reshape(values.shape[0] // 8, 8, values.shape[1])
 
@@ -1047,7 +1053,8 @@
     row = lax.broadcasted_iota(jnp.int32, (shard, shard), 0)
     gains = jnp.where(row == 0, gain_one[...], 0.0)
     gains = jnp.where(row == 1, gain_two[...], gains)
-    gains = jnp.where(row == 2, gain_latent[...], gains)
+    rest = jnp.zeros((1, shard - gain_latent.shape[1]), jnp.float32)
+    gains = jnp.where(row == 2, jnp.concatenate([gain_latent[...], rest], 1), gains)
     attention_out[:, 1280:1408] = jnp.concatenate([latent[:, RANK:], gains], 1).astype(low)
     attention_out[:, 1408:1920] = output[...].astype(low)
     for j in range(4):
@@ -1102,7 +1109,8 @@
 
 def attend_kernel(
     keys,
-    expand,
+    expand_0,
+    expand_1,
     query,
     own_segment,
     key_segment,
@@ -1115,6 +1123,7 @@
     probs,
     expanded,
     key_rope,
+    expand,
     held,
     landed,
     *scratch,
@@ -1125,6 +1134,10 @@
     rows = query.shape[0]
     count = keys.shape[0]
     fold = fold_matrix()
+    for k, block in enumerate((expand_0, expand_1)):
+        for j in range(4):
+            part = block[...].reshape(32, 64, 128)[:, 16 * j : 16 * j + 16, :]
+            expand[:, 256 * j + 128 * k : 256 * j + 128 * k + 128] = part.reshape(RANK, 128)
 
     def expand_rows(i, carry):
         part = pl.ds(pl.multiple_of(i * rows, rows), rows)
@@ -1168,8 +1181,8 @@
     width = normed.shape[1]
     token_out[:, :width] = normed
     logits = contract(normed, router[...], 1, 0)
-    lane = lanes(logits.shape)
-    named = [routes[:, r : r + 1] for r in range(6)]
+    lane = lanes(logits.shape).astype(jnp.float32)
+    named = [column(routes[r : r + 1, :]) for r in range(6)]
     chosen = [
         jnp.sum(jnp.where(lane == number + 64, logits, 0.0), 1, keepdims=True) for number in named
     ]
@@ -1181,7 +1194,7 @@
     for r in range(6):
         weight = exponents[r] / total
         high = weight.astype(low).astype(jnp.float32)
-        extra += jnp.where(lane == r, named[r].astype(jnp.float32), 0.0)
+        extra += jnp.where(lane == r, named[r], 0.0)
         extra += jnp.where(lane == 8 + r, high, 0.0)
         extra += jnp.where(lane == 16 + r, weight - high, 0.0)
         gates += jnp.where(lane == r, weight, 0.0)
@@ -1271,9 +1284,9 @@
     call(peers)
     width = middle.shape[1]
     rows = middle.shape[0]
-    lane = lanes((rows, 128))
+    lane = lanes((rows, 128)).astype(jnp.float32)
     sums = back[:, width:].astype(jnp.float32)
-    named = [routes[:, r : r + 1] for r in range(6)]
+    named = [column(routes[r : r + 1, :]) for r in range(6)]
     weight = [gates[:, r : r + 1] for r in range(6)]
     change = [
         jnp.sum(jnp.where(lane == number + 64, sums, 0.0), 1, keepdims=True) for number in named
@@ -1621,7 +1634,7 @@
             w_latent,
             attn_norm[None],
             ffn_norm[None],
-            jnp.pad(latent_norm, (0, shard - latent_norm.shape[0]))[None],
+            latent_norm[None],
             w_output.T,
             w_expand,
             shared_gate,
@@ -1638,9 +1651,6 @@
     gain_one = gains[:, 0].reshape(1, -1)
     gain_two = gains[:, 1].reshape(1, -1)
     gain_latent = gains[:, 2, : latent_norm.shape[0]].reshape(1, -1)
-    expand_w = (
-        attention_all[:, 1920:].reshape(devices, 4, 16, 256).swapaxes(1, 2).reshape(RANK, -1)
-    )
     output_blocks = column_blocks(attention_all, 11, 4)
     latent_blocks = column_blocks(attention_all, 6, 5)
     router_block = column_blocks(ffn_all, 5, 1)[0]
@@ -1685,17 +1695,25 @@
     key_segments = lax.dynamic_slice_in_dim(
         jnp.pad(segments, (key_count - tokens, 0), constant_values=-1), first_row, key_count
     )
-    attn_out, attended, probs, expanded, key_rope = joint_call(
+    attn_out, attended, probs, expanded, key_rope, expand_w = joint_call(
         attend_kernel,
         3,
         "attend",
-        (keys_all, expand_w, queries, own_segments[:, None], key_segments[None], *output_blocks),
+        (
+            keys_all,
+            *column_blocks(attention_all, 15, 2),
+            queries,
+            own_segments[:, None],
+            key_segments[None],
+            *output_blocks,
+        ),
         (
             ((tokens // 8, 8, model_width), low),
             ((tokens, HEADS * VH), low),
             ((HEADS, tokens, key_count), full),
             ((key_count, HEADS * (NOPE + VH)), low),
             ((key_count, 256), low),
+            ((RANK, HEADS * (NOPE + VH)), low),
         ),
         [pltpu.VMEM((tokens // 8, 8, model_width), low)] * 2
         + line_scratch(tokens // 8, model_width),
@@ -1703,10 +1721,11 @@
     )
     attn_out = attn_out.reshape(tokens, model_width)
 
+    route_rows = routes.T
     token_row, middle, gates = local_call(
         route_kernel,
         "route",
-        (hidden_in, attn_out, gain_two, router_block, routes),
+        (hidden_in, attn_out, gain_two, router_block, route_rows),
         (
             ((tokens, model_width + 128), low),
             ((tokens, model_width), full),
@@ -1760,7 +1779,7 @@
             middle,
             gain_two,
             gates,
-            routes,
+            route_rows,
             router_block,
             cotangent,
             *output_blocks,

time: 447 us -> 462 us (1.034)
  Pallas kernels: 413 us -> 432 us
  local copies, waits for them, and re-layouts: 13.7 us -> 8.05 us
    pallas_call x1, Pallas kernels: 73 us -> 82.4 us  [communicate(): pl.pallas_call(kernel, out_shape=shapes, in_specs=[vmem if inside else HB...]
    pallas_call x2, Pallas kernels: 95.4 us -> 101 us  [plane_gather(): pl.pallas_call(plane_gather_kernel, out_shape=jax.ShapeDtypeStruct((32, *...]
  transfers between devices with their start and end apart: 4 -> 4, of which waited for: 0 -> 0; matrix products, arithmetic and copies ran while one was open for 3% -> 2% of each run, Pallas kernels for 85% -> 87%
where the time goes in v5:
time: 462 us; the launch traced here: 457 us
  Pallas kernels  432 us (94%)
  between operations  14.1 us (3%)
  local copies, waits for them, and re-layouts  8.05 us (2%)
    pallas_call x4, Pallas kernels, joint_call(): pl.pallas_call(kernel, grid=(1,), out_shape=[jax.ShapeDtypeStruct(shape,...  153 us
    pallas_call x2, Pallas kernels, plane_gather(): pl.pallas_call(plane_gather_kernel, out_shape=jax.ShapeDtypeStruct((32, *...  101 us
    pallas_call x1, Pallas kernels, communicate(): pl.pallas_call(kernel, out_shape=shapes, in_specs=[vmem if inside else HB...  82.4 us
    pallas_call x1, Pallas kernels, experts(): pl.pallas_call(experts_kernel, grid=(2 * blocks + 2,), out_shape=(jax.Sha...  70.4 us
    pallas_call x4, Pallas kernels, local_call(): pl.pallas_call(kernel, grid=(1,), out_shape=shapes, in_specs=specs, out_s...  25.5 us
  transfers between devices with their start and end apart: 4, of which 0 were waited for; matrix products, arithmetic and copies ran while one was open for 2% of the time, Pallas kernels for 87%

profile of v5, /device:TPU:0, one launch (start us, length us, event | category | flops | bytes accessed | tf_op | source)
XLA Modules:
  0.0 457.1 jit_solution(5954058924561401716)
XLA Ops:
  7.2 0.0 all-gather.4.cloned.1.call-start
  7.2 2.3 pack.1
  9.6 0.0 all-gather.4.cloned.1.call-update
  9.6 0.0 all-gather.6.cloned.1.call-start
  9.6 0.7 all-gather.6.cloned.1.call-update
  10.3 0.0 reduce-scatter.3.cloned.1.call-start
  10.4 0.8 dynamic_slice.6
  11.2 0.8 pad_dynamic-slice_fusion
  11.9 0.6 broadcast_in_dim.23.key_segment
  12.5 1.1 convert_reduce_fusion
  13.6 0.1 multiply_sine_fusion
  13.8 0.7 copy.46.sine_tab
  14.5 0.8 dynamic-slice_bitcast_fusion
  15.3 0.7 copy.47.own_segment
  16.0 0.7 copy.45.cosine
  16.8 39.7 %gather_attention.1 = bf16[32,8,8,2176]{3,2,1,0:T(8,128)(2,1)} custom-call(bf16[8,8,2176]{2,1,0:T(8,128)(2,1)} %bitcast.76), custom_call_target="tpu_custom_call" | custom-call | bytes 17825792 | tf_op jit(solution)/shard_map/gather_attention/pallas_call | solution.py:172
  56.5 0.9 slice.16
  57.5 0.7 reshape_squeeze.10.gain_latent
  58.1 0.7 reshape_squeeze.11.gain
  58.8 0.7 reshape_squeeze.9.gain
  59.5 27.6 %project.1 = (bf16[128,2048]{1,0:T(8,128)(2,1)}, bf16[128,768]{1,0:T(8,128)(2,1)}, f32[128,512]{1,0:T(8,128)}, bf16[9,16,8,640]{3,2,1,0:T(8,128)(2,1)}) custom-call(bf16[128,2048]{1,0:T(8,128)(2,1)} %hidden.5, bf16[2048,2176]{1,0:T(8,128)(2,1)} %bitcast.45, f32[1,2048]{1,0:T(1,128)} %reshape_squeeze.9.gain, f32[1,512]{1,0:T(1,128)} %reshape_squeeze.10.gain_latent, ...), custom_call_target="tpu_custom_call" | custom-call | bytes 33554432 | tf_op jit(solution)/shard_map/project/pallas_call | solution.py:1576
  87.1 29.9 %attend.1 = (bf16[16,8,2048]{2,1,0:T(8,128)(2,1)}, bf16[128,512]{1,0:T(8,128)(2,1)}, f32[4,128,1152]{2,1,0:T(8,128)}, bf16[1152,1024]{1,0:T(8,128)(2,1)}, bf16[1...) custom-call(bf16[1152,640]{1,0:T(8,128)(2,1)} %bitcast.65, bf16[2048,2176]{1,0:T(8,128)(2,1)} %bitcast.46, ...), custom_call_target="tpu_custom_call" | custom-call | bytes 33554432 | tf_op jit(solution)/shard_map/attend/pallas_call | solution.py:1576
  117.0 0.0 all-gather.4.cloned.1.call-done.router.weights
  117.0 3.0 route.1
  120.1 16.8 %shared.1 = (f32[128,2048]{1,0:T(8,128)}, f32[128,2176]{1,0:T(8,128)}, bf16[2048,2304]{1,0:T(8,128)(2,1)}) custom-call(bf16[128,2176]{1,0:T(8,128)(2,1)} %get-tuple-element.71.normed.normed_two, bf16[128,2048]{1,0:T(8,128)(2,1)} %cotangent.3, bf16[2048,2304]{1,0:T(8,128)(2,1)} %all-gather.4.cloned.1.call-done.router.weights), custom_call_target="tpu_custom_call" | custom-call | tf_op jit(solution)/shard_map/shared/pallas_call | solution.py:1550
  136.9 0.0 reduce-scatter.3.cloned.1.call-update
  136.9 0.3 reduce-scatter.5.cloned.1.call-start
  137.2 61.7 %gather_tokens.1 = bf16[32,16,8,2176]{3,2,1,0:T(8,128)(2,1)} custom-call(bf16[16,8,2176]{2,1,0:T(8,128)(2,1)} %bitcast.67), custom_call_target="tpu_custom_call" | custom-call | bytes 35651584 | tf_op jit(solution)/shard_map/gather_tokens/pallas_call | solution.py:172
  199.0 0.0 all-gather.6.cloned.1.call-done
  199.0 70.4 %experts.1 = (bf16[16,256,2048]{2,1,0:T(8,128)(2,1)}, bf16[16,256,2176]{2,1,0:T(8,128)(2,1)}, f32[2,352,2048]{2,1,0:T(8,128)}, f32[2,352,2048]{2,1,0:T(8,128)}, f32[2,352,2048]{2,1,0:T(8,128)}) custom-call(bf16[16,256,2176]{2,1,0:T(8,128)(2,1)} %bitcast.63, bf16[16,256,2048]{2,1,0:T(8,128)(2,1)} %bitcast.88, f32[2,352,2048]{2,1,0:T(8,128)} %bitcast.89, ...), custom_call_target="tpu_custom_call" | custom-call | flops 21743271936 | bytes 104857600 | tf_op jit(solution)/shard_map/experts/pallas_call | solution.py:908
  269.4 0.0 reduce-scatter.3.cloned.1.call-done.ffn
  269.4 0.0 reduce-scatter.5.cloned.1.call-update
  269.4 82.4 %sum_tokens.1 = bf16[16,8,2176]{2,1,0:T(8,128)(2,1)} custom-call(bf16[32,16,8,2176]{3,2,1,0:T(8,128)(2,1)} %bitcast.62, f32[16,8,2176]{2,1,0:T(8,128)} %bitcast.69), custom_call_target="tpu_custom_call" | custom-call | bytes 142606336 | tf_op jit(solution)/shard_map/sum_tokens/pallas_call | solution.py:491
  351.9 64.7 %attend_back.1 = (f32[128,2048]{1,0:T(8,128)}, bf16[128,2048]{1,0:T(8,128)(2,1)}, f32[1,2048]{1,0:T(1,128)}, bf16[128,128]{1,0:T(8,128)(2,1)}, f32[8,8,1536]{2,1...) custom-call(bf16[128,2176]{1,0:T(8,128)(2,1)} %bitcast.68, f32[128,2048]{1,0:T(8,128)} %get-tuple-element.74.middle, ...), custom_call_target="tpu_custom_call" | custom-call | bytes 67108864 | tf_op jit(solution)/shard_map/attend_back/pallas_call | solution.py:1576
  416.6 0.0 reduce-scatter.5.cloned.1.call-done
  416.6 30.5 %finish.1 = (bf16[128,2048]{1,0:T(8,128)(2,1)}, f32[8,8,768]{2,1,0:T(8,128)}, bf16[16,8,2048]{2,1,0:T(8,128)(2,1)}) custom-call(bf16[128,2048]{1,0:T(8,128)(2,1)} %bitcast.72, bf16[128,640]{1,0:T(8,128)(2,1)} %bitcast.81, f32[128,512]{1,0:T(8,128)} %get-tuple-element.85.latent, f32[1,512]{1,0:T(1,128)} %reshape_squeeze.10.gain_latent, ...), custom_call_target="tpu_custom_call" | custom-call | bytes 33554432 | tf_op jit(solution)/shard_map/finish/pallas_call | solution.py:1576
  447.1 3.2 unpack.1
  (7 shorter events, 0.0 us)
Async XLA Ops:
  7.2 109.8 %all-gather.4.cloned.1.call-start = ((), (), s32[]{:S(2)}) async-start(), calls=%async_computation.2 | async-start | bytes 9732096 | tf_op jit(solution)/shard_map/all_gather | solution.py:1647
  9.6 189.4 %all-gather.6.cloned.1.call-start = ((), (), s32[]{:S(2)}) async-start(), calls=%async_computation.5 | async-start | bytes 17301504 | tf_op jit(solution)/shard_map/all_gather | solution.py:1648
  10.3 259.1 %reduce-scatter.3.cloned.1.call-start = ((), (), s32[]{:S(2)}) async-start(), calls=%async_computation.3 | async-start | bytes 9732096 | tf_op jit(solution)/shard_map/reduce_scatter | solution.py:1747
  136.9 279.7 %reduce-scatter.5.cloned.1.call-start = ((), (), s32[]{:S(2)}) async-start(), calls=%async_computation.4 | async-start | bytes 17301504 | tf_op jit(solution)/shard_map/reduce_scatter | solution.py:1760
Sparse Core Ops, SparseCore 0:
  10.8 63.9 all-gather.3
  77.1 85.2 all-gather.5
  166.1 100.8 reduce-scatter.2
  271.3 125.8 reduce-scatter.4
